TPU v7x, 32 devices: a whole 2x2x4 slice. The times are simulated.
32 devices in a mesh: ctx: 16 (over z, x, core), head: 2 (over y).
Axes of the slice: x: 2, y: 2, z: 4, core: 2. Of those that a mesh axis runs over, the one named last changes fastest.
Arguments:
- hidden_in: bfloat16 [4096, 1536], P(('ctx', 'head')), may hold values from -6 to 6
- block_order: int32 [2, 32], replicated, may hold values from 0 to 31, as said below
- doc_ids: int32 [2, 2048], replicated, may hold values from 0 to 3, as said below
- attn_gain: bfloat16 [2, 1536], P(None, 'ctx'), may hold values from 0.5 to 1.5
- w_query: bfloat16 [2, 1536, 1536], P(None, 'ctx', 'head'), may hold values from -0.15625 to 0.15625
- w_key: bfloat16 [2, 1536, 768], P(None, 'ctx', 'head'), may hold values from -0.15625 to 0.15625
- w_value: bfloat16 [2, 1536, 768], P(None, 'ctx', 'head'), may hold values from -0.15625 to 0.15625
- w_out: bfloat16 [2, 1536, 1536], P(None, 'head', 'ctx'), may hold values from -1.75 to 1.75
- mlp_gain: bfloat16 [2, 1536], P(None, 'ctx'), may hold values from 0.5 to 1.5
- w_gate: bfloat16 [2, 1536, 4096], P(None, 'ctx', 'head'), may hold values from -0.15625 to 0.15625
- w_up: bfloat16 [2, 1536, 4096], P(None, 'ctx', 'head'), may hold values from -0.15625 to 0.15625
- w_down: bfloat16 [2, 4096, 1536], P(None, 'head', 'ctx'), may hold values from -0.09375 to 0.09375
- cotangent: bfloat16 [4096, 1536], P(('ctx', 'head')), may hold values from -6 to 6
Outputs:
- out_hidden: bfloat16 [4096, 1536], P(('ctx', 'head'))
- d_hidden: float32 [4096, 1536], P(('ctx', 'head'))
- d_attn_gain: float32 [2, 1536], P(None, 'ctx')
- d_w_query: float32 [2, 1536, 1536], P(None, 'ctx', 'head')
- d_w_key: float32 [2, 1536, 768], P(None, 'ctx', 'head')
- d_w_value: float32 [2, 1536, 768], P(None, 'ctx', 'head')
- d_w_out: float32 [2, 1536, 1536], P(None, 'head', 'ctx')
- d_mlp_gain: float32 [2, 1536], P(None, 'ctx')
- d_w_gate: float32 [2, 1536, 4096], P(None, 'ctx', 'head')
- d_w_up: float32 [2, 1536, 4096], P(None, 'ctx', 'head')
- d_w_down: float32 [2, 4096, 1536], P(None, 'head', 'ctx')
Inputs may be any that keep to these rules, and one draw needn't show every extreme that they name: `block_order`: each row holds every number of 0 to 31 once. `doc_ids`: each row never falls from one position to the next.
All inputs are finite; a program needn't handle non-finite values.
Results may differ from a plain program's by a relative error of at most 0.025.
Values may be sent and summed in bfloat16 or wider, within the bound.
A program may use at most 320 MiB of HBM per device.

v0:
```python
import math

import jax
import jax.numpy as jnp
from jax import lax
from jax.sharding import PartitionSpec as P

HEAD_SIZE = 96
SEQS = 2
BLK = 64


NEG = -1e30
EPS = 1e-05
THETA = 100000.0


def rope_tables(positions):
    half_dim = HEAD_SIZE // 2
    freq_row = jnp.exp(
        jnp.arange(half_dim, dtype=jnp.float32) * (-2.0 * math.log(THETA) / HEAD_SIZE)
    )
    angles = positions.astype(jnp.float32)[:, None] * freq_row[None, :]
    return (jnp.cos(angles), jnp.sin(angles))


def rotate(tensor, cosine, sine_table):
    half_dim = tensor.shape[-1] // 2
    first_half = tensor[..., :half_dim]
    second_half = tensor[..., half_dim:]
    cos_wide = cosine[:, None, :]
    sin_wide = sine_table[:, None, :]
    return jnp.concatenate(
        [
            first_half * cos_wide - second_half * sin_wide,
            second_half * cos_wide + first_half * sin_wide,
        ],
        axis=-1,
    )


def rotate_back(incoming, cosine, sine_table):
    half_dim = incoming.shape[-1] // 2
    first_half = incoming[..., :half_dim]
    second_half = incoming[..., half_dim:]
    cos_wide = cosine[:, None, :]
    sin_wide = sine_table[:, None, :]
    return jnp.concatenate(
        [
            first_half * cos_wide + second_half * sin_wide,
            second_half * cos_wide - first_half * sin_wide,
        ],
        axis=-1,
    )


def key_span():
    return 1024


def masked_scores(grouped_heads, key_block, q_positions, q_docs, k_positions, k_docs):
    scores = jnp.einsum(
        "qhgd,khd->hgqk", grouped_heads, key_block, preferred_element_type=jnp.float32
    )
    allowed = (k_positions[None, :] <= q_positions[:, None]) & (k_docs[None, :] == q_docs[:, None])
    return jnp.where(allowed, scores, NEG)


def split_blocks(seq_keys, seq_values, k_positions, k_docs):
    length = seq_keys.shape[0]
    span = key_span()
    count = length // span
    return (
        seq_keys.reshape(count, span, seq_keys.shape[1], seq_keys.shape[2]),
        k_positions.reshape(count, span),
        k_docs.reshape(count, span),
        seq_values.reshape(count, span, seq_values.shape[1], seq_values.shape[2]),
    )


def attend_forward(grouped_heads, seq_keys, seq_values, q_positions, q_docs, k_positions, k_docs):
    q_len, heads_kv, group_size = (
        grouped_heads.shape[0],
        grouped_heads.shape[1],
        grouped_heads.shape[2],
    )
    blocked = split_blocks(seq_keys, seq_values, k_positions, k_docs)

    def stat_step(carry, blocks_in):
        run_max, run_sum = carry
        scores = masked_scores(
            grouped_heads, blocks_in[0], q_positions, q_docs, blocks_in[1], blocks_in[2]
        )
        new_max = jnp.maximum(run_max, jnp.max(scores, axis=-1))
        run_sum = run_sum * jnp.exp(run_max - new_max) + jnp.sum(
            jnp.exp(scores - new_max[..., None]), axis=-1
        )
        return ((new_max, run_sum), None)

    start_stats = (
        jnp.full((heads_kv, group_size, q_len), NEG, jnp.float32),
        jnp.zeros((heads_kv, group_size, q_len), jnp.float32),
    )
    (row_max, row_sum), unused = lax.scan(stat_step, start_stats, blocked)

    def value_step(total, blocks_in):
        scores = masked_scores(
            grouped_heads, blocks_in[0], q_positions, q_docs, blocks_in[1], blocks_in[2]
        )
        probs = (jnp.exp(scores - row_max[..., None]) / row_sum[..., None]).astype(jnp.bfloat16)
        return (
            total
            + jnp.einsum("hgqk,khd->qhgd", probs, blocks_in[3], preferred_element_type=jnp.float32),
            None,
        )

    mixed, unused = lax.scan(
        value_step, jnp.zeros((q_len, heads_kv, group_size, HEAD_SIZE), jnp.float32), blocked
    )
    return (mixed, row_max, row_sum)


def attend_backward(
    grouped_heads,
    seq_keys,
    seq_values,
    q_positions,
    q_docs,
    k_positions,
    k_docs,
    row_max,
    row_sum,
    grad_out,
):
    q_len, heads_kv, group_size = (
        grouped_heads.shape[0],
        grouped_heads.shape[1],
        grouped_heads.shape[2],
    )
    length = seq_keys.shape[0]
    blocked = split_blocks(seq_keys, seq_values, k_positions, k_docs)

    def block_probs(blocks_in):
        scores = masked_scores(
            grouped_heads, blocks_in[0], q_positions, q_docs, blocks_in[1], blocks_in[2]
        )
        probs = jnp.exp(scores - row_max[..., None]) / row_sum[..., None]
        grad_probs = jnp.einsum(
            "qhgd,khd->hgqk", grad_out, blocks_in[3], preferred_element_type=jnp.float32
        )
        return (probs, grad_probs)

    def delta_step(total, blocks_in):
        probs, grad_probs = block_probs(blocks_in)
        return (total + jnp.sum(probs * grad_probs, axis=-1), None)

    delta, unused = lax.scan(
        delta_step, jnp.zeros((heads_kv, group_size, q_len), jnp.float32), blocked
    )

    def grad_step(grad_query, blocks_in):
        probs, grad_probs = block_probs(blocks_in)
        grad_scores = (probs * (grad_probs - delta[..., None])).astype(jnp.bfloat16)
        grad_query = grad_query + jnp.einsum(
            "hgqk,khd->qhgd", grad_scores, blocks_in[0], preferred_element_type=jnp.float32
        )
        grad_key = jnp.einsum(
            "hgqk,qhgd->khd", grad_scores, grouped_heads, preferred_element_type=jnp.float32
        )
        grad_value = jnp.einsum(
            "hgqk,qhgd->khd",
            probs.astype(jnp.bfloat16),
            grad_out,
            preferred_element_type=jnp.float32,
        )
        return (grad_query, (grad_key, grad_value))

    grad_query, (grad_keys, grad_values) = lax.scan(
        grad_step, jnp.zeros((q_len, heads_kv, group_size, HEAD_SIZE), jnp.float32), blocked
    )
    return (
        grad_query,
        grad_keys.reshape(length, heads_kv, HEAD_SIZE),
        grad_values.reshape(length, heads_kv, HEAD_SIZE),
    )


def fetch_weights(gain_a, query_w, key_w, value_w, out_w, gain_m, gate_w, up_w, down_w):
    return (
        lax.all_gather(gain_a, "ctx", axis=0, tiled=True),
        lax.all_gather(query_w, "ctx", axis=0, tiled=True),
        lax.all_gather(key_w, "ctx", axis=0, tiled=True),
        lax.all_gather(value_w, "ctx", axis=0, tiled=True),
        lax.all_gather(out_w, "ctx", axis=1, tiled=True),
        lax.all_gather(gain_m, "ctx", axis=0, tiled=True),
        lax.all_gather(gate_w, "ctx", axis=0, tiled=True),
        lax.all_gather(up_w, "ctx", axis=0, tiled=True),
        lax.all_gather(down_w, "ctx", axis=1, tiled=True),
    )


def refetch_weights(gain_a, query_w, key_w, value_w, out_w, gain_m, gate_w, up_w, down_w):
    return (
        lax.all_gather(gain_a, "ctx", axis=0, tiled=True),
        lax.all_gather(query_w, "ctx", axis=0, tiled=True),
        lax.all_gather(key_w, "ctx", axis=0, tiled=True),
        lax.all_gather(value_w, "ctx", axis=0, tiled=True),
        lax.all_gather(out_w, "ctx", axis=1, tiled=True),
        lax.all_gather(gain_m, "ctx", axis=0, tiled=True),
        lax.all_gather(gate_w, "ctx", axis=0, tiled=True),
        lax.all_gather(up_w, "ctx", axis=0, tiled=True),
        lax.all_gather(down_w, "ctx", axis=1, tiled=True),
    )


def prepare(fetched):
    gain_a, query_w, key_w, value_w, out_w, gain_m, gate_w, up_w, down_w = fetched
    joined_qkv = jnp.concatenate([query_w, key_w, value_w], axis=1)
    joined_gu = jnp.concatenate([gate_w, up_w], axis=1)
    return (
        gain_a.astype(jnp.float32),
        joined_qkv,
        out_w,
        gain_m.astype(jnp.float32),
        joined_gu,
        down_w,
    )


def gather_rows(normed_rows):
    return lax.all_gather(normed_rows, "head", axis=0, tiled=True)


def gather_grads(grad_low):
    return lax.all_gather(grad_low, "head", axis=0, tiled=True)


def branch_total(mixed, weight):
    return lax.psum_scatter(
        jnp.dot(mixed, weight, preferred_element_type=jnp.float32).astype(jnp.bfloat16),
        "head",
        scatter_dimension=0,
        tiled=True,
    ).astype(jnp.float32)


def input_total(grads_in, weight):
    return lax.psum_scatter(
        lax.dot_general(
            grads_in, weight, (((1,), (1,)), ((), ())), preferred_element_type=jnp.float32
        ).astype(jnp.bfloat16),
        "head",
        scatter_dimension=0,
        tiled=True,
    ).astype(jnp.float32)


def norm_back(grad_res, normed_gradient, value_rows, inverse_norm, gain):
    normalized_input = value_rows * inverse_norm
    gain_gradient = jnp.sum(normed_gradient * normalized_input, axis=0)
    scaled_rows = normed_gradient * gain
    grad_res = grad_res + inverse_norm * (
        scaled_rows
        - normalized_input * jnp.mean(scaled_rows * normalized_input, axis=-1, keepdims=True)
    )
    return (grad_res, gain_gradient)


def transpose_dot(left, right):
    return lax.dot_general(
        left, right, (((0,), (0,)), ((), ())), preferred_element_type=jnp.float32
    )


def local(
    hidden_in,
    block_order,
    doc_ids,
    attn_gain,
    w_query,
    w_key,
    w_value,
    w_out,
    mlp_gain,
    w_gate,
    w_up,
    w_down,
    cotangent,
):
    ctx_count = lax.axis_size("ctx")
    head_count = lax.axis_size("head")
    own_rows = hidden_in.shape[0]
    token_rows = own_rows * head_count
    ctx_index = lax.axis_index("ctx")
    offsets = jnp.arange(BLK, dtype=jnp.int32)
    local_blocks = lax.dynamic_slice(block_order, (jnp.int32(0), 2 * ctx_index), (SEQS, 2))
    q_positions = (local_blocks[:, :, None] * BLK + offsets[None, None, :]).reshape(SEQS, 2 * BLK)
    q_docs = jnp.take_along_axis(doc_ids, q_positions, axis=1)
    k_positions = (block_order[:, :, None] * BLK + offsets[None, None, :]).reshape(
        SEQS, ctx_count * 2 * BLK
    )
    k_docs = jnp.take_along_axis(doc_ids, k_positions, axis=1)
    cosine, sine_table = rope_tables(q_positions.reshape(token_rows))
    scale_q = HEAD_SIZE ** (-0.5)
    layer_total = w_query.shape[0]
    residual = hidden_in.astype(jnp.float32)
    records = []
    for layer_number in range(layer_total):
        fetched = fetch_weights(
            attn_gain[layer_number],
            w_query[layer_number],
            w_key[layer_number],
            w_value[layer_number],
            w_out[layer_number],
            mlp_gain[layer_number],
            w_gate[layer_number],
            w_up[layer_number],
            w_down[layer_number],
        )
        prepared = prepare(fetched)
        gain_a, joined_qkv, out_w, gain_m, joined_gu, down_w = prepared
        q_width = fetched[1].shape[1]
        kv_width = fetched[2].shape[1]
        ff_width = fetched[6].shape[1]
        heads_q = q_width // HEAD_SIZE
        heads_kv = kv_width // HEAD_SIZE
        group_size = heads_q // heads_kv
        residual_in = residual
        inverse_a = lax.rsqrt(jnp.mean(residual * residual, axis=-1, keepdims=True) + EPS)
        normed_a = gather_rows((residual * inverse_a * gain_a).astype(jnp.bfloat16))
        projected = jnp.dot(normed_a, joined_qkv, preferred_element_type=jnp.float32)
        query_matrix = (
            rotate(
                projected[:, :q_width].reshape(token_rows, heads_q, HEAD_SIZE), cosine, sine_table
            )
            * scale_q
        ).astype(jnp.bfloat16)
        keys_local = (
            rotate(
                projected[:, q_width : q_width + kv_width].reshape(token_rows, heads_kv, HEAD_SIZE),
                cosine,
                sine_table,
            )
            .astype(jnp.bfloat16)
            .reshape(token_rows, kv_width)
        )
        values_local = projected[:, q_width + kv_width :].astype(jnp.bfloat16)
        keys_all, values_all = (
            lax.all_gather(keys_local, "ctx", axis=0, tiled=True),
            lax.all_gather(values_local, "ctx", axis=0, tiled=True),
        )
        grouped_heads = query_matrix.reshape(SEQS, 2 * BLK, heads_kv, group_size, HEAD_SIZE)
        keys_seq = keys_all.reshape(ctx_count, SEQS, 2 * BLK, heads_kv, HEAD_SIZE)
        values_seq = values_all.reshape(ctx_count, SEQS, 2 * BLK, heads_kv, HEAD_SIZE)
        mixed_parts = []
        maxima = []
        totals = []
        for seq_id in range(SEQS):
            mixed, row_max, row_sum = attend_forward(
                grouped_heads[seq_id],
                keys_seq[:, seq_id].reshape(-1, heads_kv, HEAD_SIZE),
                values_seq[:, seq_id].reshape(-1, heads_kv, HEAD_SIZE),
                q_positions[seq_id],
                q_docs[seq_id],
                k_positions[seq_id],
                k_docs[seq_id],
            )
            mixed_parts.append(mixed)
            maxima.append(row_max)
            totals.append(row_sum)
        attended = (
            jnp.concatenate(mixed_parts, axis=0).reshape(token_rows, q_width).astype(jnp.bfloat16)
        )
        middle = residual + branch_total(attended, out_w)
        inverse_m = lax.rsqrt(jnp.mean(middle * middle, axis=-1, keepdims=True) + EPS)
        normed_m = gather_rows((middle * inverse_m * gain_m).astype(jnp.bfloat16))
        gate_up = jnp.dot(normed_m, joined_gu, preferred_element_type=jnp.float32)
        gate_part = gate_up[:, :ff_width]
        up_part = gate_up[:, ff_width:]
        activated = (jax.nn.silu(gate_part) * up_part).astype(jnp.bfloat16)
        residual = middle + branch_total(activated, down_w)
        kept_weights = None
        kept_kv = None
        records.append(
            (
                residual_in,
                inverse_a,
                normed_a,
                query_matrix,
                keys_local,
                values_local,
                kept_kv,
                maxima,
                totals,
                attended,
                middle,
                inverse_m,
                normed_m,
                gate_part,
                up_part,
                activated,
                kept_weights,
                q_width,
                kv_width,
                ff_width,
            )
        )
    out_hidden = residual.astype(jnp.bfloat16)
    grad_res = cotangent.astype(jnp.float32)
    collected = []
    for layer_number in reversed(range(layer_total)):
        (
            residual_in,
            inverse_a,
            normed_a,
            query_matrix,
            keys_local,
            values_local,
            kept_kv,
            maxima,
            totals,
            attended,
            middle,
            inverse_m,
            normed_m,
            gate_part,
            up_part,
            activated,
            kept_weights,
            q_width,
            kv_width,
            ff_width,
        ) = records[layer_number]
        heads_q = q_width // HEAD_SIZE
        heads_kv = kv_width // HEAD_SIZE
        group_size = heads_q // heads_kv
        prepared = prepare(
            refetch_weights(
                attn_gain[layer_number],
                w_query[layer_number],
                w_key[layer_number],
                w_value[layer_number],
                w_out[layer_number],
                mlp_gain[layer_number],
                w_gate[layer_number],
                w_up[layer_number],
                w_down[layer_number],
            )
        )
        gain_a, joined_qkv, out_w, gain_m, joined_gu, down_w = prepared
        grad_rows_m = gather_grads(grad_res.astype(jnp.bfloat16))
        grad_act = lax.dot_general(
            grad_rows_m, down_w, (((1,), (1,)), ((), ())), preferred_element_type=jnp.float32
        )
        grad_down = transpose_dot(activated, grad_rows_m)
        sigmoid_g = jax.nn.sigmoid(gate_part)
        grad_gate = grad_act * up_part * sigmoid_g * (1.0 + gate_part * (1.0 - sigmoid_g))
        grad_up = grad_act * gate_part * sigmoid_g
        grad_gu = jnp.concatenate([grad_gate, grad_up], axis=1).astype(jnp.bfloat16)
        grad_joined_gu = transpose_dot(normed_m, grad_gu)
        grad_norm_m = input_total(grad_gu, joined_gu)
        grad_res, grad_gain_m = norm_back(grad_res, grad_norm_m, middle, inverse_m, gain_m)
        grad_rows_a = gather_grads(grad_res.astype(jnp.bfloat16))
        grad_attended = lax.dot_general(
            grad_rows_a, out_w, (((1,), (1,)), ((), ())), preferred_element_type=jnp.float32
        ).astype(jnp.bfloat16)
        grad_out_w = transpose_dot(attended, grad_rows_a)
        keys_all, values_all = (
            lax.all_gather(keys_local, "ctx", axis=0, tiled=True),
            lax.all_gather(values_local, "ctx", axis=0, tiled=True),
        )
        grouped_heads = query_matrix.reshape(SEQS, 2 * BLK, heads_kv, group_size, HEAD_SIZE)
        grad_grouped = grad_attended.reshape(SEQS, 2 * BLK, heads_kv, group_size, HEAD_SIZE)
        keys_seq = keys_all.reshape(ctx_count, SEQS, 2 * BLK, heads_kv, HEAD_SIZE)
        values_seq = values_all.reshape(ctx_count, SEQS, 2 * BLK, heads_kv, HEAD_SIZE)
        query_parts = []
        kv_parts = []
        for seq_id in range(SEQS):
            grad_query, grad_keys, grad_values = attend_backward(
                grouped_heads[seq_id],
                keys_seq[:, seq_id].reshape(-1, heads_kv, HEAD_SIZE),
                values_seq[:, seq_id].reshape(-1, heads_kv, HEAD_SIZE),
                q_positions[seq_id],
                q_docs[seq_id],
                k_positions[seq_id],
                k_docs[seq_id],
                maxima[seq_id],
                totals[seq_id],
                grad_grouped[seq_id],
            )
            query_parts.append(grad_query)
            kv_parts.append(
                jnp.concatenate(
                    [
                        grad_keys.reshape(ctx_count, 2 * BLK, kv_width),
                        grad_values.reshape(ctx_count, 2 * BLK, kv_width),
                    ],
                    axis=-1,
                )
            )
        grad_query_all = jnp.concatenate(query_parts, axis=0).reshape(
            token_rows, heads_q, HEAD_SIZE
        )
        grad_kv_all = jnp.stack(kv_parts, axis=1).reshape(ctx_count * token_rows, 2 * kv_width)
        grad_kv = lax.psum_scatter(grad_kv_all, "ctx", scatter_dimension=0, tiled=True)
        grad_q_pre = (
            (rotate_back(grad_query_all, cosine, sine_table) * scale_q)
            .astype(jnp.bfloat16)
            .reshape(token_rows, q_width)
        )
        grad_k_pre = (
            rotate_back(
                grad_kv[:, :kv_width].reshape(token_rows, heads_kv, HEAD_SIZE), cosine, sine_table
            )
            .astype(jnp.bfloat16)
            .reshape(token_rows, kv_width)
        )
        grad_v_pre = grad_kv[:, kv_width:].astype(jnp.bfloat16)
        grad_qkv = jnp.concatenate([grad_q_pre, grad_k_pre, grad_v_pre], axis=1)
        grad_joined_qkv = transpose_dot(normed_a, grad_qkv)
        grad_norm_a = input_total(grad_qkv, joined_qkv)
        grad_res, grad_gain_a = norm_back(grad_res, grad_norm_a, residual_in, inverse_a, gain_a)
        grad_gain_a, grad_gain_m = lax.psum((grad_gain_a, grad_gain_m), "head")
        shard_grads = (
            lax.psum_scatter(grad_gain_a, "ctx", scatter_dimension=0, tiled=True),
            lax.psum_scatter(grad_joined_qkv[:, :q_width], "ctx", scatter_dimension=0, tiled=True),
            lax.psum_scatter(
                grad_joined_qkv[:, q_width : q_width + kv_width],
                "ctx",
                scatter_dimension=0,
                tiled=True,
            ),
            lax.psum_scatter(
                grad_joined_qkv[:, q_width + kv_width :], "ctx", scatter_dimension=0, tiled=True
            ),
            lax.psum_scatter(grad_out_w, "ctx", scatter_dimension=1, tiled=True),
            lax.psum_scatter(grad_gain_m, "ctx", scatter_dimension=0, tiled=True),
            lax.psum_scatter(grad_joined_gu[:, :ff_width], "ctx", scatter_dimension=0, tiled=True),
            lax.psum_scatter(grad_joined_gu[:, ff_width:], "ctx", scatter_dimension=0, tiled=True),
            lax.psum_scatter(grad_down, "ctx", scatter_dimension=1, tiled=True),
        )
        collected.append(shard_grads)
    collected = collected[::-1]

    def layer_stack(position):
        return jnp.stack([entry[position] for entry in collected], axis=0)

    return (
        out_hidden,
        grad_res,
        layer_stack(0),
        layer_stack(1),
        layer_stack(2),
        layer_stack(3),
        layer_stack(4),
        layer_stack(5),
        layer_stack(6),
        layer_stack(7),
        layer_stack(8),
    )


def solution(mesh):
    return jax.shard_map(
        local,
        mesh=mesh,
        in_specs=(
            P(("ctx", "head"), None),
            P(),
            P(),
            P(None, "ctx"),
            P(None, "ctx", "head"),
            P(None, "ctx", "head"),
            P(None, "ctx", "head"),
            P(None, "head", "ctx"),
            P(None, "ctx"),
            P(None, "ctx", "head"),
            P(None, "ctx", "head"),
            P(None, "head", "ctx"),
            P(("ctx", "head"), None),
        ),
        out_specs=(
            P(("ctx", "head"), None),
            P(("ctx", "head"), None),
            P(None, "ctx"),
            P(None, "ctx", "head"),
            P(None, "ctx", "head"),
            P(None, "ctx", "head"),
            P(None, "head", "ctx"),
            P(None, "ctx"),
            P(None, "ctx", "head"),
            P(None, "ctx", "head"),
            P(None, "head", "ctx"),
        ),
        check_vma=False,
    )
```

profile of v0, /device:TPU:0, one launch (start us, length us, event | category | flops | bytes accessed | tf_op | source)
XLA Modules:
  0.0 3719.7 jit_solution(4299345659437477847)
XLA Ops:
  16.7 63.1 %all-reduce.10 = (bf16[1536]{0:T(1024)(128)(2,1)}, bf16[1536]{0:T(1024)(128)(2,1)S(1)}, bf16[1536]{0:T(1024)(128)(2,1)}, bf16[1536]{0:T(1024)(128)(2,1)}) all-reduce(bf16[1536]{0:T(1024)(128)(2,1)S(1)} %dynamic-update-slice.3, bf16[1536]{0:T(1024)(128)(2,1)S(1)} %dynamic-update-slice, ...), channel_id=16, replica_groups=mesh['ctx'=16,'head'=2] {'ctx'}, use_global_device_ids=true, to_apply=%add.3 | all-reduce | flops 6144 | bytes 24576
  92.3 44.2 %all-gather.45.cloned.1.call-done = bf16[1,1536,768]{2,1,0:T(8,128)(2,1)} async-done(((bf16[1,96,768]{2,1,0:T(8,128)(2,1)}), bf16[1,1536,768]{2,1,0:T(8,128)(2,1)}) %all-gather.45.cloned.1.call-update) | async-done | bytes 2359312 | tf_op jit(solution)/shard_map/all_gather | solution.py:191
  146.6 34.9 gather_fusion
  350.9 50.5 %all-gather.55.cloned.1.call-done = bf16[1,1536,2048]{2,1,0:T(8,128)(2,1)} async-done(((bf16[1,96,2048]{2,1,0:T(8,128)(2,1)}), bf16[1,1536,2048]{2,1,0:T(8,128)(2,1)}) %all-gather.55.cloned.1.call-update) | async-done | bytes 6291472 | tf_op jit(solution)/shard_map/all_gather | solution.py:197
  401.4 63.6 %all-gather.53.cloned.1.call-done = bf16[1,1536,2048]{2,1,0:T(8,128)(2,1)} async-done(((bf16[1,96,2048]{2,1,0:T(8,128)(2,1)}), bf16[1,1536,2048]{2,1,0:T(8,128)(2,1)}) %all-gather.53.cloned.1.call-update) | async-done | bytes 6291472 | tf_op jit(solution)/shard_map/all_gather | solution.py:196
  474.9 53.0 %all-gather.57.cloned.1.call-done = bf16[1,2048,1536]{1,2,0:T(8,128)(2,1)} async-done(((bf16[1,2048,96]{1,2,0:T(8,128)(2,1)}), bf16[1,2048,1536]{1,2,0:T(8,128)(2,1)}) %all-gather.57.cloned.1.call-update) | async-done | bytes 6291472 | tf_op jit(solution)/shard_map/all_gather | solution.py:198
  590.1 39.6 %all-gather.61.cloned.1.call-done = bf16[1,1536,384]{2,1,0:T(8,128)(2,1)} async-done(((bf16[1,96,384]{2,1,0:T(8,128)(2,1)}), bf16[1,1536,384]{2,1,0:T(8,128)(2,1)}) %all-gather.61.cloned.1.call-update) | async-done | bytes 1179664 | tf_op jit(solution)/shard_map/all_gather | solution.py:192
  629.7 43.4 %all-gather.59.cloned.1.call-done = bf16[1,1536,768]{2,1,0:T(8,128)(2,1)} async-done(((bf16[1,96,768]{2,1,0:T(8,128)(2,1)}), bf16[1,1536,768]{2,1,0:T(8,128)(2,1)}) %all-gather.59.cloned.1.call-update) | async-done | bytes 2359312 | tf_op jit(solution)/shard_map/all_gather | solution.py:191
  684.2 41.9 %all-gather.43.cloned.1.call-done = bf16[4096,384]{0,1:T(8,128)(2,1)} async-done(((bf16[256,384]{0,1:T(8,128)(2,1)}), bf16[4096,384]{0,1:T(8,128)(2,1)}) %all-gather.43.cloned.1.call-update) | async-done | bytes 3145744 | tf_op jit(solution)/shard_map/all_gather | solution.py:349
  908.8 49.3 %all-gather.69.cloned.1.call-done = bf16[1,1536,2048]{2,1,0:T(8,128)(2,1)} async-done(((bf16[1,96,2048]{2,1,0:T(8,128)(2,1)}), bf16[1,1536,2048]{2,1,0:T(8,128)(2,1)}) %all-gather.69.cloned.1.call-update) | async-done | bytes 6291472 | tf_op jit(solution)/shard_map/all_gather | solution.py:197
  958.1 63.4 %all-gather.67.cloned.1.call-done = bf16[1,1536,2048]{2,1,0:T(8,128)(2,1)} async-done(((bf16[1,96,2048]{2,1,0:T(8,128)(2,1)}), bf16[1,1536,2048]{2,1,0:T(8,128)(2,1)}) %all-gather.67.cloned.1.call-update) | async-done | bytes 6291472 | tf_op jit(solution)/shard_map/all_gather | solution.py:196
  1031.7 52.8 %all-gather.71.cloned.1.call-done = bf16[1,2048,1536]{1,2,0:T(8,128)(2,1)} async-done(((bf16[1,2048,96]{1,2,0:T(8,128)(2,1)}), bf16[1,2048,1536]{1,2,0:T(8,128)(2,1)}) %all-gather.71.cloned.1.call-update) | async-done | bytes 6291472 | tf_op jit(solution)/shard_map/all_gather | solution.py:198
  1148.4 137.8 %while.209 = (s32[]{:T(128)}, f32[128,4,2,96]{0,3,2,1:T(8,128)S(1)}, f32[2,1024,4,96]{1,0,3,2:T(2,128)}, f32[2,1024,4,96]{1,0,3,2:T(2,128)}, bf16[2,1024,4,96]{1...) while((s32[]{:T(128)}, f32[128,4,2,96]{0,3,2,1:T(8,128)S(1)}, ...), condition=%wide.region_38.39_spmd.clone, body=%wide.region_37.38_spmd.clone.sunk | while | flops 1014562816 | bytes 55612644 | solution.py:178
  1313.2 137.8 %while.211 = (s32[]{:T(128)}, f32[128,4,2,96]{0,3,2,1:T(8,128)S(1)}, f32[2,1024,4,96]{1,0,3,2:T(2,128)}, f32[2,1024,4,96]{1,0,3,2:T(2,128)}, bf16[2,1024,4,96]{1...) while((s32[]{:T(128)}, f32[128,4,2,96]{0,3,2,1:T(8,128)S(1)}, ...), condition=%wide.region_43.44_spmd.clone, body=%wide.region_42.43_spmd.clone.sunk | while | flops 1014562816 | bytes 55612644 | solution.py:178
  1520.8 133.5 %reduce-scatter.35.cloned.1.call-done = f32[256,768]{0,1:T(8,128)} async-done(((f32[4096,768]{0,1:T(8,128)}), f32[256,768]{0,1:T(8,128)}) %reduce-scatter.35.cloned.1.call-update) | async-done | bytes 786448 | tf_op jit(solution)/shard_map/reduce_scatter | solution.py:505
  1775.9 137.8 %while.215 = (s32[]{:T(128)}, f32[128,4,2,96]{0,3,2,1:T(8,128)S(1)}, f32[2,1024,4,96]{1,0,3,2:T(2,128)}, f32[2,1024,4,96]{1,0,3,2:T(2,128)}, bf16[2,1024,4,96]{1...) while((s32[]{:T(128)}, f32[128,4,2,96]{0,3,2,1:T(8,128)S(1)}, ...), condition=%wide.region_58.59_spmd.clone, body=%wide.region_57.58_spmd.clone.sunk | while | flops 1014562816 | bytes 55612644 | solution.py:178
  1940.3 137.8 %while.213 = (s32[]{:T(128)}, f32[128,4,2,96]{0,3,2,1:T(8,128)S(1)}, f32[2,1024,4,96]{1,0,3,2:T(2,128)}, f32[2,1024,4,96]{1,0,3,2:T(2,128)}, bf16[2,1024,4,96]{1...) while((s32[]{:T(128)}, f32[128,4,2,96]{0,3,2,1:T(8,128)S(1)}, ...), condition=%wide.region_53.54_spmd.clone, body=%wide.region_52.53_spmd.clone.sunk | while | flops 1014562816 | bytes 55612644 | solution.py:178
  2240.2 41.7 %reduce-scatter.41.cloned.1.call-done = f32[256,768]{0,1:T(8,128)} async-done(((f32[4096,768]{0,1:T(8,128)}), f32[256,768]{0,1:T(8,128)}) %reduce-scatter.41.cloned.1.call-update) | async-done | bytes 786448 | tf_op jit(solution)/shard_map/reduce_scatter | solution.py:505
  2314.6 46.4 %reduce-scatter.59.cloned.1.call-done = f32[768,96]{0,1:T(8,128)} async-done(((f32[768,1536]{0,1:T(8,128)}), f32[768,96]{0,1:T(8,128)}) %reduce-scatter.59.cloned.1.call-update) | async-done | bytes 294928 | tf_op jit(solution)/shard_map/reduce_scatter | solution.py:536
  2361.0 78.5 %reduce-scatter.57.cloned.1.call-done = f32[768,96]{0,1:T(8,128)} async-done(((f32[768,1536]{0,1:T(8,128)}), f32[768,96]{0,1:T(8,128)}) %reduce-scatter.57.cloned.1.call-update) | async-done | bytes 294928 | tf_op jit(solution)/shard_map/reduce_scatter | solution.py:536
  2441.4 136.2 %reduce-scatter.63.cloned.1.call-done = f32[96,2048]{1,0:T(8,128)} async-done(((f32[1536,2048]{1,0:T(8,128)}), f32[96,2048]{1,0:T(8,128)}) %reduce-scatter.63.cloned.1.call-update) | async-done | bytes 786448 | tf_op jit(solution)/shard_map/reduce_scatter | solution.py:538
  2577.6 138.4 %reduce-scatter.61.cloned.1.call-done = f32[96,2048]{1,0:T(8,128)} async-done(((f32[1536,2048]{1,0:T(8,128)}), f32[96,2048]{1,0:T(8,128)}) %reduce-scatter.61.cloned.1.call-update) | async-done | bytes 786448 | tf_op jit(solution)/shard_map/reduce_scatter | solution.py:538
  2718.6 135.7 %reduce-scatter.67.cloned.1.call-done = f32[96,2048]{1,0:T(8,128)} async-done(((f32[1536,2048]{1,0:T(8,128)}), f32[96,2048]{1,0:T(8,128)}) %reduce-scatter.67.cloned.1.call-update) | async-done | bytes 786448 | tf_op jit(solution)/shard_map/reduce_scatter | solution.py:539
  2854.4 138.2 %reduce-scatter.65.cloned.1.call-done = f32[96,2048]{1,0:T(8,128)} async-done(((f32[1536,2048]{1,0:T(8,128)}), f32[96,2048]{1,0:T(8,128)}) %reduce-scatter.65.cloned.1.call-update) | async-done | bytes 786448 | tf_op jit(solution)/shard_map/reduce_scatter | solution.py:539
  2995.4 135.5 %reduce-scatter.71.cloned.1.call-done = f32[2048,96]{0,1:T(8,128)} async-done(((f32[2048,1536]{0,1:T(8,128)}), f32[2048,96]{0,1:T(8,128)}) %reduce-scatter.71.cloned.1.call-update) | async-done | bytes 786448 | tf_op jit(solution)/shard_map/reduce_scatter | solution.py:540
  3130.9 138.4 %reduce-scatter.69.cloned.1.call-done = f32[2048,96]{0,1:T(8,128)} async-done(((f32[2048,1536]{0,1:T(8,128)}), f32[2048,96]{0,1:T(8,128)}) %reduce-scatter.69.cloned.1.call-update) | async-done | bytes 786448 | tf_op jit(solution)/shard_map/reduce_scatter | solution.py:540
  3290.1 61.4 %all-reduce.8 = (f32[1536]{0:T(1024)S(1)}, f32[1536]{0:T(1024)S(1)}, f32[1536]{0:T(1024)S(1)}, f32[1536]{0:T(1024)S(1)}) all-reduce(f32[1536]{0:T(1024)S(1)} %copy-done.146, f32[1536]{0:T(1024)S(1)} %get-tuple-element.2177, f32[1536]{0:T(1024)S(1)} %copy-done.145, ...), channel_id=31, replica_groups=mesh['ctx'=16,'head'=2] {'ctx'}, use_global_device_ids=true, to_apply=%region_67.68.clone | all-reduce | flops 6144 | bytes 49152
  3360.2 61.5 %reduce-scatter.49.cloned.1.call-done = f32[96,384]{1,0:T(8,128)} async-done(((f32[1536,384]{1,0:T(8,128)}), f32[96,384]{1,0:T(8,128)}) %reduce-scatter.49.cloned.1.call-update) | async-done | bytes 147472 | tf_op jit(solution)/shard_map/reduce_scatter | solution.py:527
  3423.4 63.9 %reduce-scatter.55.cloned.1.call-done = f32[96,384]{1,0:T(8,128)} async-done(((f32[1536,384]{1,0:T(8,128)}), f32[96,384]{1,0:T(8,128)}) %reduce-scatter.55.cloned.1.call-update) | async-done | bytes 147472 | tf_op jit(solution)/shard_map/reduce_scatter | solution.py:533
  3487.3 66.2 %reduce-scatter.53.cloned.1.call-done = f32[96,384]{1,0:T(8,128)} async-done(((f32[1536,384]{1,0:T(8,128)}), f32[96,384]{1,0:T(8,128)}) %reduce-scatter.53.cloned.1.call-update) | async-done | bytes 147472 | tf_op jit(solution)/shard_map/reduce_scatter | solution.py:533
  3555.2 76.8 %reduce-scatter.47.cloned.1.call-done = f32[96,768]{1,0:T(8,128)} async-done(((f32[1536,768]{1,0:T(8,128)}), f32[96,768]{1,0:T(8,128)}) %reduce-scatter.47.cloned.1.call-update) | async-done | bytes 294928 | tf_op jit(solution)/shard_map/reduce_scatter | solution.py:526
  3632.1 79.0 %reduce-scatter.45.cloned.1.call-done = f32[96,768]{1,0:T(8,128)} async-done(((f32[1536,768]{1,0:T(8,128)}), f32[96,768]{1,0:T(8,128)}) %reduce-scatter.45.cloned.1.call-update) | async-done | bytes 294928 | tf_op jit(solution)/shard_map/reduce_scatter | solution.py:526
  (924 shorter events, 1694.9 us)
Async XLA Ops:
  10.5 126.0 %all-gather.45.cloned.1.call-start = ((), (), s32[]{:S(2)}) async-start(), calls=%async_computation.52 | async-start | bytes 2506752 | tf_op jit(solution)/shard_map/all_gather | solution.py:191
  12.3 174.4 %all-gather.37.cloned.1.call-start = ((), (), s32[]{:S(2)}) async-start(), calls=%async_computation.24 | async-start | bytes 3342336 | tf_op jit(solution)/shard_map/all_gather | solution.py:350
  143.5 173.4 %all-gather.51.cloned.1.call-start = ((), (), s32[]{:S(2)}) async-start(), calls=%async_computation.55 | async-start | bytes 2506752 | tf_op jit(solution)/shard_map/all_gather | solution.py:194
  144.3 192.1 %reduce-scatter.25.cloned.1.call-start = ((), (), s32[]{:S(2)}) async-start(), calls=%async_computation.26 | async-start | bytes 1179648 | tf_op jit(solution)/shard_map/reduce_scatter | solution.py:239
  321.7 143.3 %all-gather.53.cloned.1.call-start = ((), (), s32[]{:S(2)}) async-start(), calls=%async_computation.56 | async-start | bytes 6684672 | tf_op jit(solution)/shard_map/all_gather | solution.py:196
  322.7 205.2 %all-gather.57.cloned.1.call-start = ((), (), s32[]{:S(2)}) async-start(), calls=%async_computation.58 | async-start | bytes 6684672 | tf_op jit(solution)/shard_map/all_gather | solution.py:198
  324.9 224.7 %reduce-scatter.27.cloned.1.call-start = ((), (), s32[]{:S(2)}) async-start(), calls=%async_computation.27 | async-start | bytes 1179648 | tf_op jit(solution)/shard_map/reduce_scatter | solution.py:239
  534.8 138.4 %all-gather.59.cloned.1.call-start = ((), (), s32[]{:S(2)}) async-start(), calls=%async_computation.59 | async-start | bytes 2506752 | tf_op jit(solution)/shard_map/all_gather | solution.py:191
  535.3 190.9 %all-gather.43.cloned.1.call-start = ((), (), s32[]{:S(2)}) async-start(), calls=%async_computation.29 | async-start | bytes 3342336 | tf_op jit(solution)/shard_map/all_gather | solution.py:349
  681.8 185.2 %all-gather.65.cloned.1.call-start = ((), (), s32[]{:S(2)}) async-start(), calls=%async_computation.62 | async-start | bytes 2506752 | tf_op jit(solution)/shard_map/all_gather | solution.py:194
  682.4 211.8 %reduce-scatter.29.cloned.1.call-start = ((), (), s32[]{:S(2)}) async-start(), calls=%async_computation.30 | async-start | bytes 1179648 | tf_op jit(solution)/shard_map/reduce_scatter | solution.py:239
  871.3 150.2 %all-gather.67.cloned.1.call-start = ((), (), s32[]{:S(2)}) async-start(), calls=%async_computation.63 | async-start | bytes 6684672 | tf_op jit(solution)/shard_map/all_gather | solution.py:196
  871.9 212.6 %all-gather.71.cloned.1.call-start = ((), (), s32[]{:S(2)}) async-start(), calls=%async_computation.65 | async-start | bytes 6684672 | tf_op jit(solution)/shard_map/all_gather | solution.py:198
  872.7 244.3 %reduce-scatter.33.cloned.1.call-start = ((), (), s32[]{:S(2)}) async-start(), calls=%async_computation.32 | async-start | bytes 1179648 | tf_op jit(solution)/shard_map/reduce_scatter | solution.py:248
  1100.8 553.5 %reduce-scatter.35.cloned.1.call-start = ((), (), s32[]{:S(2)}) async-start(), calls=%async_computation.33 | async-start | bytes 13369344 | tf_op jit(solution)/shard_map/reduce_scatter | solution.py:505
  1519.5 158.2 %reduce-scatter.37.cloned.1.call-start = ((), (), s32[]{:S(2)}) async-start(), calls=%async_computation.34 | async-start | bytes 1179648 | tf_op jit(solution)/shard_map/reduce_scatter | solution.py:248
  1726.4 555.5 %reduce-scatter.41.cloned.1.call-start = ((), (), s32[]{:S(2)}) async-start(), calls=%async_computation.36 | async-start | bytes 13369344 | tf_op jit(solution)/shard_map/reduce_scatter | solution.py:505
  2147.2 213.8 %reduce-scatter.59.cloned.1.call-start = ((), (), s32[]{:S(2)}) async-start(), calls=%async_computation.45 | async-start | bytes 5013504 | tf_op jit(solution)/shard_map/reduce_scatter | solution.py:536
  2151.3 288.2 %reduce-scatter.57.cloned.1.call-start = ((), (), s32[]{:S(2)}) async-start(), calls=%async_computation.44 | async-start | bytes 5013504 | tf_op jit(solution)/shard_map/reduce_scatter | solution.py:536
  2155.6 422.0 %reduce-scatter.63.cloned.1.call-start = ((), (), s32[]{:S(2)}) async-start(), calls=%async_computation.47 | async-start | bytes 13369344 | tf_op jit(solution)/shard_map/reduce_scatter | solution.py:538
  2190.5 525.5 %reduce-scatter.61.cloned.1.call-start = ((), (), s32[]{:S(2)}) async-start(), calls=%async_computation.46 | async-start | bytes 13369344 | tf_op jit(solution)/shard_map/reduce_scatter | solution.py:538
  2222.3 632.0 %reduce-scatter.67.cloned.1.call-start = ((), (), s32[]{:S(2)}) async-start(), calls=%async_computation.49 | async-start | bytes 13369344 | tf_op jit(solution)/shard_map/reduce_scatter | solution.py:539
  2223.1 769.5 %reduce-scatter.65.cloned.1.call-start = ((), (), s32[]{:S(2)}) async-start(), calls=%async_computation.48 | async-start | bytes 13369344 | tf_op jit(solution)/shard_map/reduce_scatter | solution.py:539
  2223.7 907.3 %reduce-scatter.71.cloned.1.call-start = ((), (), s32[]{:S(2)}) async-start(), calls=%async_computation.51 | async-start | bytes 13369344 | tf_op jit(solution)/shard_map/reduce_scatter | solution.py:540
  2231.0 1038.3 %reduce-scatter.69.cloned.1.call-start = ((), (), s32[]{:S(2)}) async-start(), calls=%async_computation.50 | async-start | bytes 13369344 | tf_op jit(solution)/shard_map/reduce_scatter | solution.py:540
  2239.0 1049.7 %reduce-scatter.43.cloned.1.call-start = ((), (), s32[]{:S(2)}) async-start(), calls=%async_computation.37 | async-start | bytes 1179648 | tf_op jit(solution)/shard_map/reduce_scatter | solution.py:248
  2288.6 1071.6 %reduce-scatter.51.cloned.1.call-start = ((), (), s32[]{:S(2)}) async-start(), calls=%async_computation.41 | async-start | bytes 2506752 | tf_op jit(solution)/shard_map/reduce_scatter | solution.py:527
  2295.7 1126.0 %reduce-scatter.49.cloned.1.call-start = ((), (), s32[]{:S(2)}) async-start(), calls=%async_computation.40 | async-start | bytes 2506752 | tf_op jit(solution)/shard_map/reduce_scatter | solution.py:527
  2302.7 1184.6 %reduce-scatter.55.cloned.1.call-start = ((), (), s32[]{:S(2)}) async-start(), calls=%async_computation.43 | async-start | bytes 2506752 | tf_op jit(solution)/shard_map/reduce_scatter | solution.py:533
  2303.3 1250.3 %reduce-scatter.53.cloned.1.call-start = ((), (), s32[]{:S(2)}) async-start(), calls=%async_computation.42 | async-start | bytes 2506752 | tf_op jit(solution)/shard_map/reduce_scatter | solution.py:533
  2304.0 1328.0 %reduce-scatter.47.cloned.1.call-start = ((), (), s32[]{:S(2)}) async-start(), calls=%async_computation.39 | async-start | bytes 5013504 | tf_op jit(solution)/shard_map/reduce_scatter | solution.py:526
  2309.1 1402.0 %reduce-scatter.45.cloned.1.call-start = ((), (), s32[]{:S(2)}) async-start(), calls=%async_computation.38 | async-start | bytes 5013504 | tf_op jit(solution)/shard_map/reduce_scatter | solution.py:526
  (186 other events, 8687.8 us)
Sparse Core Ops, SparseCore 0:
  10.9 41.0 all-gather.48
  95.2 41.2 all-gather.44
  142.0 44.2 all-gather.36
  188.9 46.0 all-gather.38
  237.6 40.4 all-gather.50
  339.6 61.8 all-gather.54
  404.6 60.4 all-gather.52
  467.4 60.4 all-gather.56
  551.8 38.3 all-gather.62
  631.8 41.2 all-gather.58
  680.2 45.9 all-gather.42
  728.9 43.3 all-gather.40
  774.4 41.1 all-gather.64
  897.3 60.7 all-gather.68
  961.0 60.4 all-gather.66
  1024.1 60.4 all-gather.70
  1519.6 134.6 reduce-scatter.34
  2147.3 134.5 reduce-scatter.40
  2286.3 74.6 reduce-scatter.58
  2364.9 74.5 reduce-scatter.56
  2443.9 133.6 reduce-scatter.62
  2582.2 133.7 reduce-scatter.60
  2720.6 133.7 reduce-scatter.66
  2858.8 133.7 reduce-scatter.64
  2997.2 133.7 reduce-scatter.70
  3135.5 133.7 reduce-scatter.68
  3292.3 63.0 reduce-scatter.50
  3359.6 62.0 reduce-scatter.48
  3425.3 61.9 reduce-scatter.54
  3491.6 61.9 reduce-scatter.52
  3557.4 74.6 reduce-scatter.46
  3636.4 74.5 reduce-scatter.44
  (10 shorter events, 213.3 us)
where the time goes:
time: 3770 us; the launch traced here: 3720 us
  waiting for transfers between devices  2140 us (57%)
  local copies, waits for them, and re-layouts  905 us (24%)
  matrix products  302 us (8%)
  blocking collectives  228 us (6%)
  other arithmetic  120 us (3%)
    dynamic_update_slice x32, local copies, waits for them, and re-layouts, attend_backward(): lax.scan(grad_step, jnp.zeros((q_len, heads_kv, group_size, HEAD_SIZE), j...  467 us
    reduce_scatter x2, waiting for transfers between devices, local(): lax.psum_scatter(grad_joined_gu[:, :ff_width], 'ctx', scatter_dimension=0...  275 us
    reduce_scatter x2, waiting for transfers between devices, local(): lax.psum_scatter(grad_joined_gu[:, ff_width:], 'ctx', scatter_dimension=0...  274 us
    reduce_scatter x2, waiting for transfers between devices, local(): lax.psum_scatter(grad_down, 'ctx', scatter_dimension=1, tiled=True)  274 us
    reduce_scatter x2, waiting for transfers between devices, local(): lax.psum_scatter(grad_kv_all, 'ctx', scatter_dimension=0, tiled=True)  175 us
    reduce_scatter x2, waiting for transfers between devices, local(): lax.psum_scatter(grad_joined_qkv[:, :q_width], 'ctx', scatter_dimension=0...  156 us
    reduce_scatter x2, waiting for transfers between devices, local(): lax.psum_scatter(grad_joined_qkv[:, q_width + kv_width:], 'ctx', scatter_...  130 us
    all_gather x2, waiting for transfers between devices, fetch_weights(): lax.all_gather(gate_w, 'ctx', axis=0, tiled=True)  127 us
  transfers between devices with their start and end apart: 42, of which 37 were waited for; matrix products, arithmetic and copies ran while one was open for 12% of the time, Pallas kernels for 0%

commit v1 on v0

v1 whole, which is shorter than its diff:
```python
import math

import jax
import jax.numpy as jnp
from jax import lax
from jax.experimental import pallas as pl
from jax.experimental.pallas import tpu as pltpu
from jax.sharding import PartitionSpec as P

HEAD_SIZE = 96
HALF = HEAD_SIZE // 2
SEQS = 2
BLK = 64
ROWS = 2 * BLK

NEG = -1e30
EPS = 1e-05
THETA = 100000.0
VMEM_LIMIT = 56 * 1024 * 1024
BF16 = jnp.bfloat16
F32 = jnp.float32


def ring_of(chips):
    return list(range(0, chips, 2)) + list(range(chips - 1, 0, -2))


def rope_tables(positions):
    freq_row = jnp.exp(jnp.arange(HALF, dtype=F32) * (-2.0 * math.log(THETA) / HEAD_SIZE))
    angles = positions.astype(F32)[:, None] * freq_row[None, :]
    return (jnp.cos(angles), jnp.sin(angles))


def rotate(tensor, cosine, sine_table):
    first, second = tensor[..., :HALF], tensor[..., HALF:]
    cos_wide, sin_wide = cosine[:, None, :], sine_table[:, None, :]
    return jnp.concatenate(
        [first * cos_wide - second * sin_wide, second * cos_wide + first * sin_wide], axis=-1
    )


def rotate_back(tensor, cosine, sine_table):
    first, second = tensor[..., :HALF], tensor[..., HALF:]
    cos_wide, sin_wide = cosine[:, None, :], sine_table[:, None, :]
    return jnp.concatenate(
        [first * cos_wide + second * sin_wide, second * cos_wide - first * sin_wide], axis=-1
    )


def dot(left, right):
    return jnp.dot(left, right, preferred_element_type=F32)


def dot_nt(left, right):
    return lax.dot_general(left, right, (((1,), (1,)), ((), ())), preferred_element_type=F32)


def dot_tn(left, right):
    return lax.dot_general(left, right, (((0,), (0,)), ((), ())), preferred_element_type=F32)


def row_tile(keys):
    return 256 if keys <= 2048 else 64


def gathered(own_ref, sib_ref):
    count = own_ref.shape[0]
    return jnp.concatenate(
        [own_ref[j] for j in range(count)] + [sib_ref[j] for j in range(count)], axis=1
    )


def mask_rows(kpos_ref, qpos_ref, qstart_ref, start, rows):
    kpos = kpos_ref[0]
    parts = []
    done = 0
    while done < rows:
        at = (start + done) % ROWS
        size = min(rows - done, ROWS - at)
        qpos = qpos_ref[0, at : at + size, :]
        qstart = qstart_ref[0, at : at + size, :]
        parts.append((kpos <= qpos) & (kpos >= qstart))
        done += size
    return parts


def masked(scores, parts):
    out = []
    at = 0
    for part in parts:
        size = part.shape[0]
        out.append(jnp.where(part, scores[at : at + size, :], NEG))
        at += size
    return jnp.concatenate(out, axis=0) if len(out) > 1 else out[0]


def attend_kernel(
    q_ref, ko_ref, ks_ref, vo_ref, vs_ref, kpos_ref, qpos_ref, qstart_ref, o_ref, lse_ref
):
    total = q_ref.shape[2]
    kt = gathered(ko_ref, ks_ref)
    vt = gathered(vo_ref, vs_ref)
    tile = min(total, row_tile(kt.shape[1]))
    for at in range(0, total, tile):
        q = q_ref[0, 0, at : at + tile, :]
        scores = masked(dot(q, kt), mask_rows(kpos_ref, qpos_ref, qstart_ref, at, tile))
        top = jnp.max(scores, axis=1, keepdims=True)
        weights = jnp.exp(scores - top)
        norm = jnp.sum(weights, axis=1, keepdims=True)
        probs = (weights * (1.0 / norm)).astype(BF16)
        o_ref[0, 0, at : at + tile, :] = dot_nt(probs, vt).astype(BF16)
        lse_ref[0, 0, at : at + tile, :] = top + jnp.log(norm)


def attend_back_kernel(
    q_ref,
    do_ref,
    lse_ref,
    ko_ref,
    ks_ref,
    vo_ref,
    vs_ref,
    kpos_ref,
    qpos_ref,
    qstart_ref,
    dq_ref,
    dko_ref,
    dks_ref,
    dvo_ref,
    dvs_ref,
):
    total = q_ref.shape[2]
    kt = gathered(ko_ref, ks_ref)
    vt = gathered(vo_ref, vs_ref)
    tile = min(total, row_tile(kt.shape[1]))
    dkt = None
    dvt = None
    for at in range(0, total, tile):
        q = q_ref[0, 0, at : at + tile, :]
        grad = do_ref[0, 0, at : at + tile, :]
        scores = masked(dot(q, kt), mask_rows(kpos_ref, qpos_ref, qstart_ref, at, tile))
        probs = jnp.exp(scores - lse_ref[0, 0, at : at + tile, :])
        dprobs = dot(grad, vt)
        delta = jnp.sum(probs * dprobs, axis=1, keepdims=True)
        dscores = (probs * (dprobs - delta)).astype(BF16)
        dq_ref[0, 0, at : at + tile, :] = dot_nt(dscores, kt)
        dk_part = dot_tn(q, dscores)
        dv_part = dot_tn(grad, probs.astype(BF16))
        dkt = dk_part if dkt is None else dkt + dk_part
        dvt = dv_part if dvt is None else dvt + dv_part
    count = dko_ref.shape[0]
    for j in range(count):
        dko_ref[j] = dkt[:, j * ROWS : (j + 1) * ROWS].astype(BF16)
        dks_ref[j] = dkt[:, (count + j) * ROWS : (count + j + 1) * ROWS].astype(BF16)
        dvo_ref[j] = dvt[:, j * ROWS : (j + 1) * ROWS].astype(BF16)
        dvs_ref[j] = dvt[:, (count + j) * ROWS : (count + j + 1) * ROWS].astype(BF16)


def attention_specs(q, kv_own, kpos):
    slots = kv_own.shape[0]
    kv_heads = kv_own.shape[1] // (2 * HEAD_SIZE)
    keys = kpos.shape[2]
    rows = q.shape[2]
    unit = pl.BlockSpec((1, 1, rows, HEAD_SIZE), lambda s, h: (s, h, 0, 0))
    column = pl.BlockSpec((1, 1, rows, 1), lambda s, h: (s, h, 0, 0))
    k_spec = pl.BlockSpec((slots, HEAD_SIZE, ROWS), lambda s, h: (0, h, s))
    v_spec = pl.BlockSpec((slots, HEAD_SIZE, ROWS), lambda s, h: (0, kv_heads + h, s))
    kpos_spec = pl.BlockSpec((1, 1, keys), lambda s, h: (s, 0, 0))
    q_spec = pl.BlockSpec((1, ROWS, 1), lambda s, h: (s, 0, 0))
    return kv_heads, unit, column, k_spec, v_spec, kpos_spec, q_spec


def attend_forward(q, kv_own, kv_sib, kpos, qpos, qstart):
    kv_heads, unit, column, k_spec, v_spec, kpos_spec, q_spec = attention_specs(q, kv_own, kpos)
    rows, keys = q.shape[2], kpos.shape[2]
    work = SEQS * kv_heads * rows * keys
    return pl.pallas_call(
        attend_kernel,
        grid=(SEQS, kv_heads),
        in_specs=[unit, k_spec, k_spec, v_spec, v_spec, kpos_spec, q_spec, q_spec],
        out_specs=[unit, column],
        out_shape=[
            jax.ShapeDtypeStruct(q.shape, BF16),
            jax.ShapeDtypeStruct(q.shape[:3] + (1,), F32),
        ],
        compiler_params=pltpu.CompilerParams(vmem_limit_bytes=VMEM_LIMIT),
        cost_estimate=pl.CostEstimate(
            flops=8 * HEAD_SIZE * work, bytes_accessed=8 * 2**20, transcendentals=work
        ),
    )(q, kv_own, kv_sib, kv_own, kv_sib, kpos, qpos, qstart)


def attend_backward(q, grad, lse, kv_own, kv_sib, kpos, qpos, qstart):
    kv_heads, unit, column, k_spec, v_spec, kpos_spec, q_spec = attention_specs(q, kv_own, kpos)
    rows, keys = q.shape[2], kpos.shape[2]
    work = SEQS * kv_heads * rows * keys
    slots = kv_own.shape[0]
    grad_spec = pl.BlockSpec((slots, HEAD_SIZE, ROWS), lambda s, h: (0, h, s))
    grad_shape = jax.ShapeDtypeStruct((slots, kv_heads * HEAD_SIZE, SEQS * ROWS), BF16)
    return pl.pallas_call(
        attend_back_kernel,
        grid=(SEQS, kv_heads),
        in_specs=[
            unit, unit, column, k_spec, k_spec, v_spec, v_spec, kpos_spec, q_spec, q_spec
        ],
        out_specs=[unit, grad_spec, grad_spec, grad_spec, grad_spec],
        out_shape=[jax.ShapeDtypeStruct(q.shape, F32)] + [grad_shape] * 4,
        compiler_params=pltpu.CompilerParams(vmem_limit_bytes=VMEM_LIMIT),
        cost_estimate=pl.CostEstimate(
            flops=20 * HEAD_SIZE * work, bytes_accessed=16 * 2**20, transcendentals=work
        ),
    )(q, grad, lse, kv_own, kv_sib, kv_own, kv_sib, kpos, qpos, qstart)


def build(n_ctx):
    chips = n_ctx // 2
    ring = ring_of(chips)

    def shifted(step):
        pairs = []
        for at, chip in enumerate(ring):
            target = ring[(at + step) % chips]
            pairs += [(chip * 2 + core, target * 2 + core) for core in range(2)]
        return pairs

    up, down = shifted(1), shifted(-1)
    sibling = [(i, i ^ 1) for i in range(n_ctx)]

    def send_up(value):
        return lax.ppermute(value, "ctx", up)

    def send_down(value):
        return lax.ppermute(value, "ctx", down)

    def swap_core(value):
        return lax.ppermute(value, "ctx", sibling)

    def swap_head(value):
        return lax.ppermute(value, "head", [(0, 1), (1, 0)])

    def ring_gather(shard):
        got = {0: shard}
        low, high = shard, shard
        half = chips // 2
        for step in range(1, half):
            low, high = send_up(low), send_down(high)
            got[chips - step] = low
            got[step] = high
        cut = shard.shape[0] // 2
        got[half] = jnp.concatenate([send_up(low[:cut]), send_down(high[cut:])], axis=0)
        return [got[j] for j in range(chips)]

    def ring_scatter(slots):
        low = slots[chips - 1][0].astype(BF16)
        high = slots[1][1].astype(BF16)
        for step in range(1, chips):
            low, high = send_up(low), send_down(high)
            own_low = slots[(chips - 1 - step) % chips][0].astype(F32)
            own_high = slots[(1 + step) % chips][1].astype(F32)
            low, high = low.astype(F32) + own_low, high.astype(F32) + own_high
            if step < chips - 1:
                low, high = low.astype(BF16), high.astype(BF16)
        return low, high

    def weight_gather(shard):
        own = jnp.concatenate(ring_gather(shard), axis=0)
        return own, swap_core(own)

    def weight_scatter(grad):
        db, cut = grad.shape[0] // chips, grad.shape[1] // 2
        slots = [
            (grad[j * db : (j + 1) * db, :cut], grad[j * db : (j + 1) * db, cut:])
            for j in range(chips)
        ]
        return jnp.concatenate(ring_scatter(slots), axis=1)

    def local(
        hidden_in,
        block_order,
        doc_ids,
        attn_gain,
        w_query,
        w_key,
        w_value,
        w_out,
        mlp_gain,
        w_gate,
        w_up,
        w_down,
        cotangent,
    ):
        layers, db = w_query.shape[0], w_query.shape[1]
        width = db * n_ctx
        side = width // 2
        q_width, kv_width, ff_width = w_query.shape[2], w_key.shape[2], w_gate.shape[2]
        heads_q, heads_kv = q_width // HEAD_SIZE, kv_width // HEAD_SIZE
        group = heads_q // heads_kv
        own_rows = hidden_in.shape[0]
        token_rows = own_rows * 2
        ctx = lax.axis_index("ctx")
        head = lax.axis_index("head")
        core = ctx % 2
        place_of = [0] * chips
        for at, chip in enumerate(ring):
            place_of[chip] = at
        place = jnp.array(place_of, jnp.int32)[ctx // 2]

        slot_ids = jnp.arange(n_ctx, dtype=jnp.int32)
        along = (place + slot_ids % chips) % chips
        chip_of = jnp.where(along < chips // 2, 2 * along, 2 * (chips - 1 - along) + 1)
        block_of = chip_of * 2 + (core + slot_ids // chips) % 2
        block_hot = (block_of[:, None] == slot_ids[None, :]).astype(F32)
        feature = jnp.arange(width, dtype=jnp.int32)
        wanted = jnp.repeat(block_of, db) * db + feature % db
        to_ring = (feature[:, None] == wanted[None, :]).astype(BF16)

        def reorder(rows):
            return dot(rows, to_ring)

        def restore(rows):
            return lax.dot_general(
                rows,
                to_ring.astype(F32),
                (((1,), (1,)), ((), ())),
                precision=lax.Precision.HIGHEST,
                preferred_element_type=F32,
            )

        fetched = []
        for layer in range(layers):
            attn_shard = jnp.concatenate(
                [w_query[layer], w_key[layer], w_value[layer], w_out[layer].T], axis=1
            )
            mlp_shard = jnp.concatenate([w_gate[layer], w_up[layer], w_down[layer].T], axis=1)
            fetched.append((weight_gather(attn_shard), weight_gather(mlp_shard)))
        gains = lax.all_gather(
            jnp.concatenate([attn_gain, mlp_gain], axis=0), "ctx", axis=1, tiled=True
        )
        gains = reorder(gains)

        offsets = jnp.arange(BLK, dtype=jnp.int32)
        first = (head == 0)[..., None, None]
        order = jnp.where(first, block_order, block_order[::-1])
        docs = jnp.where(first, doc_ids, doc_ids[::-1])
        own_blocks = lax.dynamic_slice(order, (jnp.int32(0), 2 * ctx), (SEQS, 2))
        q_positions = (own_blocks[:, :, None] * BLK + offsets[None, None, :]).reshape(SEQS, ROWS)
        ring_blocks = jnp.einsum(
            "ac,scb->sab", block_hot, order.reshape(SEQS, n_ctx, 2).astype(F32)
        ).astype(jnp.int32)
        k_positions = (ring_blocks[..., None] * BLK + offsets).reshape(SEQS, 1, n_ctx * ROWS)
        doc_blocks = docs.reshape(SEQS, -1, BLK)
        own_hot = (own_blocks[:, :, None] == jnp.arange(doc_blocks.shape[1])).astype(F32)
        q_docs = jnp.einsum("sab,sbj->saj", own_hot, doc_blocks.astype(F32)).astype(jnp.int32)
        q_docs = q_docs.reshape(SEQS, ROWS)
        q_starts = jnp.sum((docs[:, None, :] < q_docs[:, :, None]).astype(jnp.int32), axis=2)
        kpos = k_positions
        qpos, qstart = q_positions[:, :, None], q_starts[:, :, None]
        cosine, sine_table = rope_tables(q_positions.reshape(token_rows))
        scale_q = HEAD_SIZE ** (-0.5)

        def both_rows(rows):
            return jnp.concatenate([rows, swap_head(rows)], axis=0)

        def to_owner(parts):
            return parts[:own_rows] + swap_head(parts[own_rows:].astype(BF16)).astype(F32)

        def project(rows, weight, lo, hi):
            own, sib = weight
            return dot(rows[:, :side], own[:, lo:hi]) + dot(rows[:, side:], sib[:, lo:hi])

        def project_back(rows, weight, lo, hi):
            own, sib = weight
            return jnp.concatenate(
                [dot_nt(rows, own[:, lo:hi]), dot_nt(rows, sib[:, lo:hi])], axis=1
            )

        def weight_grad(left, right):
            lefts = jnp.concatenate([left[:, :side], swap_core(left[:, side:])], axis=0)
            rights = jnp.concatenate([right, swap_core(right)], axis=0)
            return dot_tn(lefts, rights)

        def units(rows):
            shaped = rows.reshape(SEQS, ROWS, heads_kv, group, HEAD_SIZE)
            return shaped.transpose(0, 2, 3, 1, 4).reshape(SEQS, heads_kv, group * ROWS, HEAD_SIZE)

        def from_units(parts):
            shaped = parts.reshape(SEQS, heads_kv, group, ROWS, HEAD_SIZE)
            return shaped.transpose(0, 3, 1, 2, 4).reshape(token_rows, q_width)

        qkv_width = q_width + 2 * kv_width
        attn_width = qkv_width + q_width
        residual = reorder(hidden_in)
        grad_res = reorder(cotangent)
        records = []
        for layer in range(layers):
            attn_w, mlp_w = fetched[layer]
            gain_a, gain_m = gains[layer], gains[layers + layer]
            residual_in = residual
            inverse_a = lax.rsqrt(jnp.mean(residual * residual, axis=-1, keepdims=True) + EPS)
            normed_a = both_rows((residual * inverse_a * gain_a).astype(BF16))
            projected = project(normed_a, attn_w, 0, qkv_width)
            q_rows = rotate(
                projected[:, :q_width].reshape(token_rows, heads_q, HEAD_SIZE), cosine, sine_table
            )
            queries = units((q_rows * scale_q).astype(BF16).reshape(token_rows, q_width))
            keys = rotate(
                projected[:, q_width : q_width + kv_width].reshape(
                    token_rows, heads_kv, HEAD_SIZE
                ),
                cosine,
                sine_table,
            ).reshape(token_rows, kv_width)
            kv_shard = jnp.concatenate([keys, projected[:, q_width + kv_width :]], axis=1)
            kv_own = jnp.stack(ring_gather(kv_shard.astype(BF16).T), axis=0)
            kv_sib = swap_core(kv_own)
            mixed, lse = attend_forward(queries, kv_own, kv_sib, kpos, qpos, qstart)
            attended = from_units(mixed)
            middle = residual + to_owner(project_back(attended, attn_w, qkv_width, attn_width))
            inverse_m = lax.rsqrt(jnp.mean(middle * middle, axis=-1, keepdims=True) + EPS)
            normed_m = both_rows((middle * inverse_m * gain_m).astype(BF16))
            gate_up = project(normed_m, mlp_w, 0, 2 * ff_width)
            gate_part, up_part = gate_up[:, :ff_width], gate_up[:, ff_width:]
            activated = (jax.nn.silu(gate_part) * up_part).astype(BF16)
            residual = middle + to_owner(
                project_back(activated, mlp_w, 2 * ff_width, 3 * ff_width)
            )
            records.append(
                (
                    residual_in,
                    inverse_a,
                    normed_a,
                    queries,
                    kv_own,
                    kv_sib,
                    lse,
                    attended,
                    middle,
                    inverse_m,
                    normed_m,
                    gate_part,
                    up_part,
                    activated,
                )
            )
        out_hidden = lax.dot_general(
            residual.astype(BF16), to_ring, (((1,), (1,)), ((), ())), preferred_element_type=F32
        ).astype(BF16)

        def norm_back(grad_res, normed_gradient, value_rows, inverse_norm, gain):
            normalized = value_rows * inverse_norm
            gain_gradient = jnp.sum(normed_gradient * normalized, axis=0)
            scaled = normed_gradient * gain
            mean = jnp.mean(scaled * normalized, axis=-1, keepdims=True)
            return grad_res + inverse_norm * (scaled - normalized * mean), gain_gradient

        d_attn = [None] * layers
        d_mlp = [None] * layers
        d_gains = [None] * (2 * layers)
        for layer in reversed(range(layers)):
            attn_w, mlp_w = fetched[layer]
            gain_a, gain_m = gains[layer], gains[layers + layer]
            (
                residual_in,
                inverse_a,
                normed_a,
                queries,
                kv_own,
                kv_sib,
                lse,
                attended,
                middle,
                inverse_m,
                normed_m,
                gate_part,
                up_part,
                activated,
            ) = records[layer]
            grad_rows_m = both_rows(grad_res.astype(BF16))
            grad_act = project(grad_rows_m, mlp_w, 2 * ff_width, 3 * ff_width)
            sigmoid_g = jax.nn.sigmoid(gate_part)
            grad_gate = grad_act * up_part * sigmoid_g * (1.0 + gate_part * (1.0 - sigmoid_g))
            grad_up = grad_act * gate_part * sigmoid_g
            grad_gu = jnp.concatenate([grad_gate, grad_up], axis=1).astype(BF16)
            grad_norm_m = to_owner(project_back(grad_gu, mlp_w, 0, 2 * ff_width))
            d_down = weight_scatter(weight_grad(grad_rows_m, activated))
            d_gu = weight_scatter(weight_grad(normed_m, grad_gu))
            grad_res, d_gains[layers + layer] = norm_back(
                grad_res, grad_norm_m, middle, inverse_m, gain_m
            )
            grad_rows_a = both_rows(grad_res.astype(BF16))
            grad_attended = project(grad_rows_a, attn_w, qkv_width, attn_width).astype(BF16)
            d_out = weight_grad(grad_rows_a, attended)
            grad_q, dk_own, dk_sib, dv_own, dv_sib = attend_backward(
                queries, units(grad_attended), lse, kv_own, kv_sib, kpos, qpos, qstart
            )
            dk_back, dv_back = swap_core(dk_sib), swap_core(dv_sib)
            kv_slots = [
                (
                    dk_own[j].astype(F32) + dk_back[j].astype(F32),
                    dv_own[j].astype(F32) + dv_back[j].astype(F32),
                )
                for j in range(chips)
            ]
            grad_k, grad_v = ring_scatter(kv_slots)
            grad_q_pre = rotate_back(
                from_units(grad_q).reshape(token_rows, heads_q, HEAD_SIZE), cosine, sine_table
            )
            grad_k_pre = rotate_back(
                grad_k.T.reshape(token_rows, heads_kv, HEAD_SIZE), cosine, sine_table
            )
            grad_qkv = jnp.concatenate(
                [
                    (grad_q_pre * scale_q).reshape(token_rows, q_width),
                    grad_k_pre.reshape(token_rows, kv_width),
                    grad_v.T,
                ],
                axis=1,
            ).astype(BF16)
            grad_norm_a = to_owner(project_back(grad_qkv, attn_w, 0, qkv_width))
            d_qkv = weight_grad(normed_a, grad_qkv)
            d_attn[layer] = weight_scatter(jnp.concatenate([d_qkv, d_out], axis=1))
            d_mlp[layer] = (d_gu, d_down)
            grad_res, d_gains[layer] = norm_back(
                grad_res, grad_norm_a, residual_in, inverse_a, gain_a
            )
        d_hidden = restore(grad_res)
        d_gains = restore(jnp.stack(d_gains, axis=0))
        d_gains = lax.psum_scatter(d_gains, "ctx", scatter_dimension=1, tiled=True)
        d_gains = d_gains + swap_head(d_gains)
        k_at, v_at = q_width, q_width + kv_width

        def stack(parts):
            return jnp.stack(parts, axis=0)

        return (
            out_hidden,
            d_hidden,
            d_gains[:layers],
            stack([part[:, :k_at] for part in d_attn]),
            stack([part[:, k_at:v_at] for part in d_attn]),
            stack([part[:, v_at:qkv_width] for part in d_attn]),
            stack([part[:, qkv_width:].T for part in d_attn]),
            d_gains[layers:],
            stack([part[0][:, :ff_width] for part in d_mlp]),
            stack([part[0][:, ff_width:] for part in d_mlp]),
            stack([part[1].T for part in d_mlp]),
        )

    return local


def solution(mesh):
    return jax.shard_map(
        build(mesh.shape["ctx"]),
        mesh=mesh,
        in_specs=(
            P(("ctx", "head"), None),
            P(),
            P(),
            P(None, "ctx"),
            P(None, "ctx", "head"),
            P(None, "ctx", "head"),
            P(None, "ctx", "head"),
            P(None, "head", "ctx"),
            P(None, "ctx"),
            P(None, "ctx", "head"),
            P(None, "ctx", "head"),
            P(None, "head", "ctx"),
            P(("ctx", "head"), None),
        ),
        out_specs=(
            P(("ctx", "head"), None),
            P(("ctx", "head"), None),
            P(None, "ctx"),
            P(None, "ctx", "head"),
            P(None, "ctx", "head"),
            P(None, "ctx", "head"),
            P(None, "head", "ctx"),
            P(None, "ctx"),
            P(None, "ctx", "head"),
            P(None, "ctx", "head"),
            P(None, "head", "ctx"),
        ),
        check_vma=False,
    )
```

time: 3770 us -> 1270 us (0.34)
  waiting for transfers between devices: 2140 us -> 636 us
  local copies, waits for them, and re-layouts: 905 us -> 98.5 us
  blocking collectives: 228 us -> 30.7 us
  starting transfers between devices: 2.06 us -> 197 us
  matrix products: 302 us -> 143 us
  Pallas kernels: 0 us -> 64.4 us
  other arithmetic: 120 us -> 66.6 us
    reduce_scatter x24 -> x0, waiting for transfers between devices: 1580 us -> none  [the longest x2 275 us: local(): lax.psum_scatter(grad_joined_gu[:, :ff_width], 'ctx', scatter_dimension=0...]
    ppermute x0 -> x203, waiting for transfers between devices: none -> 587 us  [the longest x80 262 us: send_down(): return lax.ppermute(value, 'ctx', down)]
    all_gather x18 -> x0, waiting for transfers between devices: 559 us -> none  [the longest x2 127 us: fetch_weights(): lax.all_gather(gate_w, 'ctx', axis=0, tiled=True)]
    dynamic_update_slice x32 -> x0, local copies, waits for them, and re-layouts: 467 us -> none  [attend_backward(): lax.scan(grad_step, jnp.zeros((q_len, heads_kv, group_size, HEAD_SIZE), j...]
    ppermute x0 -> x203, starting transfers between devices: none -> 197 us  [the longest x80 100 us: send_down(): return lax.ppermute(value, 'ctx', down)]
    dot_general x96 -> x47, matrix products: 302 us -> 138 us  [the longest x19 51.2 us: dot(): return jnp.dot(left, right, preferred_element_type=F32)]
    slice x37 -> x20, local copies, waits for them, and re-layouts: 152 us -> 5.44 us  [the longest x2 3.05 us: weight_scatter(): grad[j * db:(j + 1) * db, cut:]]
    another operation x30 -> x16, local copies, waits for them, and re-layouts: 134 us -> 7.03 us  [the longest x8 2.89 us: stack(): return jnp.stack(parts, axis=0)]
  transfers between devices with their start and end apart: 42 -> 204, of which waited for: 37 -> 110; matrix products, arithmetic and copies ran while one was open for 12% -> 23% of each run, Pallas kernels for 0% -> 5%
where the time goes in v1:
time: 1270 us; the launch traced here: 1250 us
  waiting for transfers between devices  636 us (50%)
  starting transfers between devices  197 us (16%)
  matrix products  143 us (11%)
  local copies, waits for them, and re-layouts  98.5 us (8%)
  other arithmetic  66.6 us (5%)
  Pallas kernels  64.4 us (5%)
  blocking collectives  30.7 us (2%)
  between operations  17.2 us (1%)
    ppermute x80, waiting for transfers between devices, send_down(): return lax.ppermute(value, 'ctx', down)  262 us
    ppermute x80, waiting for transfers between devices, send_up(): return lax.ppermute(value, 'ctx', up)  243 us
    ppermute x80, starting transfers between devices, send_down(): return lax.ppermute(value, 'ctx', down)  100 us
    ppermute x17, waiting for transfers between devices, swap_head(): return lax.ppermute(value, 'head', [(0, 1), (1, 0)])  81.6 us
    ppermute x80, starting transfers between devices, send_up(): return lax.ppermute(value, 'ctx', up)  70.6 us
    dot_general x19, matrix products, dot(): return jnp.dot(left, right, preferred_element_type=F32)  51.2 us
    unnamed x2, waiting for transfers between devices  49.5 us
    dot_general x16, matrix products, dot_nt(): lax.dot_general(left, right, (((1,), (1,)), ((), ())), preferred_element_...  44.3 us
  transfers between devices with their start and end apart: 204, of which 110 were waited for; matrix products, arithmetic and copies ran while one was open for 23% of the time, Pallas kernels for 5%

profile of v1, /device:TPU:0, one launch (start us, length us, event | category | flops | bytes accessed | tf_op | source)
XLA Modules:
  0.0 1254.5 jit_solution(13441623251274535690)
XLA Ops:
  18.9 30.7 %all-gather = bf16[16,96,4]{1,2,0:T(4,128)(2,1)S(1)} all-gather(bf16[1,96,4]{1,2,0:T(4,128)(2,1)S(1)} %maximum_bitcast_fusion.4), channel_id=1, replica_groups=mesh['ctx'=16,'head'=2] {'ctx'}, dimensions={0}, use_global_device_ids=true | all-gather | bytes 13056 | tf_op jit(solution)/shard_map/all_gather | solution.py:336
  72.6 31.4 %collective-permute-done.2 = bf16[96,2304]{1,0:T(8,128)(2,1)S(1)} collective-permute-done((bf16[96,2304]{1,0:T(8,128)(2,1)}, bf16[96,2304]{1,0:T(8,128)(2,1)S(1)}, u32[]{:S(2)}, u32[]{:S(2)}) %collective-permute-start.2) | collective-permute-done | bytes 442400 | tf_op jit(solution)/shard_map/ppermute | solution.py:233
  106.2 7.3 collective-permute-done.33
  118.5 58.6 %collective-permute-done.5 = bf16[96,2304]{1,0:T(8,128)(2,1)S(1)} collective-permute-done((bf16[96,2304]{1,0:T(8,128)(2,1)}, bf16[96,2304]{1,0:T(8,128)(2,1)S(1)}, u32[]{:S(2)}, u32[]{:S(2)}) %collective-permute-start.5) | collective-permute-done | bytes 442400 | tf_op jit(solution)/shard_map/ppermute | solution.py:230
  207.4 29.4 %collective-permute-done.7 = bf16[48,2304]{1,0:T(8,128)(2,1)S(1)} collective-permute-done((bf16[48,2304]{1,0:T(8,128)(2,1)S(1)}, bf16[48,2304]{1,0:T(8,128)(2,1)S(1)}, u32[]{:S(2)}, u32[]{:S(2)}) %collective-permute-start.7) | collective-permute-done | bytes 221216 | tf_op jit(solution)/shard_map/ppermute | solution.py:230
  237.8 13.2 %collective-permute-done.8 = bf16[48,2304]{1,0:T(8,128)(2,1)S(1)} collective-permute-done((bf16[48,2304]{1,0:T(8,128)(2,1)S(1)}, bf16[48,2304]{1,0:T(8,128)(2,1)S(1)}, u32[]{:S(2)}, u32[]{:S(2)}) %collective-permute-start.8) | collective-permute-done | bytes 221216 | tf_op jit(solution)/shard_map/ppermute | solution.py:233
  255.5 31.5 %collective-permute-done.26 = bf16[96,6144]{1,0:T(8,128)(2,1)S(1)} collective-permute-done((bf16[96,6144]{1,0:T(8,128)(2,1)S(1)}, bf16[96,6144]{1,0:T(8,128)(2,1)S(1)}, u32[]{:S(2)}, u32[]{:S(2)}) %collective-permute-start.26) | collective-permute-done | bytes 1179680 | tf_op jit(solution)/shard_map/ppermute | solution.py:230
  288.7 14.1 %collective-permute-done.27 = bf16[48,6144]{1,0:T(8,128)(2,1)S(1)} collective-permute-done((bf16[48,6144]{1,0:T(8,128)(2,1)S(1)}, bf16[48,6144]{1,0:T(8,128)(2,1)S(1)}, u32[]{:S(2)}, u32[]{:S(2)}) %collective-permute-start.27) | collective-permute-done | bytes 589856 | tf_op jit(solution)/shard_map/ppermute | solution.py:230
  305.0 12.7 %collective-permute-done.28 = bf16[48,6144]{1,0:T(8,128)(2,1)S(1)} collective-permute-done((bf16[48,6144]{1,0:T(8,128)(2,1)S(1)}, bf16[48,6144]{1,0:T(8,128)(2,1)S(1)}, u32[]{:S(2)}, u32[]{:S(2)}) %collective-permute-start.28) | collective-permute-done | bytes 589856 | tf_op jit(solution)/shard_map/ppermute | solution.py:233
  330.8 7.8 collective-permute-done.10
  343.5 7.2 collective-permute-done.11
  352.8 30.0 %collective-permute-done.12 = bf16[768,256]{1,0:T(8,128)(2,1)S(1)} collective-permute-done((bf16[768,256]{1,0:T(8,128)(2,1)S(1)}, bf16[768,256]{1,0:T(8,128)(2,1)S(1)}, u32[]{:S(2)}, u32[]{:S(2)}) %collective-permute-start.12) | collective-permute-done | bytes 393248 | tf_op jit(solution)/shard_map/ppermute | solution.py:233
  398.8 11.6 collective-permute-done.58
  423.5 15.6 %shard_map.221 = (bf16[2,4,256,96]{3,2,1,0:T(8,128)(2,1)}, f32[2,4,256,1]{3,2,1,0:T(8,128)}) custom-call(bf16[2,4,256,96]{3,2,1,0:T(8,128)(2,1)} %bitcast.361, bf16[8,768,256]{2,1,0:T(8,128)(2,1)} %copy-done.8, bf16[8,768,256]{2,1,0:T(8,128)(2,1)} %collective-permute-done.18.ks_ref.vs_ref, bf16[8,768,256]{2,1,0:T(8,128)(2,1)} %copy-done.8, ...), custom_call_target="tpu_custom_call" | custom-call | flops 3221225472 | bytes 8388608 | tf_op jit(solution)/shard_map/pallas_call | solution.py:177
  447.9 7.2 collective-permute-done.19
  458.7 7.1 collective-permute-done.20
  504.8 8.3 collective-permute-done.41
  516.2 8.4 collective-permute-done.42
  553.2 15.6 %shard_map.222 = (bf16[2,4,256,96]{3,2,1,0:T(8,128)(2,1)}, f32[2,4,256,1]{3,2,1,0:T(8,128)}) custom-call(bf16[2,4,256,96]{3,2,1,0:T(8,128)(2,1)} %bitcast.363, bf16[8,768,256]{2,1,0:T(8,128)(2,1)} %bitcast_dynamic-update-slice_fusion.2.ko_ref.vo_ref, bf16[8,768,256]{2,1,0:T(8,128)(2,1)} %collective-permute-done.49.ks_ref.vs_ref, ...), custom_call_target="tpu_custom_call" | custom-call | flops 3221225472 | bytes 8388608 | tf_op jit(solution)/shard_map/pallas_call | solution.py:177
  568.8 10.0 copy.108
  586.7 8.0 collective-permute-done.50
  691.8 16.6 %shard_map.223 = (f32[2,4,256,96]{3,2,1,0:T(8,128)}, bf16[8,384,256]{2,1,0:T(8,128)(2,1)}, bf16[8,384,256]{2,1,0:T(8,128)(2,1)}, bf16[8,384,256]{2,1,0:T(8,128)(2,1)}, bf16[8,384,256]{2,1,0:T(8,128)(2,1)}) custom-call(bf16[2,4,256,96]{3,2,1,0:T(8,128)(2,1)} %bitcast.364, bf16[2,4,256,96]{3,2,1,0:T(8,128)(2,1)} %bitcast.399, ...), custom_call_target="tpu_custom_call" | custom-call | flops 8053063680 | bytes 16777216 | tf_op jit(solution)/shard_map/pallas_call | solution.py:200
  729.7 8.0 fusion.405
  894.7 9.2 collective-permute-done.170
  908.2 7.4 collective-permute-done.83
  955.8 16.6 %shard_map.224 = (f32[2,4,256,96]{3,2,1,0:T(8,128)}, bf16[8,384,256]{2,1,0:T(8,128)(2,1)}, bf16[8,384,256]{2,1,0:T(8,128)(2,1)}, bf16[8,384,256]{2,1,0:T(8,128)(2,1)}, bf16[8,384,256]{2,1,0:T(8,128)(2,1)}) custom-call(bf16[2,4,256,96]{3,2,1,0:T(8,128)(2,1)} %bitcast.362, bf16[2,4,256,96]{3,2,1,0:T(8,128)(2,1)} %bitcast.400, ...), custom_call_target="tpu_custom_call" | custom-call | flops 8053063680 | bytes 16777216 | tf_op jit(solution)/shard_map/pallas_call | solution.py:200
  1032.4 8.0 fusion.406
  1046.5 7.7 collective-permute-done.157
  1060.7 9.1 collective-permute-done.95
  1080.1 8.1 collective-permute-done.97
  1098.5 7.4 collective-permute-done.99
  1138.9 49.4 %reduce-scatter.4.cloned.1.call-done = f32[96,4]{1,0:T(8,128)} async-done(((f32[1536,4]{1,0:T(8,128)}), f32[96,4]{1,0:T(8,128)}) %reduce-scatter.4.cloned.1.call-update) | async-done | bytes 1552
  (982 shorter events, 724.0 us)
Async XLA Ops:
  7.2 1181.1 %reduce-scatter.4.cloned.1.call-start = ((), (), s32[]{:S(2)}) async-start(), calls=%async_computation.1 | async-start | bytes 835584
  11.4 57.4 %collective-permute-start.1 = (bf16[96,2304]{1,0:T(8,128)(2,1)}, bf16[96,2304]{1,0:T(8,128)(2,1)}, u32[]{:S(2)}, u32[]{:S(2)}) collective-permute-start(bf16[96,2304]{1,0:T(8,128)(2,1)} %get-tuple-element.220), channel_id=1, source_target_pairs={{0,4},{2,6},{8,0},{10,2},{16,8},{18,10},{24,16},{26,18},{28,24},{3... | collective-permute-start | bytes 1327112 | tf_op jit(solution)/shard_map/ppermute | solution.py:233
  14.3 100.0 %collective-permute-start.4 = (bf16[96,2304]{1,0:T(8,128)(2,1)}, bf16[96,2304]{1,0:T(8,128)(2,1)}, u32[]{:S(2)}, u32[]{:S(2)}) collective-permute-start(bf16[96,2304]{1,0:T(8,128)(2,1)} %get-tuple-element.220), channel_id=1, source_target_pairs={{0,8},{2,10},{8,16},{10,18},{16,24},{18,26},{24,28},{26,30},{28,20... | collective-permute-start | bytes 1327112 | tf_op jit(solution)/shard_map/ppermute | solution.py:230
  15.4 55.3 %collective-permute-start.32 = (bf16[96,2304]{1,0:T(8,128)(2,1)}, bf16[96,2304]{1,0:T(8,128)(2,1)}, u32[]{:S(2)}, u32[]{:S(2)}) collective-permute-start(bf16[96,2304]{1,0:T(8,128)(2,1)} %get-tuple-element.218), channel_id=1, source_target_pairs={{0,4},{2,6},{8,0},{10,2},{16,8},{18,10},{24,16},{26,18},{28,24},{3... | collective-permute-start | bytes 1327112 | tf_op jit(solution)/shard_map/ppermute | solution.py:233
  17.3 97.0 %collective-permute-start.35 = (bf16[96,2304]{1,0:T(8,128)(2,1)}, bf16[96,2304]{1,0:T(8,128)(2,1)}, u32[]{:S(2)}, u32[]{:S(2)}) collective-permute-start(bf16[96,2304]{1,0:T(8,128)(2,1)} %get-tuple-element.218), channel_id=1, source_target_pairs={{0,8},{2,10},{8,16},{10,18},{16,24},{18,26},{24,28},{26,30},{28,20... | collective-permute-start | bytes 1327112 | tf_op jit(solution)/shard_map/ppermute | solution.py:230
  65.6 49.7 %collective-permute-start.21 = (bf16[96,6144]{1,0:T(8,128)(2,1)S(1)}, bf16[96,6144]{1,0:T(8,128)(2,1)S(1)}, u32[]{:S(2)}, u32[]{:S(2)}) collective-permute-start(bf16[96,6144]{1,0:T(8,128)(2,1)S(1)} %get-tuple-element.178), channel_id=1, source_target_pairs={{0,4},{2,6},{8,0},{10,2},{16,8},{18,10},{24,16},{26,18},{28,24},{3... | collective-permute-start | bytes 3538952 | tf_op jit(solution)/shard_map/ppermute | solution.py:233
  104.0 80.3 %collective-permute-start.52 = (bf16[96,6144]{1,0:T(8,128)(2,1)S(1)}, bf16[96,6144]{1,0:T(8,128)(2,1)S(1)}, u32[]{:S(2)}, u32[]{:S(2)}) collective-permute-start(bf16[96,6144]{1,0:T(8,128)(2,1)S(1)} %get-tuple-element.176), channel_id=1, source_target_pairs={{0,4},{2,6},{8,0},{10,2},{16,8},{18,10},{24,16},{26,18},{28,24},{3... | collective-permute-start | bytes 3538952 | tf_op jit(solution)/shard_map/ppermute | solution.py:233
  113.5 76.1 %collective-permute-start.24 = (bf16[96,6144]{1,0:T(8,128)(2,1)S(1)}, bf16[96,6144]{1,0:T(8,128)(2,1)S(1)}, u32[]{:S(2)}, u32[]{:S(2)}) collective-permute-start(bf16[96,6144]{1,0:T(8,128)(2,1)S(1)} %get-tuple-element.178), channel_id=1, source_target_pairs={{0,8},{2,10},{8,16},{10,18},{16,24},{18,26},{24,28},{26,30},{28,20... | collective-permute-start | bytes 3538952 | tf_op jit(solution)/shard_map/ppermute | solution.py:230
  114.3 85.5 %collective-permute-start.55 = (bf16[96,6144]{1,0:T(8,128)(2,1)S(1)}, bf16[96,6144]{1,0:T(8,128)(2,1)S(1)}, u32[]{:S(2)}, u32[]{:S(2)}) collective-permute-start(bf16[96,6144]{1,0:T(8,128)(2,1)S(1)} %get-tuple-element.176), channel_id=1, source_target_pairs={{0,8},{2,10},{8,16},{10,18},{16,24},{18,26},{24,28},{26,30},{28,20... | collective-permute-start | bytes 3538952 | tf_op jit(solution)/shard_map/ppermute | solution.py:230
  114.3 62.8 %collective-permute-start.5 = (bf16[96,2304]{1,0:T(8,128)(2,1)}, bf16[96,2304]{1,0:T(8,128)(2,1)S(1)}, u32[]{:S(2)}, u32[]{:S(2)}) collective-permute-start(bf16[96,2304]{1,0:T(8,128)(2,1)} %collective-permute-done.4), channel_id=1, source_target_pairs={{0,8},{2,10},{8,16},{10,18},{16,24},{18,26},{24,28},{26,30},{28,20... | collective-permute-start | bytes 1327112 | tf_op jit(solution)/shard_map/ppermute | solution.py:230
  115.3 67.4 %collective-permute-start.36 = (bf16[96,2304]{1,0:T(8,128)(2,1)}, bf16[96,2304]{1,0:T(8,128)(2,1)S(1)}, u32[]{:S(2)}, u32[]{:S(2)}) collective-permute-start(bf16[96,2304]{1,0:T(8,128)(2,1)} %collective-permute-done.35), channel_id=1, source_target_pairs={{0,8},{2,10},{8,16},{10,18},{16,24},{18,26},{24,28},{26,30},{28,20... | collective-permute-start | bytes 1327112 | tf_op jit(solution)/shard_map/ppermute | solution.py:230
  189.5 61.5 %collective-permute-start.22 = (bf16[96,6144]{1,0:T(8,128)(2,1)S(1)}, bf16[96,6144]{1,0:T(8,128)(2,1)S(1)}, u32[]{:S(2)}, u32[]{:S(2)}) collective-permute-start(bf16[96,6144]{1,0:T(8,128)(2,1)S(1)} %collective-permute-done.21), channel_id=1, source_target_pairs={{0,4},{2,6},{8,0},{10,2},{16,8},{18,10},{24,16},{26,18},{28,24},{3... | collective-permute-start | bytes 3538952 | tf_op jit(solution)/shard_map/ppermute | solution.py:233
  197.3 55.8 %collective-permute-start.25 = (bf16[96,6144]{1,0:T(8,128)(2,1)S(1)}, bf16[96,6144]{1,0:T(8,128)(2,1)S(1)}, u32[]{:S(2)}, u32[]{:S(2)}) collective-permute-start(bf16[96,6144]{1,0:T(8,128)(2,1)S(1)} %collective-permute-done.24), channel_id=1, source_target_pairs={{0,8},{2,10},{8,16},{10,18},{16,24},{18,26},{24,28},{26,30},{28,20... | collective-permute-start | bytes 3538952 | tf_op jit(solution)/shard_map/ppermute | solution.py:230
  199.9 141.6 %collective-permute-start.53 = (bf16[96,6144]{1,0:T(8,128)(2,1)S(1)}, bf16[96,6144]{1,0:T(8,128)(2,1)S(1)}, u32[]{:S(2)}, u32[]{:S(2)}) collective-permute-start(bf16[96,6144]{1,0:T(8,128)(2,1)S(1)} %collective-permute-done.52), channel_id=1, source_target_pairs={{0,4},{2,6},{8,0},{10,2},{16,8},{18,10},{24,16},{26,18},{28,24},{3... | collective-permute-start | bytes 3538952 | tf_op jit(solution)/shard_map/ppermute | solution.py:233
  206.8 135.2 %collective-permute-start.56 = (bf16[96,6144]{1,0:T(8,128)(2,1)S(1)}, bf16[96,6144]{1,0:T(8,128)(2,1)S(1)}, u32[]{:S(2)}, u32[]{:S(2)}) collective-permute-start(bf16[96,6144]{1,0:T(8,128)(2,1)S(1)} %collective-permute-done.55), channel_id=1, source_target_pairs={{0,8},{2,10},{8,16},{10,18},{16,24},{18,26},{24,28},{26,30},{28,20... | collective-permute-start | bytes 3538952 | tf_op jit(solution)/shard_map/ppermute | solution.py:230
  251.0 76.3 %collective-permute-start.38 = (bf16[48,2304]{1,0:T(8,128)(2,1)S(1)}, bf16[48,2304]{1,0:T(8,128)(2,1)S(1)}, u32[]{:S(2)}, u32[]{:S(2)}) collective-permute-start(bf16[48,2304]{1,0:T(8,128)(2,1)S(1)} %slice.1190), channel_id=1, source_target_pairs={{0,8},{2,10},{8,16},{10,18},{16,24},{18,26},{24,28},{26,30},{28,20... | collective-permute-start | bytes 663560 | tf_op jit(solution)/shard_map/ppermute | solution.py:230
  323.6 142.3 %collective-permute-start.29 = (bf16[768,6144]{1,0:T(8,128)(2,1)}, bf16[768,6144]{1,0:T(8,128)(2,1)}, u32[]{:S(2)}, u32[]{:S(2)}) collective-permute-start(bf16[768,6144]{1,0:T(8,128)(2,1)} %constant_dynamic-update-slice_fusion.9), channel_id=1, source_target_pairs={{0,2},{2,0},{4,6},{6,4},{8,10},{10,8},{12,14},{14,12},{16,18},{18,... | collective-permute-start | bytes 28311560 | tf_op jit(solution)/shard_map/ppermute | solution.py:236
  341.4 54.8 %collective-permute-start.54 = (bf16[96,6144]{1,0:T(8,128)(2,1)S(1)}, bf16[96,6144]{1,0:T(8,128)(2,1)S(1)}, u32[]{:S(2)}, u32[]{:S(2)}) collective-permute-start(bf16[96,6144]{1,0:T(8,128)(2,1)S(1)} %collective-permute-done.53), channel_id=1, source_target_pairs={{0,4},{2,6},{8,0},{10,2},{16,8},{18,10},{24,16},{26,18},{28,24},{3... | collective-permute-start | bytes 3538952 | tf_op jit(solution)/shard_map/ppermute | solution.py:233
  342.0 51.6 %collective-permute-start.57 = (bf16[96,6144]{1,0:T(8,128)(2,1)S(1)}, bf16[96,6144]{1,0:T(8,128)(2,1)S(1)}, u32[]{:S(2)}, u32[]{:S(2)}) collective-permute-start(bf16[96,6144]{1,0:T(8,128)(2,1)S(1)} %collective-permute-done.56), channel_id=1, source_target_pairs={{0,8},{2,10},{8,16},{10,18},{16,24},{18,26},{24,28},{26,30},{28,20... | collective-permute-start | bytes 3538952 | tf_op jit(solution)/shard_map/ppermute | solution.py:230
  392.4 104.3 %collective-permute-start.40 = (bf16[768,2304]{1,0:T(8,128)(2,1)}, bf16[768,2304]{1,0:T(8,128)(2,1)}, u32[]{:S(2)}, u32[]{:S(2)}) collective-permute-start(bf16[768,2304]{1,0:T(8,128)(2,1)} %constant_dynamic-update-slice_fusion.18), channel_id=1, source_target_pairs={{0,2},{2,0},{4,6},{6,4},{8,10},{10,8},{12,14},{14,12},{16,18},{18,... | collective-permute-start | bytes 10616840 | tf_op jit(solution)/shard_map/ppermute | solution.py:236
  491.3 112.7 %collective-permute-start.60 = (bf16[768,6144]{1,0:T(8,128)(2,1)}, bf16[768,6144]{1,0:T(8,128)(2,1)}, u32[]{:S(2)}, u32[]{:S(2)}) collective-permute-start(bf16[768,6144]{1,0:T(8,128)(2,1)} %constant_dynamic-update-slice_fusion.27), channel_id=1, source_target_pairs={{0,2},{2,0},{4,6},{6,4},{8,10},{10,8},{12,14},{14,12},{16,18},{18,... | collective-permute-start | bytes 28311560 | tf_op jit(solution)/shard_map/ppermute | solution.py:236
  603.1 63.5 %collective-permute-start.187 = (bf16[256,768]{1,0:T(8,128)(2,1)S(1)}, bf16[256,768]{1,0:T(8,128)(2,1)S(1)}, u32[]{:S(2)}, u32[]{:S(2)}) collective-permute-start(bf16[256,768]{1,0:T(8,128)(2,1)S(1)} %get-tuple-element.195), channel_id=1, source_target_pairs={{0,2},{2,0},{4,6},{6,4},{8,10},{10,8},{12,14},{14,12},{16,18},{18,... | collective-permute-start | bytes 1179656 | tf_op jit(solution)/shard_map/ppermute | solution.py:236
  607.8 114.3 %collective-permute-start.131 = (bf16[256,768]{0,1:T(8,128)(2,1)}, bf16[256,768]{0,1:T(8,128)(2,1)}, u32[]{:S(2)}, u32[]{:S(2)}) collective-permute-start(bf16[256,768]{0,1:T(8,128)(2,1)} %bitcast.351), channel_id=1, source_target_pairs={{0,2},{2,0},{4,6},{6,4},{8,10},{10,8},{12,14},{14,12},{16,18},{18,... | collective-permute-start | bytes 1179656 | tf_op jit(solution)/shard_map/ppermute | solution.py:236
  658.4 69.7 %collective-permute-start.149 = (bf16[256,4096]{1,0:T(8,128)(2,1)}, bf16[256,4096]{1,0:T(8,128)(2,1)}, u32[]{:S(2)}, u32[]{:S(2)}) collective-permute-start(bf16[256,4096]{1,0:T(8,128)(2,1)} %pad_maximum_fusion), channel_id=1, source_target_pairs={{0,2},{2,0},{4,6},{6,4},{8,10},{10,8},{12,14},{14,12},{16,18},{18,... | collective-permute-start | bytes 6291464 | tf_op jit(solution)/shard_map/ppermute | solution.py:236
  666.5 55.7 %collective-permute-start.130 = (bf16[256,768]{1,0:T(8,128)(2,1)S(1)}, bf16[256,768]{1,0:T(8,128)(2,1)}, u32[]{:S(2)}, u32[]{:S(2)}) collective-permute-start(bf16[256,768]{1,0:T(8,128)(2,1)S(1)} %get-tuple-element.193), channel_id=1, source_target_pairs={{0,2},{2,0},{4,6},{6,4},{8,10},{10,8},{12,14},{14,12},{16,18},{18,... | collective-permute-start | bytes 1179656 | tf_op jit(solution)/shard_map/ppermute | solution.py:236
  722.1 409.6 %collective-permute-start.103 = (bf16[256,768]{1,0:T(8,128)(2,1)}, bf16[256,768]{1,0:T(8,128)(2,1)}, u32[]{:S(2)}, u32[]{:S(2)}) collective-permute-start(bf16[256,768]{1,0:T(8,128)(2,1)} %get-tuple-element.209), channel_id=1, source_target_pairs={{0,2},{2,0},{4,6},{6,4},{8,10},{10,8},{12,14},{14,12},{16,18},{18,... | collective-permute-start | bytes 1179656 | tf_op jit(solution)/shard_map/ppermute | solution.py:236
  739.1 258.0 %collective-permute-start.122 = (bf16[256,768]{0,1:T(8,128)(2,1)}, bf16[256,768]{0,1:T(8,128)(2,1)}, u32[]{:S(2)}, u32[]{:S(2)}) collective-permute-start(bf16[256,768]{0,1:T(8,128)(2,1)} %bitcast.352), channel_id=1, source_target_pairs={{0,2},{2,0},{4,6},{6,4},{8,10},{10,8},{12,14},{14,12},{16,18},{18,... | collective-permute-start | bytes 1179656 | tf_op jit(solution)/shard_map/ppermute | solution.py:236
  822.5 96.3 %collective-permute-start.172 = (bf16[256,2048]{1,0:T(8,128)(2,1)S(1)}, bf16[256,2048]{1,0:T(8,128)(2,1)S(1)}, u32[]{:S(2)}, u32[]{:S(2)}) collective-permute-start(bf16[256,2048]{1,0:T(8,128)(2,1)S(1)} %copy-done.18), channel_id=1, source_target_pairs={{0,2},{2,0},{4,6},{6,4},{8,10},{10,8},{12,14},{14,12},{16,18},{18,... | collective-permute-start | bytes 3145736 | tf_op jit(solution)/shard_map/ppermute | solution.py:236
  1120.9 90.4 %collective-permute-start.162 = (bf16[96,2048]{1,0:T(8,128)(2,1)}, bf16[96,2048]{1,0:T(8,128)(2,1)}, u32[]{:S(2)}, u32[]{:S(2)}) collective-permute-start(bf16[96,2048]{1,0:T(8,128)(2,1)} %get-tuple-element.79), channel_id=1, source_target_pairs={{0,4},{2,6},{8,0},{10,2},{16,8},{18,10},{24,16},{26,18},{28,24},{3... | collective-permute-start | bytes 1179656 | tf_op jit(solution)/shard_map/ppermute | solution.py:233
  1121.1 90.2 %collective-permute-start.146 = (bf16[96,2048]{1,0:T(8,128)(2,1)}, bf16[96,2048]{1,0:T(8,128)(2,1)}, u32[]{:S(2)}, u32[]{:S(2)}) collective-permute-start(bf16[96,2048]{1,0:T(8,128)(2,1)} %get-tuple-element.80), channel_id=1, source_target_pairs={{0,8},{2,10},{8,16},{10,18},{16,24},{18,26},{24,28},{26,30},{28,20... | collective-permute-start | bytes 1179656 | tf_op jit(solution)/shard_map/ppermute | solution.py:230
  1136.9 54.0 %collective-permute-start.123 = (bf16[96,1152]{1,0:T(8,128)(2,1)}, bf16[96,1152]{1,0:T(8,128)(2,1)S(1)}, u32[]{:S(2)}, u32[]{:S(2)}) collective-permute-start(bf16[96,1152]{1,0:T(8,128)(2,1)} %get-tuple-element.153), channel_id=1, source_target_pairs={{0,4},{2,6},{8,0},{10,2},{16,8},{18,10},{24,16},{26,18},{28,24},{3... | collective-permute-start | bytes 663560 | tf_op jit(solution)/shard_map/ppermute | solution.py:233
  1138.2 52.7 %collective-permute-start.105 = (bf16[96,1152]{1,0:T(8,128)(2,1)S(1)}, bf16[96,1152]{1,0:T(8,128)(2,1)}, u32[]{:S(2)}, u32[]{:S(2)}) collective-permute-start(bf16[96,1152]{1,0:T(8,128)(2,1)S(1)} %get-tuple-element.154), channel_id=1, source_target_pairs={{0,8},{2,10},{8,16},{10,18},{16,24},{18,26},{24,28},{26,30},{28,20... | collective-permute-start | bytes 663560 | tf_op jit(solution)/shard_map/ppermute | solution.py:230
  (298 other events, 5155.5 us)
Sparse Core Ops, SparseCore 0:
  1131.9 56.4 reduce-scatter.3

commit v2 on v1

--- a/solution.py
+++ b/solution.py
@@ -1,3 +1,4 @@
+import functools
 import math
 
 import jax
@@ -17,6 +18,8 @@
 EPS = 1e-05
 THETA = 100000.0
 VMEM_LIMIT = 56 * 1024 * 1024
+KERNEL_VMEM = 62 * 1024 * 1024
+MESH = pl.DeviceIdType.MESH
 BF16 = jnp.bfloat16
 F32 = jnp.float32
 
@@ -63,11 +66,8 @@
     return 256 if keys <= 2048 else 64
 
 
-def gathered(own_ref, sib_ref):
-    count = own_ref.shape[0]
-    return jnp.concatenate(
-        [own_ref[j] for j in range(count)] + [sib_ref[j] for j in range(count)], axis=1
-    )
+def gathered(ref):
+    return jnp.concatenate([ref[j] for j in range(ref.shape[0])], axis=1)
 
 
 def mask_rows(kpos_ref, qpos_ref, qstart_ref, start, rows):
@@ -94,12 +94,10 @@
     return jnp.concatenate(out, axis=0) if len(out) > 1 else out[0]
 
 
-def attend_kernel(
-    q_ref, ko_ref, ks_ref, vo_ref, vs_ref, kpos_ref, qpos_ref, qstart_ref, o_ref, lse_ref
-):
+def attend_kernel(q_ref, k_ref, v_ref, kpos_ref, qpos_ref, qstart_ref, o_ref, lse_ref):
     total = q_ref.shape[2]
-    kt = gathered(ko_ref, ks_ref)
-    vt = gathered(vo_ref, vs_ref)
+    kt = gathered(k_ref)
+    vt = gathered(v_ref)
     tile = min(total, row_tile(kt.shape[1]))
     for at in range(0, total, tile):
         q = q_ref[0, 0, at : at + tile, :]
@@ -116,22 +114,18 @@
     q_ref,
     do_ref,
     lse_ref,
-    ko_ref,
-    ks_ref,
-    vo_ref,
-    vs_ref,
+    k_ref,
+    v_ref,
     kpos_ref,
     qpos_ref,
     qstart_ref,
     dq_ref,
-    dko_ref,
-    dks_ref,
-    dvo_ref,
-    dvs_ref,
+    dk_ref,
+    dv_ref,
 ):
     total = q_ref.shape[2]
-    kt = gathered(ko_ref, ks_ref)
-    vt = gathered(vo_ref, vs_ref)
+    kt = gathered(k_ref)
+    vt = gathered(v_ref)
     tile = min(total, row_tile(kt.shape[1]))
     dkt = None
     dvt = None
@@ -148,17 +142,14 @@
         dv_part = dot_tn(grad, probs.astype(BF16))
         dkt = dk_part if dkt is None else dkt + dk_part
         dvt = dv_part if dvt is None else dvt + dv_part
-    count = dko_ref.shape[0]
-    for j in range(count):
-        dko_ref[j] = dkt[:, j * ROWS : (j + 1) * ROWS].astype(BF16)
-        dks_ref[j] = dkt[:, (count + j) * ROWS : (count + j + 1) * ROWS].astype(BF16)
-        dvo_ref[j] = dvt[:, j * ROWS : (j + 1) * ROWS].astype(BF16)
-        dvs_ref[j] = dvt[:, (count + j) * ROWS : (count + j + 1) * ROWS].astype(BF16)
-
-
-def attention_specs(q, kv_own, kpos):
-    slots = kv_own.shape[0]
-    kv_heads = kv_own.shape[1] // (2 * HEAD_SIZE)
+    for j in range(dk_ref.shape[0]):
+        dk_ref[j] = dkt[:, j * ROWS : (j + 1) * ROWS].astype(BF16)
+        dv_ref[j] = dvt[:, j * ROWS : (j + 1) * ROWS].astype(BF16)
+
+
+def attention_specs(q, kv, kpos):
+    slots = kv.shape[0]
+    kv_heads = kv.shape[1] // (2 * HEAD_SIZE)
     keys = kpos.shape[2]
     rows = q.shape[2]
     unit = pl.BlockSpec((1, 1, rows, HEAD_SIZE), lambda s, h: (s, h, 0, 0))
@@ -170,14 +161,14 @@
     return kv_heads, unit, column, k_spec, v_spec, kpos_spec, q_spec
 
 
-def attend_forward(q, kv_own, kv_sib, kpos, qpos, qstart):
-    kv_heads, unit, column, k_spec, v_spec, kpos_spec, q_spec = attention_specs(q, kv_own, kpos)
+def attend_forward(q, kv, kpos, qpos, qstart):
+    kv_heads, unit, column, k_spec, v_spec, kpos_spec, q_spec = attention_specs(q, kv, kpos)
     rows, keys = q.shape[2], kpos.shape[2]
     work = SEQS * kv_heads * rows * keys
     return pl.pallas_call(
         attend_kernel,
         grid=(SEQS, kv_heads),
-        in_specs=[unit, k_spec, k_spec, v_spec, v_spec, kpos_spec, q_spec, q_spec],
+        in_specs=[unit, k_spec, v_spec, kpos_spec, q_spec, q_spec],
         out_specs=[unit, column],
         out_shape=[
             jax.ShapeDtypeStruct(q.shape, BF16),
@@ -187,29 +178,448 @@
         cost_estimate=pl.CostEstimate(
             flops=8 * HEAD_SIZE * work, bytes_accessed=8 * 2**20, transcendentals=work
         ),
-    )(q, kv_own, kv_sib, kv_own, kv_sib, kpos, qpos, qstart)
-
-
-def attend_backward(q, grad, lse, kv_own, kv_sib, kpos, qpos, qstart):
-    kv_heads, unit, column, k_spec, v_spec, kpos_spec, q_spec = attention_specs(q, kv_own, kpos)
+    )(q, kv, kv, kpos, qpos, qstart)
+
+
+def attend_backward(q, grad, lse, kv, kpos, qpos, qstart):
+    kv_heads, unit, column, k_spec, v_spec, kpos_spec, q_spec = attention_specs(q, kv, kpos)
     rows, keys = q.shape[2], kpos.shape[2]
     work = SEQS * kv_heads * rows * keys
-    slots = kv_own.shape[0]
+    slots = kv.shape[0]
     grad_spec = pl.BlockSpec((slots, HEAD_SIZE, ROWS), lambda s, h: (0, h, s))
     grad_shape = jax.ShapeDtypeStruct((slots, kv_heads * HEAD_SIZE, SEQS * ROWS), BF16)
     return pl.pallas_call(
         attend_back_kernel,
         grid=(SEQS, kv_heads),
-        in_specs=[
-            unit, unit, column, k_spec, k_spec, v_spec, v_spec, kpos_spec, q_spec, q_spec
-        ],
-        out_specs=[unit, grad_spec, grad_spec, grad_spec, grad_spec],
-        out_shape=[jax.ShapeDtypeStruct(q.shape, F32)] + [grad_shape] * 4,
+        in_specs=[unit, unit, column, k_spec, v_spec, kpos_spec, q_spec, q_spec],
+        out_specs=[unit, grad_spec, grad_spec],
+        out_shape=[jax.ShapeDtypeStruct(q.shape, F32)] + [grad_shape] * 2,
         compiler_params=pltpu.CompilerParams(vmem_limit_bytes=VMEM_LIMIT),
         cost_estimate=pl.CostEstimate(
             flops=20 * HEAD_SIZE * work, bytes_accessed=16 * 2**20, transcendentals=work
         ),
-    )(q, grad, lse, kv_own, kv_sib, kv_own, kv_sib, kpos, qpos, qstart)
+    )(q, grad, lse, kv, kv, kpos, qpos, qstart)
+
+
+def ring_neighbours(chips):
+    ctx = lax.axis_index("ctx")
+    chip, core, half = ctx // 2, ctx % 2, chips // 2
+    odd = chip % 2
+    place = odd * (chips - 1 - chip // 2) + (1 - odd) * (chip // 2)
+
+    def device(at):
+        far = at // half
+        return ((1 - far) * 2 * at + far * (2 * (chips - 1 - at) + 1)) * 2 + core
+
+    return device((place + 1) % chips), device((place + chips - 1) % chips), ctx + 1 - 2 * core
+
+
+class Links:
+    def __init__(self, chips, send_sems, recv_sems):
+        self.chips = chips
+        self.right, self.left, self.sib = ring_neighbours(chips)
+        self.head = lax.axis_index("head")
+        self.ctx = lax.axis_index("ctx")
+        self.send_sems, self.recv_sems = send_sems, recv_sems
+        self.used = 0
+        self.started = []
+
+    def greet(self):
+        barrier = pltpu.get_barrier_semaphore()
+        for target in (self.right, self.left, self.sib):
+            pl.semaphore_signal(barrier, inc=1, device_id=(target, self.head), device_id_type=MESH)
+        pl.semaphore_signal(
+            barrier, inc=1, device_id=(self.ctx, 1 - self.head), device_id_type=MESH
+        )
+        pl.semaphore_wait(barrier, 4)
+
+    def copy(self, src, dst, target):
+        copy = pltpu.make_async_remote_copy(
+            src_ref=src,
+            dst_ref=dst,
+            send_sem=self.send_sems.at[self.used],
+            recv_sem=self.recv_sems.at[self.used],
+            device_id=target,
+            device_id_type=MESH,
+        )
+        self.used += 1
+        copy.start()
+        self.started.append(copy)
+        return copy
+
+    def to_right(self, src, dst):
+        return self.copy(src, dst, (self.right, self.head))
+
+    def to_left(self, src, dst):
+        return self.copy(src, dst, (self.left, self.head))
+
+    def to_sibling(self, src, dst):
+        return self.copy(src, dst, (self.sib, self.head))
+
+    def to_head(self, src, dst):
+        return self.copy(src, dst, (self.ctx, 1 - self.head))
+
+    def finish(self):
+        for copy in self.started:
+            copy.wait_send()
+
+
+class RingGather:
+    def __init__(self, links, ref, chains, first=None):
+        self.links, self.ref, self.chains = links, ref, chains
+        self.first = first
+        self.moving = {}
+        self.arriving = []
+        self.steps = links.chips // 2
+        self.events = [(c, s) for s in range(1, self.steps + 1) for c in range(len(chains))]
+
+    @staticmethod
+    def copies(chips, chains):
+        return chains * (chips + chips)
+
+    def window(self, slot, chain, part=None):
+        r0, rn, c0, cn = self.chains[chain]
+        if part is not None:
+            rn = rn // 2
+            r0 = r0 + part * rn
+        if slot == 0 and self.first is not None:
+            return self.first.at[pl.ds(r0, rn), pl.ds(c0, cn)]
+        return self.ref.at[slot, pl.ds(r0, rn), pl.ds(c0, cn)]
+
+    def share(self, slot, chain):
+        r0, rn, c0, cn = self.chains[chain]
+        there = self.ref.at[self.links.chips + slot, pl.ds(r0, rn), pl.ds(c0, cn)]
+        self.arriving.append(self.links.to_sibling(self.window(slot, chain), there))
+
+    def issue(self, event):
+        chain, step = event
+        chips = self.links.chips
+        last = step == self.steps
+        up_from, up_to = (chips - step + 1) % chips, chips - step
+        r0, rn, c0, cn = self.chains[chain]
+
+        def there(slot, part):
+            rows = (r0, rn) if part is None else (r0 + part * (rn // 2), rn // 2)
+            return self.ref.at[slot, pl.ds(*rows), pl.ds(c0, cn)]
+
+        up = 0 if last else None
+        down = 1 if last else None
+        self.moving[event] = (
+            self.links.to_right(self.window(up_from, chain, up), there(up_to, up)),
+            self.links.to_left(self.window(step - 1, chain, down), there(step, down)),
+        )
+        if step == 1:
+            self.share(0, chain)
+
+    def land(self, event):
+        chain, step = event
+        for copy in self.moving[event]:
+            copy.wait_recv()
+        self.share(self.links.chips - step, chain)
+        if step != self.steps:
+            self.share(step, chain)
+
+    def settle(self):
+        for copy in self.arriving:
+            copy.wait_recv()
+
+
+class Queue:
+    def __init__(self, rings, depth=2):
+        self.items = [(ring, event) for ring in rings for event in ring.events]
+        self.depth = depth
+        self.landed = 0
+        self.issued = 0
+
+    def fill(self):
+        while self.issued < len(self.items) and self.issued < self.landed + self.depth:
+            ring, event = self.items[self.issued]
+            ring.issue(event)
+            self.issued += 1
+
+    def pump(self, count=1):
+        for _ in range(count):
+            if self.landed < len(self.items):
+                ring, event = self.items[self.landed]
+                ring.land(event)
+                self.landed += 1
+                self.fill()
+
+    def through(self, ring):
+        last = max(i for i, item in enumerate(self.items) if item[0] is ring)
+        self.pump(last + 1 - self.landed)
+
+
+TILE = 512
+
+
+def rms_inverse(rows):
+    return lax.rsqrt(jnp.mean(rows * rows, axis=-1, keepdims=True) + EPS)
+
+
+def forward_kernel(dims, *refs):
+    layers, chips, width, q_width, kv_width, ff = dims
+    slots = 2 * chips
+    it = iter(refs)
+    x_ref = next(it)
+    shards = [next(it) for _ in range(2 * layers)]
+    cos_ref, sin_ref, kpos_ref, qpos_ref, qstart_ref = (next(it) for _ in range(5))
+    weights = [next(it) for _ in range(2 * layers)]
+    (
+        kv_ref,
+        normed_a_ref,
+        qt_ref,
+        lse_ref,
+        att_ref,
+        middle_ref,
+        normed_m_ref,
+        gate_ref,
+        up_ref,
+        act_ref,
+        x_out_ref,
+        gain_ref,
+    ) = (next(it) for _ in range(12))
+    (
+        wt, wo, acc, proj_t, att_t, b_send, b_recv, gain_block, send_sems, recv_sems, load_sems, own_sems
+    ) = (next(it) for _ in range(12))
+
+    rows = x_ref.shape[0]
+    db = width // slots
+    heads_kv = kv_width // HEAD_SIZE
+    group = q_width // kv_width
+    qkv_width = q_width + 2 * kv_width
+    links = Links(chips, send_sems, recv_sems)
+    own_copies = []
+    for i, (shard, weight) in enumerate(zip(shards, weights)):
+        own_copies.append(pltpu.make_async_copy(shard, weight.at[0], own_sems.at[i]))
+        own_copies[-1].start()
+    links.greet()
+
+    rings = []
+    for shard, weight in zip(shards, weights):
+        wide = shard.shape[1]
+        cut = (wide // 256) * 128
+        rings.append(
+            RingGather(links, weight, [(0, db, 0, cut), (0, db, cut, wide - cut)], first=shard)
+        )
+    queue = Queue(rings)
+    queue.fill()
+
+    def ready(i):
+        queue.through(rings[i])
+        rings[i].settle()
+
+    def load(i, column, wide, target, sem):
+        copy = pltpu.make_async_copy(
+            weights[i].at[:, :, pl.ds(column, wide)], target, load_sems.at[sem]
+        )
+        copy.start()
+        return copy
+
+    def flat(ref):
+        return ref[...].reshape(width, ref.shape[-1])
+
+    ready(0)
+    for copy in own_copies:
+        copy.wait()
+    side = qkv_width + q_width
+    load(0, side, 128, gain_block, 0).wait()
+    gain_ref[...] = flat(gain_block).astype(F32).T[: gain_ref.shape[0], :]
+
+    for layer in range(layers):
+        attn, mlp = 2 * layer, 2 * layer + 1
+        if layer:
+            ready(attn)
+        tiles = [load(attn, t * TILE, TILE, wt.at[t], t) for t in range(qkv_width // TILE)]
+        out_load = load(attn, qkv_width, q_width, wo, 6)
+
+        x = x_ref[...] if layer == 0 else x_out_ref[layer - 1]
+        gain_a = gain_ref[layer : layer + 1, :]
+        normed_a_ref[layer, 0:rows, :] = (x * rms_inverse(x) * gain_a).astype(BF16)
+        swap = links.to_head(
+            normed_a_ref.at[layer, pl.ds(0, rows), :], normed_a_ref.at[layer, pl.ds(rows, rows), :]
+        )
+        for t, tile in enumerate(tiles):
+            tile.wait()
+            part = dot(normed_a_ref[layer, 0:rows, :], flat(wt.at[t]))
+            proj_t[t * TILE : (t + 1) * TILE, 0:rows] = part.T
+        swap.wait_recv()
+        for t in range(len(tiles)):
+            part = dot(normed_a_ref[layer, rows : 2 * rows, :], flat(wt.at[t]))
+            proj_t[t * TILE : (t + 1) * TILE, rows : 2 * rows] = part.T
+        queue.pump()
+
+        cosine, sine = cos_ref[...], sin_ref[...]
+
+        def turned(at):
+            low = proj_t[at : at + HALF, :]
+            high = proj_t[at + HALF : at + HEAD_SIZE, :]
+            return low * cosine - high * sine, high * cosine + low * sine
+
+        for h in range(heads_kv):
+            low, high = turned(q_width + h * HEAD_SIZE)
+            kv_ref[layer, 0, h * HEAD_SIZE : h * HEAD_SIZE + HALF, :] = low.astype(BF16)
+            kv_ref[layer, 0, h * HEAD_SIZE + HALF : (h + 1) * HEAD_SIZE, :] = high.astype(BF16)
+        kv_ref[layer, 0, kv_width : 2 * kv_width, :] = proj_t[
+            q_width + kv_width : qkv_width, :
+        ].astype(BF16)
+        wide = kv_ref.shape[-1]
+        kv_ring = RingGather(
+            links,
+            kv_ref.at[layer],
+            [(0, kv_width, 0, wide), (kv_width, kv_width, 0, wide)],
+        )
+        kv_queue = Queue([kv_ring])
+        kv_queue.fill()
+        scale = HEAD_SIZE ** (-0.5)
+        for h in range(q_width // HEAD_SIZE):
+            low, high = turned(h * HEAD_SIZE)
+            qt_ref[layer, h * HEAD_SIZE : h * HEAD_SIZE + HALF, :] = (low * scale).astype(BF16)
+            qt_ref[layer, h * HEAD_SIZE + HALF : (h + 1) * HEAD_SIZE, :] = (high * scale).astype(
+                BF16
+            )
+        for step in range(len(kv_queue.items)):
+            kv_queue.pump()
+            if step % 3 == 2:
+                queue.pump()
+        kv_ring.settle()
+
+        def unit(u, carry):
+            s, h = u // heads_kv, u % heads_kv
+            k_rows = pl.ds(pl.multiple_of(h * HEAD_SIZE, HEAD_SIZE), HEAD_SIZE)
+            v_rows = pl.ds(pl.multiple_of(kv_width + h * HEAD_SIZE, HEAD_SIZE), HEAD_SIZE)
+            lanes = pl.ds(pl.multiple_of(s * ROWS, ROWS), ROWS)
+            kt = jnp.concatenate([kv_ref[layer, j, k_rows, lanes] for j in range(slots)], axis=1)
+            vt = jnp.concatenate([kv_ref[layer, j, v_rows, lanes] for j in range(slots)], axis=1)
+            q_rows = [
+                pl.ds(pl.multiple_of((h * group + g) * HEAD_SIZE, HEAD_SIZE), HEAD_SIZE)
+                for g in range(group)
+            ]
+            qt = jnp.concatenate([qt_ref[layer, at, lanes] for at in q_rows], axis=1)
+            kpos, qpos, qstart = kpos_ref[s], qpos_ref[s], qstart_ref[s]
+            allowed = (kpos <= qpos) & (kpos >= qstart)
+            scores = masked(dot_tn(qt, kt), [allowed] * group)
+            top = jnp.max(scores, axis=1, keepdims=True)
+            raised = jnp.exp(scores - top)
+            norm = jnp.sum(raised, axis=1, keepdims=True)
+            probs = (raised * (1.0 / norm)).astype(BF16)
+            mixed = dot_nt(vt, probs)
+            for g, at in enumerate(q_rows):
+                att_t[at, lanes] = mixed[:, g * ROWS : (g + 1) * ROWS]
+            lse_ref[layer, u] = top + jnp.log(norm)
+            return carry
+
+        units = SEQS * heads_kv
+        for at in range(0, units, 2):
+            lax.fori_loop(at, at + 2, unit, 0)
+            queue.pump()
+        att_ref[layer] = att_t[...].T.astype(BF16)
+
+        out_load.wait()
+        branch = (layer * 2) % b_send.shape[0]
+        other = dot_nt(att_ref[layer, rows : 2 * rows, :], flat(wo))
+        b_send[branch] = other.astype(BF16)
+        swap = links.to_head(b_send.at[branch], b_recv.at[branch])
+        mine = dot_nt(att_ref[layer, 0:rows, :], flat(wo))
+        queue.pump()
+        swap.wait_recv()
+        middle = x + mine + b_recv[branch].astype(F32)
+        middle_ref[layer] = middle
+        gain_m = gain_ref[layers + layer : layers + layer + 1, :]
+        normed_m_ref[layer, 0:rows, :] = (middle * rms_inverse(middle) * gain_m).astype(BF16)
+        swap = links.to_head(
+            normed_m_ref.at[layer, pl.ds(0, rows), :], normed_m_ref.at[layer, pl.ds(rows, rows), :]
+        )
+        ready(mlp)
+
+        def load_tile(t):
+            at = (t % 2) * 3
+            return [
+                load(mlp, part * ff + t * TILE, TILE, wt.at[at + part], at + part)
+                for part in range(3)
+            ]
+
+        pending = load_tile(0)
+        swap.wait_recv()
+        normed = normed_m_ref[layer]
+        count = ff // TILE
+        for t in range(count):
+            following = load_tile(t + 1) if t + 1 < count else None
+            for copy in pending:
+                copy.wait()
+            at = (t % 2) * 3
+            columns = slice(t * TILE, (t + 1) * TILE)
+            gate = dot(normed, flat(wt.at[at]))
+            up = dot(normed, flat(wt.at[at + 1]))
+            act = (gate * jax.nn.sigmoid(gate) * up).astype(BF16)
+            gate_ref[layer, :, columns] = gate.astype(BF16)
+            up_ref[layer, :, columns] = up.astype(BF16)
+            act_ref[layer, :, columns] = act
+            down = dot_nt(act, flat(wt.at[at + 2]))
+            if t == 0:
+                acc[...] = down
+            else:
+                acc[...] += down
+            pending = following
+            queue.pump(2)
+        branch = (layer * 2 + 1) % b_send.shape[0]
+        b_send[branch] = acc[rows : 2 * rows, :].astype(BF16)
+        swap = links.to_head(b_send.at[branch], b_recv.at[branch])
+        swap.wait_recv()
+        x_out_ref[layer] = middle_ref[layer] + acc[0:rows, :] + b_recv[branch].astype(F32)
+    links.finish()
+
+
+def forward(x, shards, cosine, sine, kpos, qpos, qstart, chips, q_width, kv_width, ff):
+    layers = len(shards) // 2
+    rows, width = x.shape
+    db = shards[0].shape[0]
+    slots = 2 * chips
+    group = q_width // kv_width
+    tokens = 2 * rows
+    units = SEQS * kv_width // HEAD_SIZE
+    dims = (layers, chips, width, q_width, kv_width, ff)
+    copies = (2 * layers + layers) * RingGather.copies(chips, 2) + 4 * layers
+    any_spec = pl.BlockSpec(memory_space=pl.ANY)
+    vmem = pl.BlockSpec(memory_space=pltpu.VMEM)
+    saved = [
+        jax.ShapeDtypeStruct((layers, slots, 2 * kv_width, tokens), BF16),
+        jax.ShapeDtypeStruct((layers, tokens, width), BF16),
+        jax.ShapeDtypeStruct((layers, q_width, tokens), BF16),
+        jax.ShapeDtypeStruct((layers, units, group * ROWS, 1), F32),
+        jax.ShapeDtypeStruct((layers, tokens, q_width), BF16),
+        jax.ShapeDtypeStruct((layers, rows, width), F32),
+        jax.ShapeDtypeStruct((layers, tokens, width), BF16),
+        jax.ShapeDtypeStruct((layers, tokens, ff), BF16),
+        jax.ShapeDtypeStruct((layers, tokens, ff), BF16),
+        jax.ShapeDtypeStruct((layers, tokens, ff), BF16),
+        jax.ShapeDtypeStruct((layers, rows, width), F32),
+        jax.ShapeDtypeStruct((2 * layers, width), F32),
+    ]
+    out = pl.pallas_call(
+        functools.partial(forward_kernel, dims),
+        out_shape=[jax.ShapeDtypeStruct((slots,) + shard.shape, BF16) for shard in shards] + saved,
+        in_specs=[vmem] + [any_spec] * len(shards) + [vmem] * 5,
+        out_specs=[any_spec] * len(shards) + [vmem] * len(saved),
+        scratch_shapes=[
+            pltpu.VMEM((6, slots, db, TILE), BF16),
+            pltpu.VMEM((slots, db, q_width), BF16),
+            pltpu.VMEM((tokens, width), F32),
+            pltpu.VMEM((q_width + 2 * kv_width, tokens), F32),
+            pltpu.VMEM((q_width, tokens), F32),
+            pltpu.VMEM((2 * layers, rows, width), BF16),
+            pltpu.VMEM((2 * layers, rows, width), BF16),
+            pltpu.VMEM((slots, db, 128), BF16),
+            pltpu.SemaphoreType.DMA((copies,)),
+            pltpu.SemaphoreType.DMA((copies,)),
+            pltpu.SemaphoreType.DMA((7,)),
+            pltpu.SemaphoreType.DMA((len(shards),)),
+        ],
+        compiler_params=pltpu.CompilerParams(
+            collective_id=0, has_side_effects=True, vmem_limit_bytes=KERNEL_VMEM
+        ),
+    )(x, *shards, cosine, sine, kpos, qpos, qstart)
+    return out[: len(shards)], out[len(shards) :]
 
 
 def build(n_ctx):
@@ -262,9 +672,9 @@
                 low, high = low.astype(BF16), high.astype(BF16)
         return low, high
 
-    def weight_gather(shard):
+    def gather(shard):
         own = jnp.concatenate(ring_gather(shard), axis=0)
-        return own, swap_core(own)
+        return jnp.concatenate([own, swap_core(own)], axis=0)
 
     def weight_scatter(grad):
         db, cut = grad.shape[0] // chips, grad.shape[1] // 2
@@ -326,18 +736,6 @@
                 preferred_element_type=F32,
             )
 
-        fetched = []
-        for layer in range(layers):
-            attn_shard = jnp.concatenate(
-                [w_query[layer], w_key[layer], w_value[layer], w_out[layer].T], axis=1
-            )
-            mlp_shard = jnp.concatenate([w_gate[layer], w_up[layer], w_down[layer].T], axis=1)
-            fetched.append((weight_gather(attn_shard), weight_gather(mlp_shard)))
-        gains = lax.all_gather(
-            jnp.concatenate([attn_gain, mlp_gain], axis=0), "ctx", axis=1, tiled=True
-        )
-        gains = reorder(gains)
-
         offsets = jnp.arange(BLK, dtype=jnp.int32)
         first = (head == 0)[..., None, None]
         order = jnp.where(first, block_order, block_order[::-1])
@@ -365,14 +763,10 @@
             return parts[:own_rows] + swap_head(parts[own_rows:].astype(BF16)).astype(F32)
 
         def project(rows, weight, lo, hi):
-            own, sib = weight
-            return dot(rows[:, :side], own[:, lo:hi]) + dot(rows[:, side:], sib[:, lo:hi])
+            return dot(rows, weight[:, lo:hi])
 
         def project_back(rows, weight, lo, hi):
-            own, sib = weight
-            return jnp.concatenate(
-                [dot_nt(rows, own[:, lo:hi]), dot_nt(rows, sib[:, lo:hi])], axis=1
-            )
+            return dot_nt(rows, weight[:, lo:hi])
 
         def weight_grad(left, right):
             lefts = jnp.concatenate([left[:, :side], swap_core(left[:, side:])], axis=0)
@@ -389,59 +783,127 @@
 
         qkv_width = q_width + 2 * kv_width
         attn_width = qkv_width + q_width
-        residual = reorder(hidden_in)
         grad_res = reorder(cotangent)
-        records = []
-        for layer in range(layers):
-            attn_w, mlp_w = fetched[layer]
-            gain_a, gain_m = gains[layer], gains[layers + layer]
-            residual_in = residual
-            inverse_a = lax.rsqrt(jnp.mean(residual * residual, axis=-1, keepdims=True) + EPS)
-            normed_a = both_rows((residual * inverse_a * gain_a).astype(BF16))
-            projected = project(normed_a, attn_w, 0, qkv_width)
-            q_rows = rotate(
-                projected[:, :q_width].reshape(token_rows, heads_q, HEAD_SIZE), cosine, sine_table
+        attn_shards = [
+            jnp.concatenate(
+                [w_query[layer], w_key[layer], w_value[layer], w_out[layer].T], axis=1
             )
-            queries = units((q_rows * scale_q).astype(BF16).reshape(token_rows, q_width))
-            keys = rotate(
-                projected[:, q_width : q_width + kv_width].reshape(
-                    token_rows, heads_kv, HEAD_SIZE
-                ),
-                cosine,
-                sine_table,
-            ).reshape(token_rows, kv_width)
-            kv_shard = jnp.concatenate([keys, projected[:, q_width + kv_width :]], axis=1)
-            kv_own = jnp.stack(ring_gather(kv_shard.astype(BF16).T), axis=0)
-            kv_sib = swap_core(kv_own)
-            mixed, lse = attend_forward(queries, kv_own, kv_sib, kpos, qpos, qstart)
-            attended = from_units(mixed)
-            middle = residual + to_owner(project_back(attended, attn_w, qkv_width, attn_width))
-            inverse_m = lax.rsqrt(jnp.mean(middle * middle, axis=-1, keepdims=True) + EPS)
-            normed_m = both_rows((middle * inverse_m * gain_m).astype(BF16))
-            gate_up = project(normed_m, mlp_w, 0, 2 * ff_width)
-            gate_part, up_part = gate_up[:, :ff_width], gate_up[:, ff_width:]
-            activated = (jax.nn.silu(gate_part) * up_part).astype(BF16)
-            residual = middle + to_owner(
-                project_back(activated, mlp_w, 2 * ff_width, 3 * ff_width)
+            for layer in range(layers)
+        ]
+        mlp_shards = [
+            jnp.concatenate([w_gate[layer], w_up[layer], w_down[layer].T], axis=1)
+            for layer in range(layers)
+        ]
+
+        def forward_by_ops(residual):
+            gains = lax.all_gather(
+                jnp.concatenate([attn_gain, mlp_gain], axis=0), "ctx", axis=1, tiled=True
             )
-            records.append(
-                (
-                    residual_in,
-                    inverse_a,
-                    normed_a,
-                    queries,
-                    kv_own,
-                    kv_sib,
-                    lse,
-                    attended,
-                    middle,
-                    inverse_m,
-                    normed_m,
-                    gate_part,
-                    up_part,
-                    activated,
+            gains = reorder(gains)
+            fetched = [
+                (gather(attn), gather(mlp)) for attn, mlp in zip(attn_shards, mlp_shards)
+            ]
+            records = []
+            for layer in range(layers):
+                attn_w, mlp_w = fetched[layer]
+                gain_a, gain_m = gains[layer], gains[layers + layer]
+                residual_in = residual
+                normed_a = both_rows((residual * rms_inverse(residual) * gain_a).astype(BF16))
+                projected = project(normed_a, attn_w, 0, qkv_width)
+                q_rows = rotate(
+                    projected[:, :q_width].reshape(token_rows, heads_q, HEAD_SIZE),
+                    cosine,
+                    sine_table,
                 )
+                queries = units((q_rows * scale_q).astype(BF16).reshape(token_rows, q_width))
+                keys = rotate(
+                    projected[:, q_width : q_width + kv_width].reshape(
+                        token_rows, heads_kv, HEAD_SIZE
+                    ),
+                    cosine,
+                    sine_table,
+                ).reshape(token_rows, kv_width)
+                kv_shard = jnp.concatenate([keys, projected[:, q_width + kv_width :]], axis=1)
+                kv_own = jnp.stack(ring_gather(kv_shard.astype(BF16).T), axis=0)
+                kv = jnp.concatenate([kv_own, swap_core(kv_own)], axis=0)
+                mixed, lse = attend_forward(queries, kv, kpos, qpos, qstart)
+                attended = from_units(mixed)
+                middle = residual + to_owner(
+                    project_back(attended, attn_w, qkv_width, attn_width)
+                )
+                normed_m = both_rows((middle * rms_inverse(middle) * gain_m).astype(BF16))
+                gate_up = project(normed_m, mlp_w, 0, 2 * ff_width)
+                gate_part, up_part = gate_up[:, :ff_width], gate_up[:, ff_width:]
+                activated = (jax.nn.silu(gate_part) * up_part).astype(BF16)
+                residual = middle + to_owner(
+                    project_back(activated, mlp_w, 2 * ff_width, 3 * ff_width)
+                )
+                records.append(
+                    (
+                        residual_in,
+                        normed_a,
+                        queries,
+                        kv,
+                        lse,
+                        attended,
+                        middle,
+                        normed_m,
+                        gate_part,
+                        up_part,
+                        activated,
+                    )
+                )
+            return fetched, gains, records, residual
+
+        def forward_by_kernel(residual):
+            columns = jnp.concatenate([attn_gain, mlp_gain], axis=0).T
+            columns = jnp.pad(columns, ((0, 0), (0, 128 - columns.shape[1])))
+            shards = []
+            for layer in range(layers):
+                attn = attn_shards[layer]
+                if layer == 0:
+                    attn = jnp.concatenate([attn, columns], axis=1)
+                shards += [attn, mlp_shards[layer]]
+            weights, saved = forward(
+                residual,
+                shards,
+                cosine.T,
+                sine_table.T,
+                kpos,
+                qpos,
+                qstart,
+                chips,
+                q_width,
+                kv_width,
+                ff_width,
             )
+            weights = [weight.reshape(width, weight.shape[-1]) for weight in weights]
+            fetched = [(weights[2 * layer], weights[2 * layer + 1]) for layer in range(layers)]
+            kv, normed_a, qt, lse, att, middle, normed_m, gate, up, act, x_out, gains = saved
+            records = []
+            for layer in range(layers):
+                q_units = qt[layer].reshape(heads_kv, group, HEAD_SIZE, SEQS, ROWS)
+                q_units = q_units.transpose(3, 0, 1, 4, 2)
+                records.append(
+                    (
+                        residual if layer == 0 else x_out[layer - 1],
+                        normed_a[layer],
+                        q_units.reshape(SEQS, heads_kv, group * ROWS, HEAD_SIZE),
+                        kv[layer],
+                        lse[layer].reshape(SEQS, heads_kv, group * ROWS, 1),
+                        att[layer],
+                        middle[layer],
+                        normed_m[layer],
+                        gate[layer].astype(F32),
+                        up[layer].astype(F32),
+                        act[layer],
+                    )
+                )
+            return fetched, gains, records, x_out[layers - 1]
+
+        in_kernel = n_ctx * ROWS <= 2048
+        run_forward = forward_by_kernel if in_kernel else forward_by_ops
+        fetched, gains, records, residual = run_forward(reorder(hidden_in))
         out_hidden = lax.dot_general(
             residual.astype(BF16), to_ring, (((1,), (1,)), ((), ())), preferred_element_type=F32
         ).astype(BF16)
@@ -461,20 +923,18 @@
             gain_a, gain_m = gains[layer], gains[layers + layer]
             (
                 residual_in,
-                inverse_a,
                 normed_a,
                 queries,
-                kv_own,
-                kv_sib,
+                kv,
                 lse,
                 attended,
                 middle,
-                inverse_m,
                 normed_m,
                 gate_part,
                 up_part,
                 activated,
             ) = records[layer]
+            inverse_a, inverse_m = rms_inverse(residual_in), rms_inverse(middle)
             grad_rows_m = both_rows(grad_res.astype(BF16))
             grad_act = project(grad_rows_m, mlp_w, 2 * ff_width, 3 * ff_width)
             sigmoid_g = jax.nn.sigmoid(gate_part)
@@ -490,14 +950,14 @@
             grad_rows_a = both_rows(grad_res.astype(BF16))
             grad_attended = project(grad_rows_a, attn_w, qkv_width, attn_width).astype(BF16)
             d_out = weight_grad(grad_rows_a, attended)
-            grad_q, dk_own, dk_sib, dv_own, dv_sib = attend_backward(
-                queries, units(grad_attended), lse, kv_own, kv_sib, kpos, qpos, qstart
+            grad_q, dk, dv = attend_backward(
+                queries, units(grad_attended), lse, kv, kpos, qpos, qstart
             )
-            dk_back, dv_back = swap_core(dk_sib), swap_core(dv_sib)
+            dk_back, dv_back = swap_core(dk[chips:]), swap_core(dv[chips:])
             kv_slots = [
                 (
-                    dk_own[j].astype(F32) + dk_back[j].astype(F32),
-                    dv_own[j].astype(F32) + dv_back[j].astype(F32),
+                    dk[j].astype(F32) + dk_back[j].astype(F32),
+                    dv[j].astype(F32) + dv_back[j].astype(F32),
                 )
                 for j in range(chips)
             ]

time: 1270 us -> 1100 us (0.87)
  Pallas kernels: 64.4 us -> 441 us
  waiting for transfers between devices: 636 us -> 279 us
  starting transfers between devices: 197 us -> 124 us
  matrix products: 143 us -> 88.5 us
  local copies, waits for them, and re-layouts: 98.5 us -> 62.1 us
  blocking collectives: 30.7 us -> 0 us
  other arithmetic: 66.6 us -> 83.2 us
    pallas_call x2 -> x1, Pallas kernels: 31.3 us -> 408 us  [forward(): pl.pallas_call(functools.partial(forward_kernel, dims), out_shape=[jax.Sh...]
    ppermute x80 -> x56, waiting for transfers between devices: 243 us -> 77.7 us  [send_up(): return lax.ppermute(value, 'ctx', up)]
    ppermute x80 -> x56, waiting for transfers between devices: 262 us -> 125 us  [send_down(): return lax.ppermute(value, 'ctx', down)]
    ppermute x17 -> x9, waiting for transfers between devices: 81.6 us -> 25.7 us  [swap_head(): return lax.ppermute(value, 'head', [(0, 1), (1, 0)])]
    ppermute x80 -> x56, starting transfers between devices: 100 us -> 50.8 us  [send_down(): return lax.ppermute(value, 'ctx', down)]
    unnamed x294 -> x217, local copies, waits for them, and re-layouts: 42.1 us -> 8 us
    all_gather x1 -> x0, blocking collectives: 30.7 us -> none  [local(): lax.all_gather(jnp.concatenate([attn_gain, mlp_gain], axis=0), 'ctx', axi...]
    dot_general x19 -> x6, matrix products: 51.2 us -> 22.7 us  [dot(): return jnp.dot(left, right, preferred_element_type=F32)]
  transfers between devices with their start and end apart: 204 -> 142, of which waited for: 110 -> 78; matrix products, arithmetic and copies ran while one was open for 23% -> 20% of each run, Pallas kernels for 5% -> 40%
where the time goes in v2:
time: 1100 us; the launch traced here: 1090 us
  Pallas kernels  441 us (40%)
  waiting for transfers between devices  279 us (25%)
  starting transfers between devices  124 us (11%)
  matrix products  88.5 us (8%)
  other arithmetic  83.2 us (8%)
  local copies, waits for them, and re-layouts  62.1 us (6%)
  between operations  16.7 us (2%)
    pallas_call x1, Pallas kernels, forward(): pl.pallas_call(functools.partial(forward_kernel, dims), out_shape=[jax.Sh...  408 us
    ppermute x56, waiting for transfers between devices, send_down(): return lax.ppermute(value, 'ctx', down)  125 us
    ppermute x56, waiting for transfers between devices, send_up(): return lax.ppermute(value, 'ctx', up)  77.7 us
    ppermute x56, starting transfers between devices, send_up(): return lax.ppermute(value, 'ctx', up)  63.8 us
    ppermute x56, starting transfers between devices, send_down(): return lax.ppermute(value, 'ctx', down)  50.8 us
    unnamed x2, waiting for transfers between devices  50.1 us
    convert_element_type x60, other arithmetic, ring_scatter(): low, high = (low.astype(BF16), high.astype(BF16))  37.7 us
    dot_general x8, matrix products, dot_tn(): lax.dot_general(left, right, (((0,), (0,)), ((), ())), preferred_element_...  34 us
  transfers between devices with their start and end apart: 142, of which 78 were waited for; matrix products, arithmetic and copies ran while one was open for 20% of the time, Pallas kernels for 40%

profile of v2, /device:TPU:0, one launch (start us, length us, event | category | flops | bytes accessed | tf_op | source)
XLA Modules:
  0.0 1094.4 jit_solution(13654638997054218359)
XLA Ops:
  28.5 407.9 %shard_map.221 = (bf16[16,96,2432]{2,1,0:T(8,128)(2,1)}, bf16[16,96,6144]{2,1,0:T(8,128)(2,1)}, bf16[16,96,2304]{2,1,0:T(8,128)(2,1)}, bf16[16,96,6144]{2,1,0:T(...) custom-call(f32[128,1536]{1,0:T(8,128)} %get-tuple-element.235.refs_, ...), custom_call_target="tpu_custom_call" | custom-call | tf_op jit(solution)/shard_map/pallas_call | solution.py:599
  449.3 10.4 slice_bitcast_fusion
  470.1 5.5 fusion.47
  475.6 7.2 fusion.2
  486.3 7.8 collective-permute-done.1
  531.5 16.5 %shard_map.222 = (f32[2,4,256,96]{3,2,1,0:T(8,128)}, bf16[16,384,256]{2,1,0:T(8,128)(2,1)}, bf16[16,384,256]{2,1,0:T(8,128)(2,1)}) custom-call(bf16[2,4,256,96]{3,2,1,0:T(8,128)(2,1)} %bitcast.353, bf16[2,4,256,96]{3,2,1,0:T(8,128)(2,1)} %bitcast.354, f32[2,4,256,1]{3,2,1,0:T(8,128)} %bitcast.345, bf16[16,768,256]{2,1,0:T(8,128)(2,1)} %get-tuple-element.111.k_ref.v_ref, ...), custom_call_target="tpu_custom_call" | custom-call | flops 8053063680 | bytes 16777216 | tf_op jit(solution)/shard_map/pallas_call | solution.py:191
  553.9 5.4 collective-permute-done.132
  571.8 8.6 fusion.340
  587.3 6.7 collective-permute-done.102
  602.4 8.1 collective-permute-done.13
  612.0 4.8 collective-permute-done.5
  628.5 6.6 collective-permute-done.15
  636.4 4.4 collective-permute-done.7
  652.6 5.4 collective-permute-done.17
  659.8 4.7 collective-permute-done.9
  667.8 5.4 collective-permute-done.10
  699.3 7.2 collective-permute-done.20
  706.5 6.8 fusion.55
  713.3 7.1 fusion
  727.5 7.6 collective-permute-done.108
  739.3 5.8 collective-permute-done.21
  777.7 16.3 %shard_map.223 = (f32[2,4,256,96]{3,2,1,0:T(8,128)}, bf16[16,384,256]{2,1,0:T(8,128)(2,1)}, bf16[16,384,256]{2,1,0:T(8,128)(2,1)}) custom-call(bf16[2,4,256,96]{3,2,1,0:T(8,128)(2,1)} %bitcast.352, bf16[2,4,256,96]{3,2,1,0:T(8,128)(2,1)} %bitcast.355, f32[2,4,256,1]{3,2,1,0:T(8,128)} %bitcast.344, bf16[16,768,256]{2,1,0:T(8,128)(2,1)} %get-tuple-element.110.k_ref.v_ref, ...), custom_call_target="tpu_custom_call" | custom-call | flops 8053063680 | bytes 16777216 | tf_op jit(solution)/shard_map/pallas_call | solution.py:191
  829.3 5.4 collective-permute-done.75
  866.5 8.6 fusion.341
  882.3 6.5 collective-permute-done.95
  896.2 9.0 collective-permute-done.33
  917.5 7.5 collective-permute-done.35
  937.9 6.1 collective-permute-done.37
  965.5 5.1 fusion.36
  978.5 50.1 %reduce-scatter.4.cloned.1.call-done = f32[96,4]{1,0:T(8,128)} async-done(((f32[1536,4]{1,0:T(8,128)}), f32[96,4]{1,0:T(8,128)}) %reduce-scatter.4.cloned.1.call-update) | async-done | bytes 1552
  1034.4 6.3 fusion.5
  1071.9 4.5 collective-permute-done.66
  (712 shorter events, 402.4 us)
Async XLA Ops:
  7.2 1021.4 %reduce-scatter.4.cloned.1.call-start = ((), (), s32[]{:S(2)}) async-start(), calls=%async_computation.1 | async-start | bytes 835584
  12.2 456.9 %collective-permute-start = (bf16[128,1536]{1,0:T(8,128)(2,1)}, bf16[128,1536]{1,0:T(8,128)(2,1)}, u32[]{:S(2)}, u32[]{:S(2)}) collective-permute-start(bf16[128,1536]{1,0:T(8,128)(2,1)} %get-tuple-element.232), channel_id=1, source_target_pairs={{0,1},{1,0},{2,3},{3,2},{4,5},{5,4},{6,7},{7,6},{8,9},{9,8},{10,11... | collective-permute-start | bytes 1179656 | tf_op jit(solution)/shard_map/ppermute | solution.py:649
  438.5 126.8 %collective-permute-start.69 = (bf16[256,768]{1,0:T(8,128)(2,1)}, bf16[256,768]{1,0:T(8,128)(2,1)}, u32[]{:S(2)}, u32[]{:S(2)}) collective-permute-start(bf16[256,768]{1,0:T(8,128)(2,1)} %get-tuple-element.205), channel_id=1, source_target_pairs={{0,2},{2,0},{4,6},{6,4},{8,10},{10,8},{12,14},{14,12},{16,18},{18,... | collective-permute-start | bytes 1179656 | tf_op jit(solution)/shard_map/ppermute | solution.py:646
  441.3 53.1 %collective-permute-start.126 = (bf16[256,2048]{1,0:T(8,128)(2,1)S(1)}, bf16[256,2048]{1,0:T(8,128)(2,1)}, u32[]{:S(2)}, u32[]{:S(2)}) collective-permute-start(bf16[256,2048]{1,0:T(8,128)(2,1)S(1)} %get-tuple-element.185), channel_id=1, source_target_pairs={{0,2},{2,0},{4,6},{6,4},{8,10},{10,8},{12,14},{14,12},{16,18},{18,... | collective-permute-start | bytes 3145736 | tf_op jit(solution)/shard_map/ppermute | solution.py:646
  485.9 85.6 %collective-permute-start.87 = (bf16[256,4096]{1,0:T(8,128)(2,1)}, bf16[256,4096]{1,0:T(8,128)(2,1)}, u32[]{:S(2)}, u32[]{:S(2)}) collective-permute-start(bf16[256,4096]{1,0:T(8,128)(2,1)} %pad_maximum_fusion), channel_id=1, source_target_pairs={{0,2},{2,0},{4,6},{6,4},{8,10},{10,8},{12,14},{14,12},{16,18},{18,... | collective-permute-start | bytes 6291464 | tf_op jit(solution)/shard_map/ppermute | solution.py:646
  529.2 21.1 %collective-permute-start.131 = (bf16[96,1024]{1,0:T(8,128)(2,1)}, bf16[96,1024]{1,0:T(8,128)(2,1)S(1)}, u32[]{:S(2)}, u32[]{:S(2)}) collective-permute-start(bf16[96,1024]{1,0:T(8,128)(2,1)} %get-tuple-element.132), channel_id=1, source_target_pairs={{0,8},{2,10},{8,16},{10,18},{16,24},{18,26},{24,28},{26,30},{28,20... | collective-permute-start | bytes 589832 | tf_op jit(solution)/shard_map/ppermute | solution.py:640
  565.3 129.5 %collective-permute-start.50 = (bf16[256,768]{1,0:T(8,128)(2,1)}, bf16[256,768]{1,0:T(8,128)(2,1)}, u32[]{:S(2)}, u32[]{:S(2)}) collective-permute-start(bf16[256,768]{1,0:T(8,128)(2,1)} %get-tuple-element.213), channel_id=1, source_target_pairs={{0,2},{2,0},{4,6},{6,4},{8,10},{10,8},{12,14},{14,12},{16,18},{18,... | collective-permute-start | bytes 1179656 | tf_op jit(solution)/shard_map/ppermute | solution.py:646
  571.0 251.9 %collective-permute-start.60 = (bf16[256,768]{1,0:T(8,128)(2,1)}, bf16[256,768]{1,0:T(8,128)(2,1)}, u32[]{:S(2)}, u32[]{:S(2)}) collective-permute-start(bf16[256,768]{1,0:T(8,128)(2,1)} %get-tuple-element.204), channel_id=1, source_target_pairs={{0,2},{2,0},{4,6},{6,4},{8,10},{10,8},{12,14},{14,12},{16,18},{18,... | collective-permute-start | bytes 1179656 | tf_op jit(solution)/shard_map/ppermute | solution.py:646
  594.7 23.5 %collective-permute-start.103 = (bf16[96,2048]{1,0:T(8,128)(2,1)S(1)}, bf16[96,2048]{1,0:T(8,128)(2,1)S(1)}, u32[]{:S(2)}, u32[]{:S(2)}) collective-permute-start(bf16[96,2048]{1,0:T(8,128)(2,1)S(1)} %get-tuple-element.108), channel_id=1, source_target_pairs={{0,4},{2,6},{8,0},{10,2},{16,8},{18,10},{24,16},{26,18},{28,24},{3... | collective-permute-start | bytes 1179656 | tf_op jit(solution)/shard_map/ppermute | solution.py:643
  598.3 21.6 %collective-permute-start.89 = (bf16[96,2048]{1,0:T(8,128)(2,1)S(1)}, bf16[96,2048]{1,0:T(8,128)(2,1)S(1)}, u32[]{:S(2)}, u32[]{:S(2)}) collective-permute-start(bf16[96,2048]{1,0:T(8,128)(2,1)S(1)} %get-tuple-element.109), channel_id=1, source_target_pairs={{0,8},{2,10},{8,16},{10,18},{16,24},{18,26},{24,28},{26,30},{28,20... | collective-permute-start | bytes 1179656 | tf_op jit(solution)/shard_map/ppermute | solution.py:640
  620.0 22.2 %collective-permute-start.104 = (bf16[96,2048]{1,0:T(8,128)(2,1)S(1)}, bf16[96,2048]{1,0:T(8,128)(2,1)S(1)}, u32[]{:S(2)}, u32[]{:S(2)}) collective-permute-start(bf16[96,2048]{1,0:T(8,128)(2,1)S(1)} %get-tuple-element.106), channel_id=1, source_target_pairs={{0,4},{2,6},{8,0},{10,2},{16,8},{18,10},{24,16},{26,18},{28,24},{3... | collective-permute-start | bytes 1179656 | tf_op jit(solution)/shard_map/ppermute | solution.py:643
  624.2 19.6 %collective-permute-start.90 = (bf16[96,2048]{1,0:T(8,128)(2,1)S(1)}, bf16[96,2048]{1,0:T(8,128)(2,1)S(1)}, u32[]{:S(2)}, u32[]{:S(2)}) collective-permute-start(bf16[96,2048]{1,0:T(8,128)(2,1)S(1)} %get-tuple-element.107), channel_id=1, source_target_pairs={{0,8},{2,10},{8,16},{10,18},{16,24},{18,26},{24,28},{26,30},{28,20... | collective-permute-start | bytes 1179656 | tf_op jit(solution)/shard_map/ppermute | solution.py:640
  644.0 21.5 %collective-permute-start.105 = (bf16[96,2048]{1,0:T(8,128)(2,1)S(1)}, bf16[96,2048]{1,0:T(8,128)(2,1)S(1)}, u32[]{:S(2)}, u32[]{:S(2)}) collective-permute-start(bf16[96,2048]{1,0:T(8,128)(2,1)S(1)} %get-tuple-element.104), channel_id=1, source_target_pairs={{0,4},{2,6},{8,0},{10,2},{16,8},{18,10},{24,16},{26,18},{28,24},{3... | collective-permute-start | bytes 1179656 | tf_op jit(solution)/shard_map/ppermute | solution.py:643
  648.5 19.1 %collective-permute-start.91 = (bf16[96,2048]{1,0:T(8,128)(2,1)S(1)}, bf16[96,2048]{1,0:T(8,128)(2,1)S(1)}, u32[]{:S(2)}, u32[]{:S(2)}) collective-permute-start(bf16[96,2048]{1,0:T(8,128)(2,1)S(1)} %get-tuple-element.105), channel_id=1, source_target_pairs={{0,8},{2,10},{8,16},{10,18},{16,24},{18,26},{24,28},{26,30},{28,20... | collective-permute-start | bytes 1179656 | tf_op jit(solution)/shard_map/ppermute | solution.py:640
  692.2 278.4 %collective-permute-start.41 = (bf16[256,768]{1,0:T(8,128)(2,1)}, bf16[256,768]{1,0:T(8,128)(2,1)}, u32[]{:S(2)}, u32[]{:S(2)}) collective-permute-start(bf16[256,768]{1,0:T(8,128)(2,1)} %get-tuple-element.211), channel_id=1, source_target_pairs={{0,2},{2,0},{4,6},{6,4},{8,10},{10,8},{12,14},{14,12},{16,18},{18,... | collective-permute-start | bytes 1179656 | tf_op jit(solution)/shard_map/ppermute | solution.py:646
  694.7 53.9 %collective-permute-start.110 = (bf16[256,2048]{1,0:T(8,128)(2,1)S(1)}, bf16[256,2048]{1,0:T(8,128)(2,1)}, u32[]{:S(2)}, u32[]{:S(2)}) collective-permute-start(bf16[256,2048]{1,0:T(8,128)(2,1)S(1)} %copy-done.12), channel_id=1, source_target_pairs={{0,2},{2,0},{4,6},{6,4},{8,10},{10,8},{12,14},{14,12},{16,18},{18,... | collective-permute-start | bytes 3145736 | tf_op jit(solution)/shard_map/ppermute | solution.py:646
  698.3 25.9 %collective-permute-start.70 = (bf16[96,1152]{1,0:T(8,128)(2,1)}, bf16[96,1152]{1,0:T(8,128)(2,1)}, u32[]{:S(2)}, u32[]{:S(2)}) collective-permute-start(bf16[96,1152]{1,0:T(8,128)(2,1)} %get-tuple-element.174), channel_id=1, source_target_pairs={{0,4},{2,6},{8,0},{10,2},{16,8},{18,10},{24,16},{26,18},{28,24},{3... | collective-permute-start | bytes 663560 | tf_op jit(solution)/shard_map/ppermute | solution.py:643
  706.5 19.7 %collective-permute-start.52 = (bf16[96,1152]{1,0:T(8,128)(2,1)}, bf16[96,1152]{1,0:T(8,128)(2,1)}, u32[]{:S(2)}, u32[]{:S(2)}) collective-permute-start(bf16[96,1152]{1,0:T(8,128)(2,1)} %get-tuple-element.175), channel_id=1, source_target_pairs={{0,8},{2,10},{8,16},{10,18},{16,24},{18,26},{24,28},{26,30},{28,20... | collective-permute-start | bytes 663560 | tf_op jit(solution)/shard_map/ppermute | solution.py:640
  749.5 23.5 %collective-permute-start.22 = (bf16[128,1536]{1,0:T(8,128)(2,1)S(1)}, bf16[128,1536]{1,0:T(8,128)(2,1)S(1)}, u32[]{:S(2)}, u32[]{:S(2)}) collective-permute-start(bf16[128,1536]{1,0:T(8,128)(2,1)S(1)} %get-tuple-element.68), channel_id=1, source_target_pairs={{0,1},{1,0},{2,3},{3,2},{4,5},{5,4},{6,7},{7,6},{8,9},{9,8},{10,11... | collective-permute-start | bytes 1179656 | tf_op jit(solution)/shard_map/ppermute | solution.py:649
  766.4 37.0 %collective-permute-start.112 = (bf16[96,1024]{1,0:T(8,128)(2,1)}, bf16[96,1024]{1,0:T(8,128)(2,1)}, u32[]{:S(2)}, u32[]{:S(2)}) collective-permute-start(bf16[96,1024]{1,0:T(8,128)(2,1)} %get-tuple-element.124), channel_id=1, source_target_pairs={{0,8},{2,10},{8,16},{10,18},{16,24},{18,26},{24,28},{26,30},{28,20... | collective-permute-start | bytes 589832 | tf_op jit(solution)/shard_map/ppermute | solution.py:640
  771.1 33.5 %collective-permute-start.119 = (bf16[96,1024]{1,0:T(8,128)(2,1)}, bf16[96,1024]{1,0:T(8,128)(2,1)}, u32[]{:S(2)}, u32[]{:S(2)}) collective-permute-start(bf16[96,1024]{1,0:T(8,128)(2,1)} %get-tuple-element.125), channel_id=1, source_target_pairs={{0,4},{2,6},{8,0},{10,2},{16,8},{18,10},{24,16},{26,18},{28,24},{3... | collective-permute-start | bytes 589832 | tf_op jit(solution)/shard_map/ppermute | solution.py:643
  773.0 32.9 %collective-permute-start.73 = (bf16[96,1152]{1,0:T(8,128)(2,1)}, bf16[96,1152]{1,0:T(8,128)(2,1)}, u32[]{:S(2)}, u32[]{:S(2)}) collective-permute-start(bf16[96,1152]{1,0:T(8,128)(2,1)} %get-tuple-element.168), channel_id=1, source_target_pairs={{0,4},{2,6},{8,0},{10,2},{16,8},{18,10},{24,16},{26,18},{28,24},{3... | collective-permute-start | bytes 663560 | tf_op jit(solution)/shard_map/ppermute | solution.py:643
  823.0 41.4 %collective-permute-start.77 = (bf16[256,768]{1,0:T(8,128)(2,1)S(1)}, bf16[256,768]{1,0:T(8,128)(2,1)S(1)}, u32[]{:S(2)}, u32[]{:S(2)}) collective-permute-start(bf16[256,768]{1,0:T(8,128)(2,1)S(1)} %copy-done.60), channel_id=1, source_target_pairs={{0,2},{2,0},{4,6},{6,4},{8,10},{10,8},{12,14},{14,12},{16,18},{18,... | collective-permute-start | bytes 1179656 | tf_op jit(solution)/shard_map/ppermute | solution.py:646
  823.5 40.9 %collective-permute-start.78 = (bf16[256,4096]{1,0:T(8,128)(2,1)S(1)}, bf16[256,4096]{1,0:T(8,128)(2,1)S(1)}, u32[]{:S(2)}, u32[]{:S(2)}) collective-permute-start(bf16[256,4096]{1,0:T(8,128)(2,1)S(1)} %copy-done.27), channel_id=1, source_target_pairs={{0,2},{2,0},{4,6},{6,4},{8,10},{10,8},{12,14},{14,12},{16,18},{18,... | collective-permute-start | bytes 6291464 | tf_op jit(solution)/shard_map/ppermute | solution.py:646
  908.9 20.2 %collective-permute-start.97 = (bf16[96,2048]{1,0:T(8,128)(2,1)S(1)}, bf16[96,2048]{1,0:T(8,128)(2,1)S(1)}, u32[]{:S(2)}, u32[]{:S(2)}) collective-permute-start(bf16[96,2048]{1,0:T(8,128)(2,1)S(1)} %get-tuple-element.92), channel_id=1, source_target_pairs={{0,4},{2,6},{8,0},{10,2},{16,8},{18,10},{24,16},{26,18},{28,24},{3... | collective-permute-start | bytes 1179656 | tf_op jit(solution)/shard_map/ppermute | solution.py:643
  909.5 19.5 %collective-permute-start.81 = (bf16[96,2048]{1,0:T(8,128)(2,1)S(1)}, bf16[96,2048]{1,0:T(8,128)(2,1)S(1)}, u32[]{:S(2)}, u32[]{:S(2)}) collective-permute-start(bf16[96,2048]{1,0:T(8,128)(2,1)S(1)} %get-tuple-element.93), channel_id=1, source_target_pairs={{0,8},{2,10},{8,16},{10,18},{16,24},{18,26},{24,28},{26,30},{28,20... | collective-permute-start | bytes 1179656 | tf_op jit(solution)/shard_map/ppermute | solution.py:640
  929.3 19.3 %collective-permute-start.98 = (bf16[96,2048]{1,0:T(8,128)(2,1)S(1)}, bf16[96,2048]{1,0:T(8,128)(2,1)S(1)}, u32[]{:S(2)}, u32[]{:S(2)}) collective-permute-start(bf16[96,2048]{1,0:T(8,128)(2,1)S(1)} %get-tuple-element.90), channel_id=1, source_target_pairs={{0,4},{2,6},{8,0},{10,2},{16,8},{18,10},{24,16},{26,18},{28,24},{3... | collective-permute-start | bytes 1179656 | tf_op jit(solution)/shard_map/ppermute | solution.py:643
  929.3 19.3 %collective-permute-start.82 = (bf16[96,2048]{1,0:T(8,128)(2,1)S(1)}, bf16[96,2048]{1,0:T(8,128)(2,1)S(1)}, u32[]{:S(2)}, u32[]{:S(2)}) collective-permute-start(bf16[96,2048]{1,0:T(8,128)(2,1)S(1)} %get-tuple-element.91), channel_id=1, source_target_pairs={{0,8},{2,10},{8,16},{10,18},{16,24},{18,26},{24,28},{26,30},{28,20... | collective-permute-start | bytes 1179656 | tf_op jit(solution)/shard_map/ppermute | solution.py:640
  960.9 90.2 %collective-permute-start.100 = (bf16[96,2048]{1,0:T(8,128)(2,1)}, bf16[96,2048]{1,0:T(8,128)(2,1)}, u32[]{:S(2)}, u32[]{:S(2)}) collective-permute-start(bf16[96,2048]{1,0:T(8,128)(2,1)} %get-tuple-element.86), channel_id=1, source_target_pairs={{0,4},{2,6},{8,0},{10,2},{16,8},{18,10},{24,16},{26,18},{28,24},{3... | collective-permute-start | bytes 1179656 | tf_op jit(solution)/shard_map/ppermute | solution.py:643
  962.7 88.4 %collective-permute-start.84 = (bf16[96,2048]{1,0:T(8,128)(2,1)}, bf16[96,2048]{1,0:T(8,128)(2,1)}, u32[]{:S(2)}, u32[]{:S(2)}) collective-permute-start(bf16[96,2048]{1,0:T(8,128)(2,1)} %get-tuple-element.87), channel_id=1, source_target_pairs={{0,8},{2,10},{8,16},{10,18},{16,24},{18,26},{24,28},{26,30},{28,20... | collective-permute-start | bytes 1179656 | tf_op jit(solution)/shard_map/ppermute | solution.py:640
  976.0 55.1 %collective-permute-start.61 = (bf16[96,1152]{1,0:T(8,128)(2,1)}, bf16[96,1152]{1,0:T(8,128)(2,1)}, u32[]{:S(2)}, u32[]{:S(2)}) collective-permute-start(bf16[96,1152]{1,0:T(8,128)(2,1)} %get-tuple-element.158), channel_id=1, source_target_pairs={{0,4},{2,6},{8,0},{10,2},{16,8},{18,10},{24,16},{26,18},{28,24},{3... | collective-permute-start | bytes 663560 | tf_op jit(solution)/shard_map/ppermute | solution.py:643
  977.9 53.1 %collective-permute-start.43 = (bf16[96,1152]{1,0:T(8,128)(2,1)}, bf16[96,1152]{1,0:T(8,128)(2,1)}, u32[]{:S(2)}, u32[]{:S(2)}) collective-permute-start(bf16[96,1152]{1,0:T(8,128)(2,1)} %get-tuple-element.159), channel_id=1, source_target_pairs={{0,8},{2,10},{8,16},{10,18},{16,24},{18,26},{24,28},{26,30},{28,20... | collective-permute-start | bytes 663560 | tf_op jit(solution)/shard_map/ppermute | solution.py:640
  (216 other events, 2649.9 us)
Sparse Core Ops, SparseCore 0:
  970.7 57.7 reduce-scatter.3

commit v3 on v2

--- a/solution.py
+++ b/solution.py
@@ -259,9 +259,15 @@
     def to_head(self, src, dst):
         return self.copy(src, dst, (self.ctx, 1 - self.head))
 
+    def sent(self, copy):
+        if any(other is copy for other in self.started):
+            copy.wait_send()
+            self.started = [other for other in self.started if other is not copy]
+
     def finish(self):
         for copy in self.started:
             copy.wait_send()
+        self.started = []
 
 
 class RingGather:
@@ -622,6 +628,517 @@
     return out[: len(shards)], out[len(shards) :]
 
 
+class RingScatter:
+    def __init__(self, links, windows, landing, stage, sems, finish):
+        self.links, self.windows, self.landing = links, windows, landing
+        self.stage, self.sems, self.finish = stage, sems, finish
+        self.last = links.chips - 1
+        self.step = 0
+        self.moving = []
+
+    def issue(self):
+        self.step += 1
+        chips = self.links.chips
+        slots = ((chips - self.step) % chips, self.step % chips)
+        sends = (self.links.to_right, self.links.to_left)
+        self.moving = [
+            sends[d](self.windows[d](slots[d]), self.landing.at[d, self.step - 1])
+            for d in range(2)
+        ]
+
+    def land(self):
+        chips, wide = self.links.chips, self.landing.shape[-1]
+        loads = []
+        for d in range(2):
+            self.moving[d].wait_recv()
+            self.links.sent(self.moving[d])
+            load = pltpu.make_async_copy(
+                self.landing.at[d, self.step - 1],
+                self.stage.at[d, :, pl.ds(0, wide)],
+                self.sems.at[d],
+            )
+            load.start()
+            loads.append(load)
+        slots = ((chips - 1 - self.step) % chips, (1 + self.step) % chips)
+        for d in range(2):
+            loads[d].wait()
+            window = self.windows[d](slots[d])
+            total = window[...].astype(F32) + self.stage[d, :, 0:wide].astype(F32)
+            if self.step < self.last:
+                window[...] = total.astype(BF16)
+            else:
+                self.finish(d, total)
+        if self.step < self.last:
+            self.issue()
+
+
+class Rounds:
+    def __init__(self):
+        self.active = []
+
+    def start(self, ring):
+        ring.issue()
+        ring.left = ring.last
+        self.active.append(ring)
+
+    def pump(self, count=1):
+        for _ in range(count):
+            if self.active:
+                ring = self.active.pop(0)
+                ring.land()
+                ring.left -= 1
+                if ring.left:
+                    self.active.append(ring)
+
+    def drain(self):
+        while self.active:
+            self.pump()
+
+
+def backward_kernel(dims, *refs):
+    layers, chips, width, q_width, kv_width, ff = dims
+    slots = 2 * chips
+    it = iter(refs)
+    g_ref = next(it)
+    weights = [next(it) for _ in range(2 * layers)]
+    (
+        kv_ref, normed_a_ref, qt_ref, lse_ref, att_ref, middle_ref, normed_m_ref,
+        gate_ref, up_ref, act_ref, x_in_ref, gain_ref,
+        cos_ref, sin_ref, kpos_ref, qpos_ref, qstart_ref,
+    ) = (next(it) for _ in range(17))
+    d_hidden_ref, d_gain_ref = next(it), next(it)
+    d_mlp_ref, d_attn_ref = next(it), next(it)
+    land_mlp, land_out, land_q, land_kv, land_dkv = (next(it) for _ in range(5))
+    (
+        wt, kv_buf, dkv_sib, dw_mlp, dw_attn, a_sib, at_buf, g_act, g_gu, g_qkv, g_att, acc,
+        g_low, g2_low, b_send, b_recv, qt_l, lse_l, da_t, dq_t, dkv_sum, gu_buf, rows_f32, n_own,
+        stage, out_stage, send_sems, recv_sems, load_sems, stage_sems,
+    ) = (next(it) for _ in range(30))
+
+    rows = g_ref.shape[0]
+    tokens = 2 * rows
+    db = width // slots
+    side = width // 2
+    heads_kv = kv_width // HEAD_SIZE
+    group = q_width // kv_width
+    qkv_width = q_width + 2 * kv_width
+    links = Links(chips, send_sems, recv_sems)
+    links.greet()
+    rounds = Rounds()
+    cosine, sine = cos_ref[...], sin_ref[...]
+    scale = HEAD_SIZE ** (-0.5)
+
+    def local(src, dst, sem):
+        copy = pltpu.make_async_copy(src, dst, load_sems.at[sem])
+        copy.start()
+        return copy
+
+    def load(i, column, wide, target, sem):
+        return local(weights[i].at[:, :, pl.ds(column, wide)], target, sem)
+
+    def flat(ref):
+        return ref[...].reshape(width, ref.shape[-1])
+
+    def out_by(target):
+        def finish(d, total):
+            wide = total.shape[-1]
+            out_stage[d, :, 0:wide] = total
+            copy = pltpu.make_async_copy(
+                out_stage.at[d, :, pl.ds(0, wide)], target(d), stage_sems.at[d]
+            )
+            copy.start()
+            copy.wait()
+
+        return finish
+
+    def scatter(ref, column, wide, landing, out):
+        half = wide // 2
+
+        def window(d):
+            return lambda slot: ref.at[slot, :, pl.ds(column + d * half, half)]
+
+        rounds.start(
+            RingScatter(
+                links,
+                (window(0), window(1)),
+                landing,
+                stage,
+                stage_sems,
+                out_by(lambda d: out.at[:, pl.ds(column + d * half, half)]),
+            )
+        )
+
+    def turn_columns(own, sib):
+        at_buf[:, 0:tokens] = own.astype(F32).T.astype(BF16)
+        at_buf[:, tokens : 2 * tokens] = sib.astype(F32).T.astype(BF16)
+
+    def weight_grad(target, column, right, wide):
+        for c in range(0, wide, TILE):
+            size = min(TILE, wide - c)
+            part = dot(at_buf[...], right[:, c : c + size])
+            target[:, :, column + c : column + c + size] = part.reshape(chips, db, size).astype(
+                BF16
+            )
+
+    def norm_back(grad, value, gain, row):
+        inverse = rms_inverse(value)
+        normalized = value * inverse
+        d_gain_ref[row : row + 1, :] = jnp.sum(grad * normalized, axis=0, keepdims=True)
+        scaled = grad * gain
+        mean = jnp.mean(scaled * normalized, axis=-1, keepdims=True)
+        d_hidden_ref[...] += inverse * (scaled - normalized * mean)
+
+
+    d_hidden_ref[...] = g_ref[...]
+    for layer in reversed(range(layers)):
+        attn, mlp = 2 * layer, 2 * layer + 1
+        gain_a = gain_ref[layer : layer + 1, :]
+        gain_m = gain_ref[layers + layer : layers + layer + 1, :]
+        links.finish()
+
+        def load_tile(t):
+            at = (t % 2) * 3
+            columns = pl.ds(t * TILE, TILE)
+            return [
+                load(mlp, part * ff + t * TILE, TILE, wt.at[at + part], at + part)
+                for part in range(3)
+            ] + [
+                local(gate_ref.at[layer, :, columns], gu_buf.at[t % 2, 0], 6 + t % 2 * 2),
+                local(up_ref.at[layer, :, columns], gu_buf.at[t % 2, 1], 7 + t % 2 * 2),
+            ]
+
+        pending = load_tile(0)
+        g_low[0:rows, :] = d_hidden_ref[...].astype(BF16)
+        swap = links.to_head(g_low.at[pl.ds(0, rows), :], g_low.at[pl.ds(rows, rows), :])
+        far = pl.ds(side, side)
+        other_rows = pl.ds(tokens, tokens)
+        from_sib = [
+            links.to_sibling(act_ref.at[layer], g_act.at[other_rows, :]),
+            links.to_sibling(normed_m_ref.at[layer, :, far], a_sib.at[1]),
+            links.to_sibling(normed_a_ref.at[layer, :, far], a_sib.at[3]),
+            links.to_sibling(att_ref.at[layer], g_att.at[other_rows, :]),
+        ]
+        here = [
+            local(act_ref.at[layer], g_act.at[pl.ds(0, tokens), :], 10),
+            local(normed_m_ref.at[layer, :, pl.ds(0, side)], n_own.at[0], 11),
+            local(normed_a_ref.at[layer, :, pl.ds(0, side)], n_own.at[1], 12),
+            local(att_ref.at[layer], g_att.at[pl.ds(0, tokens), :], 13),
+            local(middle_ref.at[layer], rows_f32.at[0], 14),
+            local(x_in_ref.at[layer], rows_f32.at[1], 15),
+            local(qt_ref.at[layer], qt_l, 16),
+            local(lse_ref.at[layer], lse_l, 17),
+        ]
+        rounds.pump()
+        swap.wait_recv()
+        from_sib_g = links.to_sibling(g_low.at[:, far], a_sib.at[0])
+        count = ff // TILE
+        from_sib_gu = []
+        for t in range(count):
+            following = load_tile(t + 1) if t + 1 < count else None
+            for copy in pending:
+                copy.wait()
+            at = (t % 2) * 3
+            gate = gu_buf[t % 2, 0].astype(F32)
+            up = gu_buf[t % 2, 1].astype(F32)
+            d_act = dot(g_low[...], flat(wt.at[at + 2]))
+            sig = jax.nn.sigmoid(gate)
+            d_gate = (d_act * up * sig * (1.0 + gate * (1.0 - sig))).astype(BF16)
+            d_up = (d_act * gate * sig).astype(BF16)
+            for part, grad in enumerate((d_gate, d_up)):
+                column = part * ff + t * TILE
+                g_gu[0:tokens, column : column + TILE] = grad
+                from_sib_gu.append(
+                    links.to_sibling(
+                        g_gu.at[pl.ds(0, tokens), pl.ds(column, TILE)],
+                        g_gu.at[other_rows, pl.ds(column, TILE)],
+                    )
+                )
+            back = dot_nt(d_gate, flat(wt.at[at])) + dot_nt(d_up, flat(wt.at[at + 1]))
+            if t == 0:
+                acc[...] = back
+            else:
+                acc[...] += back
+            pending = following
+            rounds.pump(3)
+        b_send[0] = acc[rows:tokens, :].astype(BF16)
+        swap = links.to_head(b_send.at[0], b_recv.at[0])
+        out_loads = [
+            load(attn, qkv_width, TILE, wt.at[4], 4),
+            load(attn, qkv_width + TILE, q_width - TILE, wt.at[5, :, :, pl.ds(0, q_width - TILE)], 5),
+        ]
+        rounds.drain()
+        for copy in here:
+            copy.wait()
+        from_sib_g.wait_recv()
+        for copy in from_sib:
+            copy.wait_recv()
+        turn_columns(g_low[:, 0:side], a_sib[0])
+        weight_grad(dw_mlp.at[0], 0, g_act, ff)
+        scatter(dw_mlp.at[0], 0, ff, land_mlp.at[layer, 0], d_mlp_ref.at[layer, 0])
+        swap.wait_recv()
+        norm_back(
+            acc[0:rows, :] + b_recv[0].astype(F32), rows_f32[0], gain_m, layers + layer
+        )
+        g2_low[0:rows, :] = d_hidden_ref[...].astype(BF16)
+        swap = links.to_head(g2_low.at[pl.ds(0, rows), :], g2_low.at[pl.ds(rows, rows), :])
+        for copy in from_sib_gu:
+            copy.wait_recv()
+        turn_columns(n_own[0], a_sib[1])
+        for part in range(2):
+            weight_grad(dw_mlp.at[1 + part], 0, g_gu.at[:, pl.ds(part * ff, ff)], ff)
+            scatter(
+                dw_mlp.at[1 + part], 0, ff, land_mlp.at[layer, 1 + part], d_mlp_ref.at[layer, 1 + part]
+            )
+
+        swap.wait_recv()
+        from_sib_g = links.to_sibling(g2_low.at[:, far], a_sib.at[2])
+        for i, copy in enumerate(out_loads):
+            copy.wait()
+            size = TILE if i == 0 else q_width - TILE
+            part = dot(g2_low[...], flat(wt.at[4 + i, :, :, pl.ds(0, size)]))
+            da_t[i * TILE : i * TILE + size, :] = part.T.astype(BF16)
+        rounds.pump()
+
+        units = SEQS * heads_kv
+        pairs = (heads_kv + 1) // 2
+
+        def unit_copies(u, at):
+            s, h = u // heads_kv, u % heads_kv
+            lanes = pl.ds(pl.multiple_of(s * ROWS, ROWS), ROWS)
+            return [
+                pltpu.make_async_copy(
+                    kv_ref.at[
+                        layer,
+                        :,
+                        pl.ds(pl.multiple_of(part * kv_width + h * HEAD_SIZE, HEAD_SIZE), HEAD_SIZE),
+                        lanes,
+                    ],
+                    kv_buf.at[at, part],
+                    load_sems.at[6 + 2 * at + part],
+                )
+                for part in range(2)
+            ]
+
+        def unit(u, carry):
+            at = u % 2
+            s, h = u // heads_kv, u % heads_kv
+            for copy in unit_copies(u, at):
+                copy.wait()
+            ahead = jnp.minimum(u + 1, units - 1)
+
+            @pl.when(u + 1 < units)
+            def _():
+                for copy in unit_copies(ahead, 1 - at):
+                    copy.start()
+
+            kt = jnp.concatenate([kv_buf[at, 0, j] for j in range(slots)], axis=1)
+            vt = jnp.concatenate([kv_buf[at, 1, j] for j in range(slots)], axis=1)
+            lanes = pl.ds(pl.multiple_of(s * ROWS, ROWS), ROWS)
+            allowed = (kpos_ref[s] <= qpos_ref[s]) & (kpos_ref[s] >= qstart_ref[s])
+            dkt = dvt = None
+            for g in range(group):
+                head_rows = pl.ds(
+                    pl.multiple_of((h * group + g) * HEAD_SIZE, HEAD_SIZE), HEAD_SIZE
+                )
+                qt = qt_l[head_rows, lanes]
+                dot_t = da_t[head_rows, lanes]
+                scores = masked(dot_tn(qt, kt), [allowed])
+                probs = jnp.exp(scores - lse_l[u, g * ROWS : (g + 1) * ROWS, :])
+                dprobs = dot_tn(dot_t, vt)
+                delta = jnp.sum(probs * dprobs, axis=1, keepdims=True)
+                dscores = (probs * (dprobs - delta)).astype(BF16)
+                dq_t[head_rows, lanes] = dot_nt(kt, dscores)
+                dk_part = dot(qt, dscores)
+                dv_part = dot(dot_t, probs.astype(BF16))
+                dkt = dk_part if dkt is None else dkt + dk_part
+                dvt = dv_part if dvt is None else dvt + dv_part
+            spot = pl.ds(pl.multiple_of((h % 2) * SEQS * ROWS + s * ROWS, ROWS), ROWS)
+            for j in range(slots):
+                wt[h // 2, j, :, spot] = dkt[:, j * ROWS : (j + 1) * ROWS].astype(BF16)
+                wt[pairs + h // 2, j, :, spot] = dvt[:, j * ROWS : (j + 1) * ROWS].astype(BF16)
+            return carry
+
+        for copy in unit_copies(0, 0):
+            copy.start()
+        for u in range(0, units, 2):
+            lax.fori_loop(u, u + 2, unit, 0)
+            rounds.pump(2)
+
+        sent = []
+        for i in range(2 * pairs):
+            sent.append(
+                links.to_sibling(wt.at[i, pl.ds(chips, chips)], dkv_sib.at[i])
+            )
+        from_sib_g.wait_recv()
+        turn_columns(g2_low[:, 0:side], a_sib[2])
+        weight_grad(dw_attn, qkv_width, g_att, q_width)
+        scatter(dw_attn, qkv_width, q_width, land_out.at[layer], d_attn_ref.at[layer])
+        sums = Rounds()
+        for i in range(pairs):
+            for j in (i, pairs + i):
+                sent[j].wait_recv()
+                for slot in range(chips):
+                    wt[j, slot] = (wt[j, slot].astype(F32) + dkv_sib[j, slot].astype(F32)).astype(
+                        BF16
+                    )
+
+            def keep(i):
+                def finish(d, total):
+                    dkv_sum[d * pairs + i] = total
+
+                return finish
+
+            sums.start(
+                RingScatter(
+                    links,
+                    (
+                        lambda slot, i=i: wt.at[i, slot],
+                        lambda slot, i=i: wt.at[pairs + i, slot],
+                    ),
+                    land_dkv.at[layer, i],
+                    stage,
+                    stage_sems,
+                    keep(i),
+                )
+            )
+
+        def turned_back(low, high):
+            return low * cosine + high * sine, high * cosine - low * sine
+
+        for h in range(q_width // HEAD_SIZE):
+            at = h * HEAD_SIZE
+            low, high = turned_back(
+                dq_t[at : at + HALF, :], dq_t[at + HALF : at + HEAD_SIZE, :]
+            )
+            dq_t[at : at + HALF, :] = low * scale
+            dq_t[at + HALF : at + HEAD_SIZE, :] = high * scale
+        g_qkv[0:tokens, 0:q_width] = dq_t[...].T.astype(BF16)
+        mine = pl.ds(0, tokens)
+        from_sib_q = links.to_sibling(
+            g_qkv.at[mine, pl.ds(0, q_width)], g_qkv.at[other_rows, pl.ds(0, q_width)]
+        )
+        step = 0
+        while sums.active:
+            sums.pump()
+            step += 1
+            if step % 2 == 0:
+                rounds.pump()
+            if step == 4:
+                from_sib_q.wait_recv()
+                turn_columns(n_own[1], a_sib[3])
+                weight_grad(dw_attn, 0, g_qkv, q_width)
+                scatter(dw_attn, 0, q_width, land_q.at[layer], d_attn_ref.at[layer])
+        for h in range(heads_kv):
+            spot = slice((h % 2) * SEQS * ROWS, (h % 2 + 1) * SEQS * ROWS)
+            block = dkv_sum[h // 2, :, spot]
+            low, high = turned_back(block[0:HALF, :], block[HALF:HEAD_SIZE, :])
+            at = h * HEAD_SIZE
+            dq_t[at : at + HALF, :] = low
+            dq_t[at + HALF : at + HEAD_SIZE, :] = high
+            dq_t[kv_width + at : kv_width + at + HEAD_SIZE, :] = dkv_sum[pairs + h // 2, :, spot]
+        g_qkv[0:tokens, q_width:qkv_width] = dq_t[0 : 2 * kv_width, :].T.astype(BF16)
+        from_sib_kv = links.to_sibling(
+            g_qkv.at[mine, pl.ds(q_width, 2 * kv_width)],
+            g_qkv.at[other_rows, pl.ds(q_width, 2 * kv_width)],
+        )
+        links.finish()
+        tiles = [
+            load(attn, t * TILE, TILE, wt.at[t], t) for t in range(qkv_width // TILE)
+        ]
+        for t, tile in enumerate(tiles):
+            tile.wait()
+            back = dot_nt(g_qkv[0:tokens, t * TILE : (t + 1) * TILE], flat(wt.at[t]))
+            if t == 0:
+                acc[...] = back
+            else:
+                acc[...] += back
+        b_send[1] = acc[rows:tokens, :].astype(BF16)
+        swap = links.to_head(b_send.at[1], b_recv.at[1])
+        from_sib_kv.wait_recv()
+        weight_grad(dw_attn, q_width, g_qkv.at[:, pl.ds(q_width, 2 * kv_width)], 2 * kv_width)
+        scatter(dw_attn, q_width, 2 * kv_width, land_kv.at[layer], d_attn_ref.at[layer])
+        rounds.pump()
+        swap.wait_recv()
+        norm_back(acc[0:rows, :] + b_recv[1].astype(F32), rows_f32[1], gain_a, layer)
+    rounds.drain()
+    links.finish()
+
+
+def backward(grad, weights, saved, tables, chips, q_width, kv_width, ff):
+    layers = len(weights) // 2
+    rows, width = grad.shape
+    slots = 2 * chips
+    db = width // slots
+    tokens = 2 * rows
+    heads_kv = kv_width // HEAD_SIZE
+    units = SEQS * heads_kv
+    pairs = (heads_kv + 1) // 2
+    group = q_width // kv_width
+    steps = chips - 1
+    qkv_width = q_width + 2 * kv_width
+    dims = (layers, chips, width, q_width, kv_width, ff)
+    rings = 3 + 3 + pairs
+    copies = layers * (rings * 2 * steps + 4 + 4 + 1 + 2 * (ff // TILE) + 1 + 2 * pairs + 2)
+    any_spec = pl.BlockSpec(memory_space=pl.ANY)
+    vmem = pl.BlockSpec(memory_space=pltpu.VMEM)
+
+    def landing(*shape):
+        return jax.ShapeDtypeStruct(shape, BF16)
+
+    out = pl.pallas_call(
+        functools.partial(backward_kernel, dims),
+        out_shape=[
+            jax.ShapeDtypeStruct((rows, width), F32),
+            jax.ShapeDtypeStruct((2 * layers, width), F32),
+            jax.ShapeDtypeStruct((layers, 3, db, ff), F32),
+            jax.ShapeDtypeStruct((layers, db, qkv_width + q_width), F32),
+            landing(layers, 3, 2, steps, db, ff // 2),
+            landing(layers, 2, steps, db, q_width // 2),
+            landing(layers, 2, steps, db, q_width // 2),
+            landing(layers, 2, steps, db, kv_width),
+            landing(layers, pairs, 2, steps, HEAD_SIZE, 2 * SEQS * ROWS),
+        ],
+        in_specs=[vmem] + [any_spec] * (len(weights) + 11) + [vmem] * 6,
+        out_specs=[vmem] * 2 + [any_spec] * 7,
+        scratch_shapes=[
+            pltpu.VMEM((6, slots, db, TILE), BF16),
+            pltpu.VMEM((2, 2, slots, HEAD_SIZE, ROWS), BF16),
+            pltpu.VMEM((2 * pairs, chips, HEAD_SIZE, 2 * SEQS * ROWS), BF16),
+            pltpu.VMEM((3, chips, db, ff), BF16),
+            pltpu.VMEM((chips, db, qkv_width + q_width), BF16),
+            pltpu.VMEM((4, tokens, width // 2), BF16),
+            pltpu.VMEM((width // 2, 2 * tokens), BF16),
+            pltpu.VMEM((2 * tokens, ff), BF16),
+            pltpu.VMEM((2 * tokens, 2 * ff), BF16),
+            pltpu.VMEM((2 * tokens, qkv_width), BF16),
+            pltpu.VMEM((2 * tokens, q_width), BF16),
+            pltpu.VMEM((tokens, width), F32),
+            pltpu.VMEM((tokens, width), BF16),
+            pltpu.VMEM((tokens, width), BF16),
+            pltpu.VMEM((2, rows, width), BF16),
+            pltpu.VMEM((2, rows, width), BF16),
+            pltpu.VMEM((q_width, tokens), BF16),
+            pltpu.VMEM((units, group * ROWS, 1), F32),
+            pltpu.VMEM((q_width, tokens), BF16),
+            pltpu.VMEM((q_width, tokens), F32),
+            pltpu.VMEM((2 * pairs, HEAD_SIZE, 2 * SEQS * ROWS), F32),
+            pltpu.VMEM((2, 2, tokens, TILE), BF16),
+            pltpu.VMEM((2, rows, width), F32),
+            pltpu.VMEM((2, tokens, width // 2), BF16),
+            pltpu.VMEM((2, db, ff // 2), BF16),
+            pltpu.VMEM((2, db, ff // 2), F32),
+            pltpu.SemaphoreType.DMA((copies,)),
+            pltpu.SemaphoreType.DMA((copies,)),
+            pltpu.SemaphoreType.DMA((18,)),
+            pltpu.SemaphoreType.DMA((2,)),
+        ],
+        compiler_params=pltpu.CompilerParams(
+            collective_id=1, has_side_effects=True, vmem_limit_bytes=KERNEL_VMEM
+        ),
+    )(grad, *weights, *saved, *tables)
+    return out[:4]
+
+
 def build(n_ctx):
     chips = n_ctx // 2
     ring = ring_of(chips)
@@ -649,40 +1166,43 @@
         return lax.ppermute(value, "head", [(0, 1), (1, 0)])
 
     def ring_gather(shard):
-        got = {0: shard}
-        low, high = shard, shard
         half = chips // 2
-        for step in range(1, half):
-            low, high = send_up(low), send_down(high)
-            got[chips - step] = low
-            got[step] = high
+
+        def step(carry, unused):
+            carry = (send_up(carry[0]), send_down(carry[1]))
+            return carry, carry
+
+        (low, high), (lows, highs) = lax.scan(step, (shard, shard), None, length=half - 1)
         cut = shard.shape[0] // 2
-        got[half] = jnp.concatenate([send_up(low[:cut]), send_down(high[cut:])], axis=0)
-        return [got[j] for j in range(chips)]
-
-    def ring_scatter(slots):
-        low = slots[chips - 1][0].astype(BF16)
-        high = slots[1][1].astype(BF16)
-        for step in range(1, chips):
-            low, high = send_up(low), send_down(high)
-            own_low = slots[(chips - 1 - step) % chips][0].astype(F32)
-            own_high = slots[(1 + step) % chips][1].astype(F32)
-            low, high = low.astype(F32) + own_low, high.astype(F32) + own_high
-            if step < chips - 1:
-                low, high = low.astype(BF16), high.astype(BF16)
-        return low, high
+        across = jnp.concatenate([send_up(low[:cut]), send_down(high[cut:])], axis=0)
+        return jnp.concatenate([shard[None], highs, across[None], lows[::-1]], axis=0)
+
+    def ring_scatter(lows, highs):
+        def own(parts, slot):
+            return lax.dynamic_index_in_dim(parts, slot, 0, keepdims=False).astype(F32)
+
+        def step(carry, at):
+            low, high = (send_up(carry[0]), send_down(carry[1]))
+            low = low.astype(F32) + own(lows, (chips - 1 - at) % chips)
+            high = high.astype(F32) + own(highs, (1 + at) % chips)
+            return (low.astype(BF16), high.astype(BF16)), None
+
+        start = (lows[chips - 1].astype(BF16), highs[1].astype(BF16))
+        steps = jnp.arange(1, chips - 1, dtype=jnp.int32)
+        (low, high), unused = lax.scan(step, start, steps)
+        return (
+            send_up(low).astype(F32) + lows[0].astype(F32),
+            send_down(high).astype(F32) + highs[0].astype(F32),
+        )
 
     def gather(shard):
-        own = jnp.concatenate(ring_gather(shard), axis=0)
+        own = ring_gather(shard).reshape(chips * shard.shape[0], shard.shape[1])
         return jnp.concatenate([own, swap_core(own)], axis=0)
 
     def weight_scatter(grad):
         db, cut = grad.shape[0] // chips, grad.shape[1] // 2
-        slots = [
-            (grad[j * db : (j + 1) * db, :cut], grad[j * db : (j + 1) * db, cut:])
-            for j in range(chips)
-        ]
-        return jnp.concatenate(ring_scatter(slots), axis=1)
+        parts = grad.reshape(chips, db, grad.shape[1])
+        return jnp.concatenate(ring_scatter(parts[:, :, :cut], parts[:, :, cut:]), axis=1)
 
     def local(
         hidden_in,
@@ -824,7 +1344,7 @@
                     sine_table,
                 ).reshape(token_rows, kv_width)
                 kv_shard = jnp.concatenate([keys, projected[:, q_width + kv_width :]], axis=1)
-                kv_own = jnp.stack(ring_gather(kv_shard.astype(BF16).T), axis=0)
+                kv_own = ring_gather(kv_shard.astype(BF16).T)
                 kv = jnp.concatenate([kv_own, swap_core(kv_own)], axis=0)
                 mixed, lse = attend_forward(queries, kv, kpos, qpos, qstart)
                 attended = from_units(mixed)
@@ -877,31 +1397,12 @@
                 kv_width,
                 ff_width,
             )
-            weights = [weight.reshape(width, weight.shape[-1]) for weight in weights]
-            fetched = [(weights[2 * layer], weights[2 * layer + 1]) for layer in range(layers)]
-            kv, normed_a, qt, lse, att, middle, normed_m, gate, up, act, x_out, gains = saved
-            records = []
-            for layer in range(layers):
-                q_units = qt[layer].reshape(heads_kv, group, HEAD_SIZE, SEQS, ROWS)
-                q_units = q_units.transpose(3, 0, 1, 4, 2)
-                records.append(
-                    (
-                        residual if layer == 0 else x_out[layer - 1],
-                        normed_a[layer],
-                        q_units.reshape(SEQS, heads_kv, group * ROWS, HEAD_SIZE),
-                        kv[layer],
-                        lse[layer].reshape(SEQS, heads_kv, group * ROWS, 1),
-                        att[layer],
-                        middle[layer],
-                        normed_m[layer],
-                        gate[layer].astype(F32),
-                        up[layer].astype(F32),
-                        act[layer],
-                    )
-                )
-            return fetched, gains, records, x_out[layers - 1]
-
-        in_kernel = n_ctx * ROWS <= 2048
+            residual_ins = jnp.concatenate([residual[None], saved[10][: layers - 1]], axis=0)
+            tables = (cosine.T, sine_table.T, kpos, qpos, qstart)
+            records = [*saved[:10], residual_ins, saved[11]]
+            return weights, tables, records, saved[10][layers - 1]
+
+        in_kernel = n_ctx * ROWS <= 2048 and db == HEAD_SIZE
         run_forward = forward_by_kernel if in_kernel else forward_by_ops
         fetched, gains, records, residual = run_forward(reorder(hidden_in))
         out_hidden = lax.dot_general(
@@ -915,95 +1416,108 @@
             mean = jnp.mean(scaled * normalized, axis=-1, keepdims=True)
             return grad_res + inverse_norm * (scaled - normalized * mean), gain_gradient
 
-        d_attn = [None] * layers
-        d_mlp = [None] * layers
-        d_gains = [None] * (2 * layers)
-        for layer in reversed(range(layers)):
-            attn_w, mlp_w = fetched[layer]
-            gain_a, gain_m = gains[layer], gains[layers + layer]
-            (
-                residual_in,
-                normed_a,
-                queries,
-                kv,
-                lse,
-                attended,
-                middle,
-                normed_m,
-                gate_part,
-                up_part,
-                activated,
-            ) = records[layer]
-            inverse_a, inverse_m = rms_inverse(residual_in), rms_inverse(middle)
-            grad_rows_m = both_rows(grad_res.astype(BF16))
-            grad_act = project(grad_rows_m, mlp_w, 2 * ff_width, 3 * ff_width)
-            sigmoid_g = jax.nn.sigmoid(gate_part)
-            grad_gate = grad_act * up_part * sigmoid_g * (1.0 + gate_part * (1.0 - sigmoid_g))
-            grad_up = grad_act * gate_part * sigmoid_g
-            grad_gu = jnp.concatenate([grad_gate, grad_up], axis=1).astype(BF16)
-            grad_norm_m = to_owner(project_back(grad_gu, mlp_w, 0, 2 * ff_width))
-            d_down = weight_scatter(weight_grad(grad_rows_m, activated))
-            d_gu = weight_scatter(weight_grad(normed_m, grad_gu))
-            grad_res, d_gains[layers + layer] = norm_back(
-                grad_res, grad_norm_m, middle, inverse_m, gain_m
+        def backward_by_ops(grad_res):
+            d_attn = [None] * layers
+            d_mlp = [None] * layers
+            d_gains = [None] * (2 * layers)
+            for layer in reversed(range(layers)):
+                attn_w, mlp_w = fetched[layer]
+                gain_a, gain_m = gains[layer], gains[layers + layer]
+                (
+                    residual_in,
+                    normed_a,
+                    queries,
+                    kv,
+                    lse,
+                    attended,
+                    middle,
+                    normed_m,
+                    gate_part,
+                    up_part,
+                    activated,
+                ) = records[layer]
+                inverse_a, inverse_m = rms_inverse(residual_in), rms_inverse(middle)
+                grad_rows_m = both_rows(grad_res.astype(BF16))
+                grad_act = project(grad_rows_m, mlp_w, 2 * ff_width, 3 * ff_width)
+                sigmoid_g = jax.nn.sigmoid(gate_part)
+                grad_gate = grad_act * up_part * sigmoid_g * (1.0 + gate_part * (1.0 - sigmoid_g))
+                grad_up = grad_act * gate_part * sigmoid_g
+                grad_gu = jnp.concatenate([grad_gate, grad_up], axis=1).astype(BF16)
+                grad_norm_m = to_owner(project_back(grad_gu, mlp_w, 0, 2 * ff_width))
+                d_down = weight_scatter(weight_grad(grad_rows_m, activated))
+                d_gu = weight_scatter(weight_grad(normed_m, grad_gu))
+                grad_res, d_gains[layers + layer] = norm_back(
+                    grad_res, grad_norm_m, middle, inverse_m, gain_m
+                )
+                grad_rows_a = both_rows(grad_res.astype(BF16))
+                grad_attended = project(grad_rows_a, attn_w, qkv_width, attn_width).astype(BF16)
+                d_out = weight_grad(grad_rows_a, attended)
+                grad_q, dk, dv = attend_backward(
+                    queries, units(grad_attended), lse, kv, kpos, qpos, qstart
+                )
+                dk_back, dv_back = swap_core(dk[chips:]), swap_core(dv[chips:])
+                grad_k, grad_v = ring_scatter(
+                    dk[:chips].astype(F32) + dk_back.astype(F32),
+                    dv[:chips].astype(F32) + dv_back.astype(F32),
+                )
+                grad_q_pre = rotate_back(
+                    from_units(grad_q).reshape(token_rows, heads_q, HEAD_SIZE), cosine, sine_table
+                )
+                grad_k_pre = rotate_back(
+                    grad_k.T.reshape(token_rows, heads_kv, HEAD_SIZE), cosine, sine_table
+                )
+                grad_qkv = jnp.concatenate(
+                    [
+                        (grad_q_pre * scale_q).reshape(token_rows, q_width),
+                        grad_k_pre.reshape(token_rows, kv_width),
+                        grad_v.T,
+                    ],
+                    axis=1,
+                ).astype(BF16)
+                grad_norm_a = to_owner(project_back(grad_qkv, attn_w, 0, qkv_width))
+                d_qkv = weight_grad(normed_a, grad_qkv)
+                d_attn[layer] = weight_scatter(jnp.concatenate([d_qkv, d_out], axis=1))
+                d_mlp[layer] = (d_gu, d_down)
+                grad_res, d_gains[layer] = norm_back(
+                    grad_res, grad_norm_a, residual_in, inverse_a, gain_a
+                )
+            d_mlp = [
+                jnp.stack([down, gu[:, :ff_width], gu[:, ff_width:]], axis=0) for gu, down in d_mlp
+            ]
+            return (
+                grad_res,
+                jnp.stack(d_gains, axis=0),
+                jnp.stack(d_mlp, axis=0),
+                jnp.stack(d_attn, axis=0),
             )
-            grad_rows_a = both_rows(grad_res.astype(BF16))
-            grad_attended = project(grad_rows_a, attn_w, qkv_width, attn_width).astype(BF16)
-            d_out = weight_grad(grad_rows_a, attended)
-            grad_q, dk, dv = attend_backward(
-                queries, units(grad_attended), lse, kv, kpos, qpos, qstart
+
+        if in_kernel:
+            grad_res, d_gains, d_mlp, d_attn = backward(
+                grad_res, fetched, records, gains, chips, q_width, kv_width, ff_width
             )
-            dk_back, dv_back = swap_core(dk[chips:]), swap_core(dv[chips:])
-            kv_slots = [
-                (
-                    dk[j].astype(F32) + dk_back[j].astype(F32),
-                    dv[j].astype(F32) + dv_back[j].astype(F32),
-                )
-                for j in range(chips)
-            ]
-            grad_k, grad_v = ring_scatter(kv_slots)
-            grad_q_pre = rotate_back(
-                from_units(grad_q).reshape(token_rows, heads_q, HEAD_SIZE), cosine, sine_table
-            )
-            grad_k_pre = rotate_back(
-                grad_k.T.reshape(token_rows, heads_kv, HEAD_SIZE), cosine, sine_table
-            )
-            grad_qkv = jnp.concatenate(
-                [
-                    (grad_q_pre * scale_q).reshape(token_rows, q_width),
-                    grad_k_pre.reshape(token_rows, kv_width),
-                    grad_v.T,
-                ],
-                axis=1,
-            ).astype(BF16)
-            grad_norm_a = to_owner(project_back(grad_qkv, attn_w, 0, qkv_width))
-            d_qkv = weight_grad(normed_a, grad_qkv)
-            d_attn[layer] = weight_scatter(jnp.concatenate([d_qkv, d_out], axis=1))
-            d_mlp[layer] = (d_gu, d_down)
-            grad_res, d_gains[layer] = norm_back(
-                grad_res, grad_norm_a, residual_in, inverse_a, gain_a
-            )
+        else:
+            grad_res, d_gains, d_mlp, d_attn = backward_by_ops(grad_res)
         d_hidden = restore(grad_res)
-        d_gains = restore(jnp.stack(d_gains, axis=0))
-        d_gains = lax.psum_scatter(d_gains, "ctx", scatter_dimension=1, tiled=True)
+        d_gains = restore(d_gains)
         d_gains = d_gains + swap_head(d_gains)
+        bit = 1
+        while bit < n_ctx:
+            d_gains = d_gains + lax.ppermute(d_gains, "ctx", [(i, i ^ bit) for i in range(n_ctx)])
+            bit *= 2
+        d_gains = lax.dynamic_slice(d_gains, (0, ctx * db), (2 * layers, db))
         k_at, v_at = q_width, q_width + kv_width
-
-        def stack(parts):
-            return jnp.stack(parts, axis=0)
-
         return (
             out_hidden,
             d_hidden,
             d_gains[:layers],
-            stack([part[:, :k_at] for part in d_attn]),
-            stack([part[:, k_at:v_at] for part in d_attn]),
-            stack([part[:, v_at:qkv_width] for part in d_attn]),
-            stack([part[:, qkv_width:].T for part in d_attn]),
+            d_attn[:, :, :k_at],
+            d_attn[:, :, k_at:v_at],
+            d_attn[:, :, v_at:qkv_width],
+            d_attn[:, :, qkv_width:].transpose(0, 2, 1),
             d_gains[layers:],
-            stack([part[0][:, :ff_width] for part in d_mlp]),
-            stack([part[0][:, ff_width:] for part in d_mlp]),
-            stack([part[1].T for part in d_mlp]),
+            d_mlp[:, 1],
+            d_mlp[:, 2],
+            d_mlp[:, 0].transpose(0, 2, 1),
         )
 
     return local

time: 1100 us -> 874 us (0.79)
  Pallas kernels: 441 us -> 801 us
  waiting for transfers between devices: 279 us -> 2.51 us
  starting transfers between devices: 124 us -> 4.48 us
  other arithmetic: 83.2 us -> 9.33 us
  matrix products: 88.5 us -> 19.8 us
  local copies, waits for them, and re-layouts: 62.1 us -> 25 us
  between operations: 16.7 us -> 1.15 us
    pallas_call x2 -> x1, Pallas kernels: 32.9 us -> 387 us  [backward(): pl.pallas_call(functools.partial(backward_kernel, dims), out_shape=[jax.S...]
    ppermute x132 -> x4, waiting for transfers between devices: 203 us -> 2.51 us  [local(): lax.ppermute(d_gains, 'ctx', [(i, i ^ bit) for i in range(n_ctx)])]
    ppermute x132 -> x4, starting transfers between devices: 117 us -> 3.72 us  [local(): lax.ppermute(d_gains, 'ctx', [(i, i ^ bit) for i in range(n_ctx)])]
    dot_general x12 -> x0, matrix products: 51.2 us -> none  [the longest x8 34 us: dot_tn(): lax.dot_general(left, right, (((0,), (0,)), ((), ())), preferred_element_...]
    unnamed x2 -> x0, waiting for transfers between devices: 50.1 us -> none
    convert_element_type x67 -> x0, other arithmetic: 43.6 us -> none  [the longest x60 37.7 us: ring_scatter(): low, high = (low.astype(BF16), high.astype(BF16))]
    ppermute x9 -> x1, waiting for transfers between devices: 25.7 us -> 0.01 us  [swap_head(): return lax.ppermute(value, 'head', [(0, 1), (1, 0)])]
    dot_general x6 -> x2, matrix products: 22.7 us -> 5.36 us  [dot(): return jnp.dot(left, right, preferred_element_type=F32)]
  transfers between devices with their start and end apart: 142 -> 5, of which waited for: 78 -> 2; matrix products, arithmetic and copies ran while one was open for 20% -> 2% of each run, Pallas kernels for 40% -> 0%
where the time goes in v3:
time: 874 us; the launch traced here: 863 us
  Pallas kernels  801 us (92%)
  local copies, waits for them, and re-layouts  25 us (3%)
  matrix products  19.8 us (2%)
  other arithmetic  9.33 us (1%)
    pallas_call x1, Pallas kernels, forward(): pl.pallas_call(functools.partial(forward_kernel, dims), out_shape=[jax.Sh...  414 us
    pallas_call x1, Pallas kernels, backward(): pl.pallas_call(functools.partial(backward_kernel, dims), out_shape=[jax.S...  387 us
  transfers between devices with their start and end apart: 5, of which 2 were waited for; matrix products, arithmetic and copies ran while one was open for 2% of the time, Pallas kernels for 0%

profile of v3, /device:TPU:0, one launch (start us, length us, event | category | flops | bytes accessed | tf_op | source)
XLA Modules:
  0.0 863.4 jit_solution(17325696946501132348)
XLA Ops:
  0.7 1.0 slice_bitcast_fusion.11
  1.7 0.9 bitcast_dynamic-update-slice_fusion.1
  4.5 1.2 dynamic_slice.9
  7.0 5.6 rev.7
  12.6 0.7 fusion.32
  15.2 0.8 copy.53.refs_9_.refs_21_
  16.0 0.9 slice_bitcast_fusion.10
  17.0 0.9 slice_bitcast_fusion.12
  17.9 0.9 bitcast_dynamic-update-slice_fusion.3
  18.8 0.9 bitcast_dynamic-update-slice_fusion.2
  19.8 2.7 fusion.4
  22.5 2.7 fusion.10.refs_0_
  25.3 1.0 copy-done.7
  26.9 0.9 multiply_sine_fusion
  27.8 0.7 broadcast_add_fusion.refs_8_.refs_20_
  28.6 0.9 pad_maximum_fusion.3.refs_3_
  29.5 1.6 pad_maximum_fusion.1
  31.0 414.2 %shard_map.221 = (bf16[16,96,2432]{2,1,0:T(8,128)(2,1)}, bf16[16,96,6144]{2,1,0:T(8,128)(2,1)}, bf16[16,96,2304]{2,1,0:T(8,128)(2,1)}, bf16[16,96,6144]{2,1,0:T(...) custom-call(f32[128,1536]{1,0:T(8,128)} %bitcast.68, ...), custom_call_target="tpu_custom_call" | custom-call | tf_op jit(solution)/shard_map/pallas_call | solution.py:605
  445.2 1.2 slice.91
  446.4 1.3 pad_maximum_fusion.refs_15_
  447.7 386.9 %shard_map.222 = (f32[128,1536]{1,0:T(8,128)}, f32[4,1536]{1,0:T(4,128)}, f32[2,3,96,2048]{3,2,1,0:T(8,128)}, f32[2,96,2304]{2,1,0:T(8,128)}, bf16[2,3,2,7,96,10...) custom-call(f32[128,1536]{1,0:T(8,128)} %fusion.10.refs_0_, ...), custom_call_target="tpu_custom_call" | custom-call | tf_op jit(solution)/shard_map/pallas_call | solution.py:1088
  834.6 5.1 fusion
  839.7 0.8 collective-permute-start
  840.5 4.8 slice_bitcast_fusion
  845.4 1.1 slice_bitcast_fusion.3
  846.6 1.1 collective-permute-start.2
  847.7 6.1 fusion.1
  853.7 1.1 collective-permute-start.3
  854.8 2.9 fusion.11
  857.7 1.5 collective-permute-start.4
  859.2 0.8 fusion.35
  860.1 2.4 collective-permute-done.4
  (67 shorter events, 6.6 us)
Async XLA Ops:
  0.6 19.1 %copy-start = (bf16[128,1536]{1,0:T(8,128)(2,1)S(1)}, bf16[128,1536]{1,0:T(8,128)(2,1)}, u32[]{:S(2)}) copy-start(bf16[128,1536]{1,0:T(8,128)(2,1)} %param.14) | copy-start | bytes 1179652
  0.7 19.1 %copy-start.9 = (bf16[2,768,96]{1,2,0:T(8,128)(2,1)S(1)}, bf16[2,768,96]{1,2,0:T(8,128)(2,1)}, u32[]{:S(2)}) copy-start(bf16[2,768,96]{1,2,0:T(8,128)(2,1)} %param.21) | copy-start | bytes 884740
  19.8 2.7 copy-start.11
  22.5 2.7 copy-start.5
  22.5 2.7 copy-start.6
  25.1 1.1 copy-start.7
  28.6 2.4 copy-start.4
  31.0 415.4 %copy-start.2 = (f32[1536,128]{0,1:T(8,128)S(1)}, f32[1536,128]{0,1:T(8,128)}, u32[]{:S(2)}) copy-start(f32[1536,128]{0,1:T(8,128)} %fusion.4) | copy-start | bytes 2359300
  839.7 5.6 collective-permute-start
  840.5 4.9 copy-start.3
  845.3 2.4 copy-start.10
  845.3 1.3 collective-permute-start.1
  846.5 8.3 copy-start.8
  846.6 7.1 collective-permute-start.2
  853.7 9.4 %copy-start.1 = (bf16[128,1536]{1,0:T(8,128)(2,1)S(1)}, bf16[128,1536]{1,0:T(8,128)(2,1)}, u32[]{:S(2)}) copy-start(bf16[128,1536]{1,0:T(8,128)(2,1)} %param.14) | copy-start | bytes 1179652
  853.7 4.0 collective-permute-start.3
  857.7 4.8 collective-permute-start.4

commit v4 on v3

--- a/solution.py
+++ b/solution.py
@@ -331,29 +331,34 @@
 
 
 class Queue:
-    def __init__(self, rings, depth=2):
-        self.items = [(ring, event) for ring in rings for event in ring.events]
+    def __init__(self, rings, depth=4):
+        self.waiting = [(ring, event) for ring in rings for event in ring.events]
         self.depth = depth
-        self.landed = 0
-        self.issued = 0
+        self.flying = []
+        self.landed = set()
+        self.fill()
 
     def fill(self):
-        while self.issued < len(self.items) and self.issued < self.landed + self.depth:
-            ring, event = self.items[self.issued]
-            ring.issue(event)
-            self.issued += 1
+        for item in list(self.waiting):
+            if len(self.flying) == self.depth:
+                break
+            ring, (chain, step) = item
+            if step == 1 or (id(ring), chain, step - 1) in self.landed:
+                ring.issue((chain, step))
+                self.waiting.remove(item)
+                self.flying.append(item)
 
     def pump(self, count=1):
         for _ in range(count):
-            if self.landed < len(self.items):
-                ring, event = self.items[self.landed]
+            if self.flying:
+                ring, event = self.flying.pop(0)
                 ring.land(event)
-                self.landed += 1
+                self.landed.add((id(ring), *event))
                 self.fill()
 
     def through(self, ring):
-        last = max(i for i, item in enumerate(self.items) if item[0] is ring)
-        self.pump(last + 1 - self.landed)
+        while any(item[0] is ring for item in self.flying + self.waiting):
+            self.pump()
 
 
 TILE = 512
@@ -361,33 +366,36 @@
 
 def rms_inverse(rows):
     return lax.rsqrt(jnp.mean(rows * rows, axis=-1, keepdims=True) + EPS)
+
+
+def windows_of(wide, count):
+    blocks = wide // 128
+    edges = [blocks * i // count * 128 for i in range(count + 1)]
+    return [(low, high - low) for low, high in zip(edges, edges[1:])]
+
+
+CHAINS = (4, 4, 2)
 
 
 def forward_kernel(dims, *refs):
     layers, chips, width, q_width, kv_width, ff = dims
     slots = 2 * chips
+    parts = len(CHAINS)
     it = iter(refs)
-    x_ref = next(it)
-    shards = [next(it) for _ in range(2 * layers)]
+    x_ref, g_ref = next(it), next(it)
+    shards = [next(it) for _ in range(parts * layers)]
     cos_ref, sin_ref, kpos_ref, qpos_ref, qstart_ref = (next(it) for _ in range(5))
-    weights = [next(it) for _ in range(2 * layers)]
+    weights = [next(it) for _ in range(parts * layers)]
+    saved = [next(it) for _ in range(10)]
+    x_out_ref, gain_ref, g_rows_ref = next(it), next(it), next(it)
+    kept = [next(it) for _ in range(10)]
     (
-        kv_ref,
-        normed_a_ref,
-        qt_ref,
-        lse_ref,
-        att_ref,
-        middle_ref,
-        normed_m_ref,
-        gate_ref,
-        up_ref,
-        act_ref,
-        x_out_ref,
-        gain_ref,
-    ) = (next(it) for _ in range(12))
+        kv_ref, normed_a_ref, qt_ref, lse_ref, att_ref, middle_ref, normed_m_ref, gate_ref, up_ref, act_ref
+    ) = kept
     (
-        wt, wo, acc, proj_t, att_t, b_send, b_recv, gain_block, send_sems, recv_sems, load_sems, own_sems
-    ) = (next(it) for _ in range(12))
+        wt, wo, acc, proj_t, att_t, b_send, b_recv, gain_block,
+        g_rows, send_sems, recv_sems, load_sems, own_sems, save_sems,
+    ) = (next(it) for _ in range(14))
 
     rows = x_ref.shape[0]
     db = width // slots
@@ -402,18 +410,15 @@
     links.greet()
 
     rings = []
-    for shard, weight in zip(shards, weights):
-        wide = shard.shape[1]
-        cut = (wide // 256) * 128
-        rings.append(
-            RingGather(links, weight, [(0, db, 0, cut), (0, db, cut, wide - cut)], first=shard)
-        )
+    for i, (shard, weight) in enumerate(zip(shards, weights)):
+        chains = [(0, db, c0, cn) for c0, cn in windows_of(shard.shape[1], CHAINS[i % parts])]
+        rings.append(RingGather(links, weight, chains, first=shard))
     queue = Queue(rings)
-    queue.fill()
 
     def ready(i):
         queue.through(rings[i])
         rings[i].settle()
+        own_copies[i].wait()
 
     def load(i, column, wide, target, sem):
         copy = pltpu.make_async_copy(
@@ -425,18 +430,30 @@
     def flat(ref):
         return ref[...].reshape(width, ref.shape[-1])
 
+    saving = []
+
+    def save(i, layer):
+        copy = pltpu.make_async_copy(
+            kept[i].at[layer], saved[i].at[layer], save_sems.at[layer * len(kept) + i]
+        )
+        copy.start()
+        saving.append(copy)
+
+    g_rows[0:rows, :] = g_ref[...]
+    g_swap = links.to_head(g_rows.at[pl.ds(0, rows), :], g_rows.at[pl.ds(rows, rows), :])
+
     ready(0)
-    for copy in own_copies:
-        copy.wait()
     side = qkv_width + q_width
     load(0, side, 128, gain_block, 0).wait()
     gain_ref[...] = flat(gain_block).astype(F32).T[: gain_ref.shape[0], :]
 
     for layer in range(layers):
-        attn, mlp = 2 * layer, 2 * layer + 1
+        attn, gate_up, down_w = parts * layer, parts * layer + 1, parts * layer + 2
         if layer:
             ready(attn)
-        tiles = [load(attn, t * TILE, TILE, wt.at[t], t) for t in range(qkv_width // TILE)]
+        tiles = qkv_width // TILE
+        order = list(reversed(range(tiles)))
+        tile_loads = {t: load(attn, t * TILE, TILE, wt.at[t], t) for t in order}
         out_load = load(attn, qkv_width, q_width, wo, 6)
 
         x = x_ref[...] if layer == 0 else x_out_ref[layer - 1]
@@ -445,15 +462,19 @@
         swap = links.to_head(
             normed_a_ref.at[layer, pl.ds(0, rows), :], normed_a_ref.at[layer, pl.ds(rows, rows), :]
         )
-        for t, tile in enumerate(tiles):
-            tile.wait()
-            part = dot(normed_a_ref[layer, 0:rows, :], flat(wt.at[t]))
-            proj_t[t * TILE : (t + 1) * TILE, 0:rows] = part.T
+
+        def project(t, at):
+            part = dot(normed_a_ref[layer, at : at + rows, :], flat(wt.at[t]))
+            proj_t[t * TILE : (t + 1) * TILE, at : at + rows] = part.T
+
+        for t in order:
+            tile_loads[t].wait()
+            project(t, 0)
         swap.wait_recv()
-        for t in range(len(tiles)):
-            part = dot(normed_a_ref[layer, rows : 2 * rows, :], flat(wt.at[t]))
-            proj_t[t * TILE : (t + 1) * TILE, rows : 2 * rows] = part.T
-        queue.pump()
+        first_kv = q_width // TILE
+        for t in order:
+            if t >= first_kv:
+                project(t, rows)
 
         cosine, sine = cos_ref[...], sin_ref[...]
 
@@ -470,13 +491,19 @@
             q_width + kv_width : qkv_width, :
         ].astype(BF16)
         wide = kv_ref.shape[-1]
-        kv_ring = RingGather(
-            links,
-            kv_ref.at[layer],
-            [(0, kv_width, 0, wide), (kv_width, kv_width, 0, wide)],
-        )
-        kv_queue = Queue([kv_ring])
-        kv_queue.fill()
+        half = kv_width // 2
+        kv_rings = [
+            RingGather(
+                links,
+                kv_ref.at[layer],
+                [(i * half, half, 0, wide), (kv_width + i * half, half, 0, wide)],
+            )
+            for i in range(2)
+        ]
+        kv_queue = Queue(kv_rings)
+        for t in order:
+            if t < first_kv:
+                project(t, rows)
         scale = HEAD_SIZE ** (-0.5)
         for h in range(q_width // HEAD_SIZE):
             low, high = turned(h * HEAD_SIZE)
@@ -484,14 +511,11 @@
             qt_ref[layer, h * HEAD_SIZE + HALF : (h + 1) * HEAD_SIZE, :] = (high * scale).astype(
                 BF16
             )
-        for step in range(len(kv_queue.items)):
-            kv_queue.pump()
-            if step % 3 == 2:
-                queue.pump()
-        kv_ring.settle()
+        save(1, layer)
+        save(2, layer)
 
         def unit(u, carry):
-            s, h = u // heads_kv, u % heads_kv
+            h, s = u // SEQS, u % SEQS
             k_rows = pl.ds(pl.multiple_of(h * HEAD_SIZE, HEAD_SIZE), HEAD_SIZE)
             v_rows = pl.ds(pl.multiple_of(kv_width + h * HEAD_SIZE, HEAD_SIZE), HEAD_SIZE)
             lanes = pl.ds(pl.multiple_of(s * ROWS, ROWS), ROWS)
@@ -516,10 +540,25 @@
             return carry
 
         units = SEQS * heads_kv
-        for at in range(0, units, 2):
-            lax.fori_loop(at, at + 2, unit, 0)
-            queue.pump()
+        for i, ring in enumerate(kv_rings):
+            kv_queue.through(ring)
+            ring.settle()
+            queue.pump(2)
+            low, high = units * i // 2, units * (i + 1) // 2
+            if i == 0:
+                for u in range(low, high):
+                    lax.fori_loop(u, u + 1, unit, 0)
+                    kv_queue.pump(2)
+            else:
+                save(0, layer)
+                middle_unit = (low + high) // 2
+                lax.fori_loop(low, middle_unit, unit, 0)
+                queue.pump(2)
+                lax.fori_loop(middle_unit, high, unit, 0)
+        queue.pump(2)
         att_ref[layer] = att_t[...].T.astype(BF16)
+        save(3, layer)
+        save(4, layer)
 
         out_load.wait()
         branch = (layer * 2) % b_send.shape[0]
@@ -527,57 +566,80 @@
         b_send[branch] = other.astype(BF16)
         swap = links.to_head(b_send.at[branch], b_recv.at[branch])
         mine = dot_nt(att_ref[layer, 0:rows, :], flat(wo))
-        queue.pump()
+        queue.pump(2)
         swap.wait_recv()
         middle = x + mine + b_recv[branch].astype(F32)
         middle_ref[layer] = middle
+        save(5, layer)
         gain_m = gain_ref[layers + layer : layers + layer + 1, :]
         normed_m_ref[layer, 0:rows, :] = (middle * rms_inverse(middle) * gain_m).astype(BF16)
         swap = links.to_head(
             normed_m_ref.at[layer, pl.ds(0, rows), :], normed_m_ref.at[layer, pl.ds(rows, rows), :]
         )
-        ready(mlp)
+        ready(gate_up)
 
         def load_tile(t):
-            at = (t % 2) * 3
+            at = (t % 2) * 2
             return [
-                load(mlp, part * ff + t * TILE, TILE, wt.at[at + part], at + part)
-                for part in range(3)
+                load(gate_up, part * ff + t * TILE, TILE, wt.at[at + part], at + part)
+                for part in range(2)
             ]
 
         pending = load_tile(0)
         swap.wait_recv()
+        save(6, layer)
         normed = normed_m_ref[layer]
         count = ff // TILE
         for t in range(count):
             following = load_tile(t + 1) if t + 1 < count else None
             for copy in pending:
                 copy.wait()
-            at = (t % 2) * 3
+            at = (t % 2) * 2
             columns = slice(t * TILE, (t + 1) * TILE)
             gate = dot(normed, flat(wt.at[at]))
             up = dot(normed, flat(wt.at[at + 1]))
-            act = (gate * jax.nn.sigmoid(gate) * up).astype(BF16)
             gate_ref[layer, :, columns] = gate.astype(BF16)
             up_ref[layer, :, columns] = up.astype(BF16)
-            act_ref[layer, :, columns] = act
-            down = dot_nt(act, flat(wt.at[at + 2]))
+            act_ref[layer, :, columns] = (gate * jax.nn.sigmoid(gate) * up).astype(BF16)
+            pending = following
+            queue.pump()
+        for i in (7, 8, 9):
+            save(i, layer)
+        ready(down_w)
+        if layer == layers - 1:
+            break
+
+        def load_down(t):
+            return load(down_w, t * TILE, TILE, wt.at[4 + t % 2], 4 + t % 2)
+
+        pending = load_down(0)
+        for t in range(count):
+            following = load_down(t + 1) if t + 1 < count else None
+            pending.wait()
+            down = dot_nt(act_ref[layer, :, t * TILE : (t + 1) * TILE], flat(wt.at[4 + t % 2]))
             if t == 0:
                 acc[...] = down
             else:
                 acc[...] += down
             pending = following
-            queue.pump(2)
         branch = (layer * 2 + 1) % b_send.shape[0]
         b_send[branch] = acc[rows : 2 * rows, :].astype(BF16)
         swap = links.to_head(b_send.at[branch], b_recv.at[branch])
+        queue.pump(2)
         swap.wait_recv()
         x_out_ref[layer] = middle_ref[layer] + acc[0:rows, :] + b_recv[branch].astype(F32)
+    g_swap.wait_recv()
+    g_copy = pltpu.make_async_copy(g_rows, g_rows_ref, load_sems.at[0])
+    g_copy.start()
+    g_copy.wait()
+    for copy in saving:
+        copy.wait()
     links.finish()
 
 
-def forward(x, shards, cosine, sine, kpos, qpos, qstart, chips, q_width, kv_width, ff):
-    layers = len(shards) // 2
+def forward(x, grad, shards, cosine, sine, kpos, qpos, qstart, chips, q_width, kv_width, ff):
+    parts = len(CHAINS)
+    layers = len(shards) // parts
     rows, width = x.shape
     db = shards[0].shape[0]
     slots = 2 * chips
@@ -585,29 +647,34 @@
     tokens = 2 * rows
     units = SEQS * kv_width // HEAD_SIZE
     dims = (layers, chips, width, q_width, kv_width, ff)
-    copies = (2 * layers + layers) * RingGather.copies(chips, 2) + 4 * layers
-    any_spec = pl.BlockSpec(memory_space=pl.ANY)
+    copies = layers * (RingGather.copies(chips, sum(CHAINS) + 4) + 4)
+    any_spec = pl.BlockSpec(memory_space=pltpu.HBM)
     vmem = pl.BlockSpec(memory_space=pltpu.VMEM)
     saved = [
-        jax.ShapeDtypeStruct((layers, slots, 2 * kv_width, tokens), BF16),
-        jax.ShapeDtypeStruct((layers, tokens, width), BF16),
-        jax.ShapeDtypeStruct((layers, q_width, tokens), BF16),
-        jax.ShapeDtypeStruct((layers, units, group * ROWS, 1), F32),
-        jax.ShapeDtypeStruct((layers, tokens, q_width), BF16),
-        jax.ShapeDtypeStruct((layers, rows, width), F32),
-        jax.ShapeDtypeStruct((layers, tokens, width), BF16),
-        jax.ShapeDtypeStruct((layers, tokens, ff), BF16),
-        jax.ShapeDtypeStruct((layers, tokens, ff), BF16),
-        jax.ShapeDtypeStruct((layers, tokens, ff), BF16),
-        jax.ShapeDtypeStruct((layers, rows, width), F32),
-        jax.ShapeDtypeStruct((2 * layers, width), F32),
+        ((layers, slots, 2 * kv_width, tokens), BF16),
+        ((layers, tokens, width), BF16),
+        ((layers, q_width, tokens), BF16),
+        ((layers, units, group * ROWS, 1), F32),
+        ((layers, tokens, q_width), BF16),
+        ((layers, rows, width), F32),
+        ((layers, tokens, width), BF16),
+        ((layers, tokens, ff), BF16),
+        ((layers, tokens, ff), BF16),
+        ((layers, tokens, ff), BF16),
     ]
     out = pl.pallas_call(
         functools.partial(forward_kernel, dims),
-        out_shape=[jax.ShapeDtypeStruct((slots,) + shard.shape, BF16) for shard in shards] + saved,
-        in_specs=[vmem] + [any_spec] * len(shards) + [vmem] * 5,
-        out_specs=[any_spec] * len(shards) + [vmem] * len(saved),
-        scratch_shapes=[
+        out_shape=[jax.ShapeDtypeStruct((slots,) + shard.shape, BF16) for shard in shards]
+        + [jax.ShapeDtypeStruct(*entry) for entry in saved]
+        + [
+            jax.ShapeDtypeStruct((layers - 1, rows, width), F32),
+            jax.ShapeDtypeStruct((2 * layers, width), F32),
+            jax.ShapeDtypeStruct((tokens, width), BF16),
+        ],
+        in_specs=[vmem] * 2 + [any_spec] * len(shards) + [vmem] * 5,
+        out_specs=[any_spec] * (len(shards) + len(saved)) + [vmem] * 2 + [any_spec],
+        scratch_shapes=[pltpu.VMEM(*entry) for entry in saved]
+        + [
             pltpu.VMEM((6, slots, db, TILE), BF16),
             pltpu.VMEM((slots, db, q_width), BF16),
             pltpu.VMEM((tokens, width), F32),
@@ -616,21 +683,23 @@
             pltpu.VMEM((2 * layers, rows, width), BF16),
             pltpu.VMEM((2 * layers, rows, width), BF16),
             pltpu.VMEM((slots, db, 128), BF16),
+            pltpu.VMEM((tokens, width), BF16),
             pltpu.SemaphoreType.DMA((copies,)),
             pltpu.SemaphoreType.DMA((copies,)),
             pltpu.SemaphoreType.DMA((7,)),
             pltpu.SemaphoreType.DMA((len(shards),)),
+            pltpu.SemaphoreType.DMA((layers * len(saved),)),
         ],
         compiler_params=pltpu.CompilerParams(
             collective_id=0, has_side_effects=True, vmem_limit_bytes=KERNEL_VMEM
         ),
-    )(x, *shards, cosine, sine, kpos, qpos, qstart)
+    )(x, grad, *shards, cosine, sine, kpos, qpos, qstart)
     return out[: len(shards)], out[len(shards) :]
 
 
 class RingScatter:
-    def __init__(self, links, windows, landing, stage, sems, finish):
-        self.links, self.windows, self.landing = links, windows, landing
+    def __init__(self, links, windows, landings, finish, stage=None, sems=None):
+        self.links, self.windows, self.landings = links, windows, landings
         self.stage, self.sems, self.finish = stage, sems, finish
         self.last = links.chips - 1
         self.step = 0
@@ -642,56 +711,75 @@
         slots = ((chips - self.step) % chips, self.step % chips)
         sends = (self.links.to_right, self.links.to_left)
         self.moving = [
-            sends[d](self.windows[d](slots[d]), self.landing.at[d, self.step - 1])
-            for d in range(2)
+            sends[d](self.windows[d](slots[d]), self.landings[d](self.step - 1)) for d in range(2)
         ]
 
-    def land(self):
-        chips, wide = self.links.chips, self.landing.shape[-1]
-        loads = []
+    def arrive(self, place=0):
+        self.here, self.loads = [], []
         for d in range(2):
             self.moving[d].wait_recv()
             self.links.sent(self.moving[d])
-            load = pltpu.make_async_copy(
-                self.landing.at[d, self.step - 1],
-                self.stage.at[d, :, pl.ds(0, wide)],
-                self.sems.at[d],
-            )
-            load.start()
-            loads.append(load)
+            here = self.landings[d](self.step - 1)
+            if self.stage is not None:
+                there = self.stage.at[place, d, :, pl.ds(0, here.shape[-1])]
+                load = pltpu.make_async_copy(here, there, self.sems.at[2 * place + d])
+                load.start()
+                self.loads.append(load)
+                here = there
+            self.here.append(here)
+
+    def absorb(self):
+        chips = self.links.chips
+        for load in self.loads:
+            load.wait()
         slots = ((chips - 1 - self.step) % chips, (1 + self.step) % chips)
         for d in range(2):
-            loads[d].wait()
             window = self.windows[d](slots[d])
-            total = window[...].astype(F32) + self.stage[d, :, 0:wide].astype(F32)
+            total = window[...].astype(F32) + self.here[d][...].astype(F32)
             if self.step < self.last:
                 window[...] = total.astype(BF16)
             else:
                 self.finish(d, total)
         if self.step < self.last:
             self.issue()
+            return False
+        return True
 
 
 class Rounds:
-    def __init__(self):
-        self.active = []
+    def __init__(self, at_once=False):
+        self.active, self.loading, self.place, self.at_once = [], None, 0, at_once
 
     def start(self, ring):
         ring.issue()
-        ring.left = ring.last
         self.active.append(ring)
+        return ring
+
+    def absorb(self):
+        if self.loading is not None:
+            ring, self.loading = self.loading, None
+            if not ring.absorb():
+                self.active.append(ring)
 
     def pump(self, count=1):
+        self.absorb()
         for _ in range(count):
-            if self.active:
-                ring = self.active.pop(0)
-                ring.land()
-                ring.left -= 1
-                if ring.left:
-                    self.active.append(ring)
-
-    def drain(self):
-        while self.active:
+            if not self.active:
+                break
+            ring = self.active.pop(0)
+            self.place = 1 - self.place
+            ring.arrive(self.place)
+            self.absorb()
+            self.loading = ring
+        if self.at_once:
+            self.absorb()
+
+    def drain(self, rings=None):
+        def under_way():
+            pending = self.active + ([] if self.loading is None else [self.loading])
+            return [ring for ring in pending if rings is None or any(ring is one for one in rings)]
+
+        while under_way():
             self.pump()
 
 
@@ -699,21 +787,24 @@
     layers, chips, width, q_width, kv_width, ff = dims
     slots = 2 * chips
     it = iter(refs)
-    g_ref = next(it)
-    weights = [next(it) for _ in range(2 * layers)]
+    g_ref, g_rows_ref = next(it), next(it)
+    parts = len(CHAINS)
+    weights = [next(it) for _ in range(parts * layers)]
     (
         kv_ref, normed_a_ref, qt_ref, lse_ref, att_ref, middle_ref, normed_m_ref,
         gate_ref, up_ref, act_ref, x_in_ref, gain_ref,
         cos_ref, sin_ref, kpos_ref, qpos_ref, qstart_ref,
     ) = (next(it) for _ in range(17))
-    d_hidden_ref, d_gain_ref = next(it), next(it)
-    d_mlp_ref, d_attn_ref = next(it), next(it)
-    land_mlp, land_out, land_q, land_kv, land_dkv = (next(it) for _ in range(5))
+    d_hidden_ref, d_gain_ref, x_out_ref = next(it), next(it), next(it)
+    d_query_ref, d_key_ref, d_value_ref, d_out_ref, d_w_gate_ref, d_w_up_ref, d_down_ref = (
+        next(it) for _ in range(7)
+    )
+    land_down, land_gu, land_out, land_q = (next(it) for _ in range(4))
     (
-        wt, kv_buf, dkv_sib, dw_mlp, dw_attn, a_sib, at_buf, g_act, g_gu, g_qkv, g_att, acc,
+        wt, kv_buf, dkv_sib, dw_mlp, dw_attn, a_sib, at_buf, g_act, g_gu, g_att, acc,
         g_low, g2_low, b_send, b_recv, qt_l, lse_l, da_t, dq_t, dkv_sum, gu_buf, rows_f32, n_own,
-        stage, out_stage, send_sems, recv_sems, load_sems, stage_sems,
-    ) = (next(it) for _ in range(30))
+        stage, out_stage, turn_stage, land_kv, land_dkv, send_sems, recv_sems, load_sems, stage_sems,
+    ) = (next(it) for _ in range(32))
 
     rows = g_ref.shape[0]
     tokens = 2 * rows
@@ -724,6 +815,7 @@
     qkv_width = q_width + 2 * kv_width
     links = Links(chips, send_sems, recv_sems)
     links.greet()
+    g_qkv = g_gu.at[:, pl.ds(0, qkv_width)]
     rounds = Rounds()
     cosine, sine = cos_ref[...], sin_ref[...]
     scale = HEAD_SIZE ** (-0.5)
@@ -739,32 +831,38 @@
     def flat(ref):
         return ref[...].reshape(width, ref.shape[-1])
 
-    def out_by(target):
+    def write(d, total, target, turned):
+        if turned:
+            total = total.T
+            source = turn_stage.at[d, pl.ds(0, total.shape[0]), :]
+        else:
+            source = out_stage.at[d, :, pl.ds(0, total.shape[1])]
+        source[...] = total
+        copy = pltpu.make_async_copy(source, target, stage_sems.at[4 + d])
+        copy.start()
+        copy.wait()
+
+    def scatter(ref, column, sizes, landing, out, at, turned=False, staged=True):
+        offsets = (0, sizes[0])
+
+        def window(d):
+            return lambda slot: ref.at[slot, :, pl.ds(column + offsets[d], sizes[d])]
+
+        def land(d):
+            return lambda step: landing.at[d, step, :, pl.ds(0, sizes[d])]
+
         def finish(d, total):
-            wide = total.shape[-1]
-            out_stage[d, :, 0:wide] = total
-            copy = pltpu.make_async_copy(
-                out_stage.at[d, :, pl.ds(0, wide)], target(d), stage_sems.at[d]
-            )
-            copy.start()
-            copy.wait()
-
-        return finish
-
-    def scatter(ref, column, wide, landing, out):
-        half = wide // 2
-
-        def window(d):
-            return lambda slot: ref.at[slot, :, pl.ds(column + d * half, half)]
-
-        rounds.start(
+            there = pl.ds(at + offsets[d], sizes[d])
+            write(d, total, out.at[there, :] if turned else out.at[:, there], turned)
+
+        return rounds.start(
             RingScatter(
                 links,
                 (window(0), window(1)),
-                landing,
-                stage,
+                (land(0), land(1)),
+                finish,
+                stage if staged else None,
                 stage_sems,
-                out_by(lambda d: out.at[:, pl.ds(column + d * half, half)]),
             )
         )
 
@@ -789,9 +887,11 @@
         d_hidden_ref[...] += inverse * (scaled - normalized * mean)
 
 
-    d_hidden_ref[...] = g_ref[...]
+    local(g_ref, d_hidden_ref, 10).wait()
+    pairs = (heads_kv + 1) // 2
+    mlp_rings, attn_rings = [], []
     for layer in reversed(range(layers)):
-        attn, mlp = 2 * layer, 2 * layer + 1
+        attn, gate_up, down_w = parts * layer, parts * layer + 1, parts * layer + 2
         gain_a = gain_ref[layer : layer + 1, :]
         gain_m = gain_ref[layers + layer : layers + layer + 1, :]
         links.finish()
@@ -800,37 +900,60 @@
             at = (t % 2) * 3
             columns = pl.ds(t * TILE, TILE)
             return [
-                load(mlp, part * ff + t * TILE, TILE, wt.at[at + part], at + part)
-                for part in range(3)
-            ] + [
+                load(down_w, t * TILE, TILE, wt.at[at + 2], at + 2),
+                load(gate_up, t * TILE, TILE, wt.at[at], at),
+                load(gate_up, ff + t * TILE, TILE, wt.at[at + 1], at + 1),
                 local(gate_ref.at[layer, :, columns], gu_buf.at[t % 2, 0], 6 + t % 2 * 2),
                 local(up_ref.at[layer, :, columns], gu_buf.at[t % 2, 1], 7 + t % 2 * 2),
             ]
 
-        pending = load_tile(0)
-        g_low[0:rows, :] = d_hidden_ref[...].astype(BF16)
-        swap = links.to_head(g_low.at[pl.ds(0, rows), :], g_low.at[pl.ds(rows, rows), :])
+        if layer == layers - 1:
+            g_load = local(g_rows_ref, g_low, 11)
+        else:
+            g_low[0:rows, :] = d_hidden_ref[...].astype(BF16)
+            swap = links.to_head(g_low.at[pl.ds(0, rows), :], g_low.at[pl.ds(rows, rows), :])
         far = pl.ds(side, side)
         other_rows = pl.ds(tokens, tokens)
+        from_sib_act = links.to_sibling(act_ref.at[layer], g_act.at[other_rows, :])
+        here_act = local(act_ref.at[layer], g_act.at[pl.ds(0, tokens), :], 10)
+        pending = load_tile(0)
         from_sib = [
-            links.to_sibling(act_ref.at[layer], g_act.at[other_rows, :]),
             links.to_sibling(normed_m_ref.at[layer, :, far], a_sib.at[1]),
             links.to_sibling(normed_a_ref.at[layer, :, far], a_sib.at[3]),
             links.to_sibling(att_ref.at[layer], g_att.at[other_rows, :]),
         ]
         here = [
-            local(act_ref.at[layer], g_act.at[pl.ds(0, tokens), :], 10),
-            local(normed_m_ref.at[layer, :, pl.ds(0, side)], n_own.at[0], 11),
-            local(normed_a_ref.at[layer, :, pl.ds(0, side)], n_own.at[1], 12),
-            local(att_ref.at[layer], g_att.at[pl.ds(0, tokens), :], 13),
-            local(middle_ref.at[layer], rows_f32.at[0], 14),
-            local(x_in_ref.at[layer], rows_f32.at[1], 15),
+            local(normed_m_ref.at[layer, :, pl.ds(0, side)], n_own, 13),
+            local(att_ref.at[layer], g_att.at[pl.ds(0, tokens), :], 15),
+            local(middle_ref.at[layer], rows_f32, 14),
             local(qt_ref.at[layer], qt_l, 16),
             local(lse_ref.at[layer], lse_l, 17),
         ]
-        rounds.pump()
-        swap.wait_recv()
+        rounds.drain(mlp_rings)
+        if layer == layers - 1:
+            g_load.wait()
+        else:
+            swap.wait_recv()
         from_sib_g = links.to_sibling(g_low.at[:, far], a_sib.at[0])
+        here_act.wait()
+        from_sib_act.wait_recv()
+        from_sib_g.wait_recv()
+        turn_columns(g_low[:, 0:side], a_sib[0])
+        weight_grad(dw_mlp.at[0], 0, g_act, ff)
+        mlp_rings = []
+        for i in range(2):
+            size = ff // 4
+            mlp_rings.append(
+                scatter(
+                    dw_mlp.at[0],
+                    2 * i * size,
+                    (size, size),
+                    land_down.at[layer, i],
+                    d_down_ref.at[layer],
+                    2 * i * size,
+                    turned=True,
+                )
+            )
         count = ff // TILE
         from_sib_gu = []
         for t in range(count):
@@ -853,42 +976,44 @@
                         g_gu.at[other_rows, pl.ds(column, TILE)],
                     )
                 )
-            back = dot_nt(d_gate, flat(wt.at[at])) + dot_nt(d_up, flat(wt.at[at + 1]))
             if t == 0:
-                acc[...] = back
+                acc[...] = dot_nt(d_gate, flat(wt.at[at]))
             else:
-                acc[...] += back
+                acc[...] += dot_nt(d_gate, flat(wt.at[at]))
+            acc[...] += dot_nt(d_up, flat(wt.at[at + 1]))
             pending = following
-            rounds.pump(3)
+            rounds.pump(3 if len(rounds.active) > 2 else 1)
         b_send[0] = acc[rows:tokens, :].astype(BF16)
         swap = links.to_head(b_send.at[0], b_recv.at[0])
         out_loads = [
             load(attn, qkv_width, TILE, wt.at[4], 4),
             load(attn, qkv_width + TILE, q_width - TILE, wt.at[5, :, :, pl.ds(0, q_width - TILE)], 5),
         ]
-        rounds.drain()
         for copy in here:
             copy.wait()
-        from_sib_g.wait_recv()
-        for copy in from_sib:
+        for copy in from_sib + from_sib_gu:
             copy.wait_recv()
-        turn_columns(g_low[:, 0:side], a_sib[0])
-        weight_grad(dw_mlp.at[0], 0, g_act, ff)
-        scatter(dw_mlp.at[0], 0, ff, land_mlp.at[layer, 0], d_mlp_ref.at[layer, 0])
+
+        def gate_up_grad(part):
+            weight_grad(dw_mlp.at[1 + part], 0, g_gu.at[:, pl.ds(part * ff, ff)], ff)
+            out = (d_w_gate_ref, d_w_up_ref)[part].at[layer]
+            return scatter(
+                dw_mlp.at[1 + part], 0, (ff // 2, ff // 2), land_gu.at[layer, part], out, 0
+            )
+
+        turn_columns(n_own[...], a_sib[1])
+        here = [local(normed_a_ref.at[layer, :, pl.ds(0, side)], n_own, 12)]
+        mlp_rings.append(gate_up_grad(0))
+        rounds.pump(2)
         swap.wait_recv()
         norm_back(
-            acc[0:rows, :] + b_recv[0].astype(F32), rows_f32[0], gain_m, layers + layer
+            acc[0:rows, :] + b_recv[0].astype(F32), rows_f32[...], gain_m, layers + layer
         )
         g2_low[0:rows, :] = d_hidden_ref[...].astype(BF16)
         swap = links.to_head(g2_low.at[pl.ds(0, rows), :], g2_low.at[pl.ds(rows, rows), :])
-        for copy in from_sib_gu:
-            copy.wait_recv()
-        turn_columns(n_own[0], a_sib[1])
-        for part in range(2):
-            weight_grad(dw_mlp.at[1 + part], 0, g_gu.at[:, pl.ds(part * ff, ff)], ff)
-            scatter(
-                dw_mlp.at[1 + part], 0, ff, land_mlp.at[layer, 1 + part], d_mlp_ref.at[layer, 1 + part]
-            )
+        mlp_rings.append(gate_up_grad(1))
+        rounds.pump(2)
+        rounds.drain(attn_rings)
 
         swap.wait_recv()
         from_sib_g = links.to_sibling(g2_low.at[:, far], a_sib.at[2])
@@ -898,12 +1023,29 @@
             part = dot(g2_low[...], flat(wt.at[4 + i, :, :, pl.ds(0, size)]))
             da_t[i * TILE : i * TILE + size, :] = part.T.astype(BF16)
         rounds.pump()
+        if layer == layers - 1:
+            def load_down(t):
+                return load(down_w, t * TILE, TILE, wt.at[4 + t % 2], 4 + t % 2)
+
+            pending = load_down(0)
+            for t in range(count):
+                following = load_down(t + 1) if t + 1 < count else None
+                pending.wait()
+                down = dot_nt(g_act[0:tokens, t * TILE : (t + 1) * TILE], flat(wt.at[4 + t % 2]))
+                if t == 0:
+                    acc[...] = down
+                else:
+                    acc[...] += down
+                pending = following
+            b_send[2] = acc[rows:tokens, :].astype(BF16)
+            out_swap = links.to_head(b_send.at[2], b_recv.at[2])
+            rows_f32[...] += acc[0:rows, :]
+            rounds.pump(2)
 
         units = SEQS * heads_kv
-        pairs = (heads_kv + 1) // 2
 
         def unit_copies(u, at):
-            s, h = u // heads_kv, u % heads_kv
+            h, s = u // SEQS, u % SEQS
             lanes = pl.ds(pl.multiple_of(s * ROWS, ROWS), ROWS)
             return [
                 pltpu.make_async_copy(
@@ -921,7 +1063,7 @@
 
         def unit(u, carry):
             at = u % 2
-            s, h = u // heads_kv, u % heads_kv
+            h, s = u // SEQS, u % SEQS
             for copy in unit_copies(u, at):
                 copy.wait()
             ahead = jnp.minimum(u + 1, units - 1)
@@ -958,23 +1100,14 @@
                 wt[pairs + h // 2, j, :, spot] = dvt[:, j * ROWS : (j + 1) * ROWS].astype(BF16)
             return carry
 
-        for copy in unit_copies(0, 0):
-            copy.start()
-        for u in range(0, units, 2):
-            lax.fori_loop(u, u + 2, unit, 0)
-            rounds.pump(2)
-
-        sent = []
-        for i in range(2 * pairs):
-            sent.append(
-                links.to_sibling(wt.at[i, pl.ds(chips, chips)], dkv_sib.at[i])
-            )
-        from_sib_g.wait_recv()
-        turn_columns(g2_low[:, 0:side], a_sib[2])
-        weight_grad(dw_attn, qkv_width, g_att, q_width)
-        scatter(dw_attn, qkv_width, q_width, land_out.at[layer], d_attn_ref.at[layer])
-        sums = Rounds()
-        for i in range(pairs):
+        sums = Rounds(at_once=True)
+        sent = {}
+
+        def offer(i):
+            for j in (i, pairs + i):
+                sent[j] = links.to_sibling(wt.at[j, pl.ds(chips, chips)], dkv_sib.at[j])
+
+        def total_up(i):
             for j in (i, pairs + i):
                 sent[j].wait_recv()
                 for slot in range(chips):
@@ -982,25 +1115,57 @@
                         BF16
                     )
 
-            def keep(i):
-                def finish(d, total):
-                    dkv_sum[d * pairs + i] = total
-
-                return finish
+            def finish(d, total):
+                dkv_sum[d * pairs + i] = total
 
             sums.start(
                 RingScatter(
                     links,
+                    (lambda slot: wt.at[i, slot], lambda slot: wt.at[pairs + i, slot]),
                     (
-                        lambda slot, i=i: wt.at[i, slot],
-                        lambda slot, i=i: wt.at[pairs + i, slot],
+                        lambda step: land_dkv.at[i, 0, step],
+                        lambda step: land_dkv.at[i, 1, step],
                     ),
-                    land_dkv.at[layer, i],
-                    stage,
-                    stage_sems,
-                    keep(i),
+                    finish,
                 )
             )
+
+        for copy in unit_copies(0, 0):
+            copy.start()
+        for i in range(pairs):
+            low, high = units * i // pairs, units * (i + 1) // pairs
+            if i == 0:
+                middle_unit = (low + high) // 2
+                lax.fori_loop(low, middle_unit, unit, 0)
+                rounds.pump(3)
+                lax.fori_loop(middle_unit, high, unit, 0)
+                rounds.pump(3)
+            else:
+                for u in range(low, high):
+                    lax.fori_loop(u, u + 1, unit, 0)
+                    if u == low:
+                        total_up(i - 1)
+                    else:
+                        sums.pump(2)
+                    rounds.pump()
+            offer(i)
+
+        if layer == layers - 1:
+            out_swap.wait_recv()
+            links.sent(out_swap)
+            b_send[2] = (rows_f32[...] + b_recv[2].astype(F32)).astype(BF16)
+            local(b_send.at[2], x_out_ref, 11).wait()
+        here.append(local(x_in_ref.at[layer], rows_f32, 15))
+        from_sib_g.wait_recv()
+        turn_columns(g2_low[:, 0:side], a_sib[2])
+        weight_grad(dw_attn, qkv_width, g_att, q_width)
+        half = q_width // 2
+        attn_rings = [
+            scatter(
+                dw_attn, qkv_width, (half, half), land_out.at[layer], d_out_ref.at[layer], 0, turned=True
+            )
+        ]
+        total_up(pairs - 1)
 
         def turned_back(low, high):
             return low * cosine + high * sine, high * cosine - low * sine
@@ -1012,6 +1177,8 @@
             )
             dq_t[at : at + HALF, :] = low * scale
             dq_t[at + HALF : at + HEAD_SIZE, :] = high * scale
+        for copy in from_sib_gu:
+            links.sent(copy)
         g_qkv[0:tokens, 0:q_width] = dq_t[...].T.astype(BF16)
         mine = pl.ds(0, tokens)
         from_sib_q = links.to_sibling(
@@ -1021,13 +1188,19 @@
         while sums.active:
             sums.pump()
             step += 1
-            if step % 2 == 0:
+            if step % 3 == 0:
                 rounds.pump()
             if step == 4:
                 from_sib_q.wait_recv()
-                turn_columns(n_own[1], a_sib[3])
+                for copy in here:
+                    copy.wait()
+                turn_columns(n_own[...], a_sib[3])
                 weight_grad(dw_attn, 0, g_qkv, q_width)
-                scatter(dw_attn, 0, q_width, land_q.at[layer], d_attn_ref.at[layer])
+                attn_rings.append(
+                    scatter(
+                        dw_attn, 0, (half, half), land_q.at[layer], d_query_ref.at[layer], 0
+                    )
+                )
         for h in range(heads_kv):
             spot = slice((h % 2) * SEQS * ROWS, (h % 2 + 1) * SEQS * ROWS)
             block = dkv_sum[h // 2, :, spot]
@@ -1056,16 +1229,31 @@
         swap = links.to_head(b_send.at[1], b_recv.at[1])
         from_sib_kv.wait_recv()
         weight_grad(dw_attn, q_width, g_qkv.at[:, pl.ds(q_width, 2 * kv_width)], 2 * kv_width)
-        scatter(dw_attn, q_width, 2 * kv_width, land_kv.at[layer], d_attn_ref.at[layer])
+        long = -(-kv_width // 256) * 128
+        short = kv_width - long
+        for i, (out, sizes) in enumerate(
+            ((d_key_ref, (long, short)), (d_value_ref, (short, long)))
+        ):
+            attn_rings.append(
+                scatter(
+                    dw_attn,
+                    q_width + i * kv_width,
+                    sizes,
+                    land_kv.at[i],
+                    out.at[layer],
+                    0,
+                    staged=False,
+                )
+            )
         rounds.pump()
         swap.wait_recv()
-        norm_back(acc[0:rows, :] + b_recv[1].astype(F32), rows_f32[1], gain_a, layer)
+        norm_back(acc[0:rows, :] + b_recv[1].astype(F32), rows_f32[...], gain_a, layer)
     rounds.drain()
     links.finish()
 
 
-def backward(grad, weights, saved, tables, chips, q_width, kv_width, ff):
-    layers = len(weights) // 2
+def backward(grad, grad_rows, weights, saved, tables, chips, q_width, kv_width, ff):
+    layers = len(weights) // len(CHAINS)
     rows, width = grad.shape
     slots = 2 * chips
     db = width // slots
@@ -1077,9 +1265,9 @@
     steps = chips - 1
     qkv_width = q_width + 2 * kv_width
     dims = (layers, chips, width, q_width, kv_width, ff)
-    rings = 3 + 3 + pairs
-    copies = layers * (rings * 2 * steps + 4 + 4 + 1 + 2 * (ff // TILE) + 1 + 2 * pairs + 2)
-    any_spec = pl.BlockSpec(memory_space=pl.ANY)
+    rings = 4 + 4 + pairs
+    copies = 1 + layers * (rings * 2 * steps + 4 + 4 + 1 + 2 * (ff // TILE) + 1 + 2 * pairs + 2)
+    any_spec = pl.BlockSpec(memory_space=pltpu.HBM)
     vmem = pl.BlockSpec(memory_space=pltpu.VMEM)
 
     def landing(*shape):
@@ -1090,16 +1278,21 @@
         out_shape=[
             jax.ShapeDtypeStruct((rows, width), F32),
             jax.ShapeDtypeStruct((2 * layers, width), F32),
-            jax.ShapeDtypeStruct((layers, 3, db, ff), F32),
-            jax.ShapeDtypeStruct((layers, db, qkv_width + q_width), F32),
-            landing(layers, 3, 2, steps, db, ff // 2),
+            jax.ShapeDtypeStruct((rows, width), BF16),
+            jax.ShapeDtypeStruct((layers, db, q_width), F32),
+            jax.ShapeDtypeStruct((layers, db, kv_width), F32),
+            jax.ShapeDtypeStruct((layers, db, kv_width), F32),
+            jax.ShapeDtypeStruct((layers, q_width, db), F32),
+            jax.ShapeDtypeStruct((layers, db, ff), F32),
+            jax.ShapeDtypeStruct((layers, db, ff), F32),
+            jax.ShapeDtypeStruct((layers, ff, db), F32),
+            landing(layers, 2, 2, steps, db, ff // 4),
+            landing(layers, 2, 2, steps, db, ff // 2),
             landing(layers, 2, steps, db, q_width // 2),
             landing(layers, 2, steps, db, q_width // 2),
-            landing(layers, 2, steps, db, kv_width),
-            landing(layers, pairs, 2, steps, HEAD_SIZE, 2 * SEQS * ROWS),
         ],
-        in_specs=[vmem] + [any_spec] * (len(weights) + 11) + [vmem] * 6,
-        out_specs=[vmem] * 2 + [any_spec] * 7,
+        in_specs=[any_spec] * (len(weights) + 13) + [vmem] * 6,
+        out_specs=[vmem] * 2 + [any_spec] * 12,
         scratch_shapes=[
             pltpu.VMEM((6, slots, db, TILE), BF16),
             pltpu.VMEM((2, 2, slots, HEAD_SIZE, ROWS), BF16),
@@ -1110,33 +1303,35 @@
             pltpu.VMEM((width // 2, 2 * tokens), BF16),
             pltpu.VMEM((2 * tokens, ff), BF16),
             pltpu.VMEM((2 * tokens, 2 * ff), BF16),
-            pltpu.VMEM((2 * tokens, qkv_width), BF16),
             pltpu.VMEM((2 * tokens, q_width), BF16),
             pltpu.VMEM((tokens, width), F32),
             pltpu.VMEM((tokens, width), BF16),
             pltpu.VMEM((tokens, width), BF16),
-            pltpu.VMEM((2, rows, width), BF16),
-            pltpu.VMEM((2, rows, width), BF16),
+            pltpu.VMEM((3, rows, width), BF16),
+            pltpu.VMEM((3, rows, width), BF16),
             pltpu.VMEM((q_width, tokens), BF16),
             pltpu.VMEM((units, group * ROWS, 1), F32),
             pltpu.VMEM((q_width, tokens), BF16),
             pltpu.VMEM((q_width, tokens), F32),
             pltpu.VMEM((2 * pairs, HEAD_SIZE, 2 * SEQS * ROWS), F32),
             pltpu.VMEM((2, 2, tokens, TILE), BF16),
-            pltpu.VMEM((2, rows, width), F32),
-            pltpu.VMEM((2, tokens, width // 2), BF16),
-            pltpu.VMEM((2, db, ff // 2), BF16),
+            pltpu.VMEM((rows, width), F32),
+            pltpu.VMEM((tokens, width // 2), BF16),
+            pltpu.VMEM((2, 2, db, ff // 2), BF16),
             pltpu.VMEM((2, db, ff // 2), F32),
+            pltpu.VMEM((2, ff // 4, db), F32),
+            pltpu.VMEM((2, 2, steps, db, -(-kv_width // 256) * 128), BF16),
+            pltpu.VMEM((pairs, 2, steps, HEAD_SIZE, 2 * SEQS * ROWS), BF16),
             pltpu.SemaphoreType.DMA((copies,)),
             pltpu.SemaphoreType.DMA((copies,)),
             pltpu.SemaphoreType.DMA((18,)),
-            pltpu.SemaphoreType.DMA((2,)),
+            pltpu.SemaphoreType.DMA((6,)),
         ],
         compiler_params=pltpu.CompilerParams(
             collective_id=1, has_side_effects=True, vmem_limit_bytes=KERNEL_VMEM
         ),
-    )(grad, *weights, *saved, *tables)
-    return out[:4]
+    )(grad, grad_rows, *weights, *saved, *tables)
+    return out[:10]
 
 
 def build(n_ctx):
@@ -1248,18 +1443,19 @@
             return dot(rows, to_ring)
 
         def restore(rows):
-            return lax.dot_general(
-                rows,
-                to_ring.astype(F32),
-                (((1,), (1,)), ((), ())),
-                precision=lax.Precision.HIGHEST,
-                preferred_element_type=F32,
-            )
+            return dot_nt(rows, to_ring)
+
+        def thirds(rows):
+            high = lax.reduce_precision(rows, 8, 7)
+            middle = lax.reduce_precision(rows - high, 8, 7)
+            return [part.astype(BF16) for part in (high, middle, rows - high - middle)]
 
         offsets = jnp.arange(BLK, dtype=jnp.int32)
-        first = (head == 0)[..., None, None]
-        order = jnp.where(first, block_order, block_order[::-1])
-        docs = jnp.where(first, doc_ids, doc_ids[::-1])
+
+        def own_first(table):
+            return jnp.where(head == 0, table, jnp.stack([table[1], table[0]], axis=0))
+
+        order, docs = own_first(block_order), own_first(doc_ids)
         own_blocks = lax.dynamic_slice(order, (jnp.int32(0), 2 * ctx), (SEQS, 2))
         q_positions = (own_blocks[:, :, None] * BLK + offsets[None, None, :]).reshape(SEQS, ROWS)
         ring_blocks = jnp.einsum(
@@ -1303,16 +1499,16 @@
 
         qkv_width = q_width + 2 * kv_width
         attn_width = qkv_width + q_width
-        grad_res = reorder(cotangent)
+        both = reorder(jnp.concatenate([hidden_in, cotangent], axis=0))
+        grad_res = both[own_rows:]
         attn_shards = [
             jnp.concatenate(
                 [w_query[layer], w_key[layer], w_value[layer], w_out[layer].T], axis=1
             )
             for layer in range(layers)
         ]
-        mlp_shards = [
-            jnp.concatenate([w_gate[layer], w_up[layer], w_down[layer].T], axis=1)
-            for layer in range(layers)
+        gate_up_shards = [
+            jnp.concatenate([w_gate[layer], w_up[layer]], axis=1) for layer in range(layers)
         ]
 
         def forward_by_ops(residual):
@@ -1321,7 +1517,13 @@
             )
             gains = reorder(gains)
             fetched = [
-                (gather(attn), gather(mlp)) for attn, mlp in zip(attn_shards, mlp_shards)
+                (
+                    gather(attn_shards[layer]),
+                    gather(
+                        jnp.concatenate([gate_up_shards[layer], w_down[layer].T], axis=1)
+                    ),
+                )
+                for layer in range(layers)
             ]
             records = []
             for layer in range(layers):
@@ -1383,9 +1585,10 @@
                 attn = attn_shards[layer]
                 if layer == 0:
                     attn = jnp.concatenate([attn, columns], axis=1)
-                shards += [attn, mlp_shards[layer]]
+                shards += [attn, gate_up_shards[layer], w_down[layer].T]
             weights, saved = forward(
                 residual,
+                grad_res.astype(BF16),
                 shards,
                 cosine.T,
                 sine_table.T,
@@ -1397,18 +1600,14 @@
                 kv_width,
                 ff_width,
             )
-            residual_ins = jnp.concatenate([residual[None], saved[10][: layers - 1]], axis=0)
+            residual_ins = jnp.concatenate([residual[None], saved[10]], axis=0)
             tables = (cosine.T, sine_table.T, kpos, qpos, qstart)
             records = [*saved[:10], residual_ins, saved[11]]
-            return weights, tables, records, saved[10][layers - 1]
+            return weights, tables, records, saved[12]
 
         in_kernel = n_ctx * ROWS <= 2048 and db == HEAD_SIZE
         run_forward = forward_by_kernel if in_kernel else forward_by_ops
-        fetched, gains, records, residual = run_forward(reorder(hidden_in))
-        out_hidden = lax.dot_general(
-            residual.astype(BF16), to_ring, (((1,), (1,)), ((), ())), preferred_element_type=F32
-        ).astype(BF16)
-
+        fetched, gains, records, last = run_forward(both[:own_rows])
         def norm_back(grad_res, normed_gradient, value_rows, inverse_norm, gain):
             normalized = value_rows * inverse_norm
             gain_gradient = jnp.sum(normed_gradient * normalized, axis=0)
@@ -1481,43 +1680,47 @@
                 grad_res, d_gains[layer] = norm_back(
                     grad_res, grad_norm_a, residual_in, inverse_a, gain_a
                 )
-            d_mlp = [
-                jnp.stack([down, gu[:, :ff_width], gu[:, ff_width:]], axis=0) for gu, down in d_mlp
-            ]
+            attn_grads, mlp_grads = jnp.stack(d_attn, axis=0), [jnp.stack(part) for part in zip(*d_mlp)]
+            k_at, v_at = q_width, q_width + kv_width
             return (
                 grad_res,
                 jnp.stack(d_gains, axis=0),
-                jnp.stack(d_mlp, axis=0),
-                jnp.stack(d_attn, axis=0),
+                last.astype(BF16),
+                attn_grads[:, :, :k_at],
+                attn_grads[:, :, k_at:v_at],
+                attn_grads[:, :, v_at:qkv_width],
+                attn_grads[:, :, qkv_width:].transpose(0, 2, 1),
+                mlp_grads[0][:, :, :ff_width],
+                mlp_grads[0][:, :, ff_width:],
+                mlp_grads[1].transpose(0, 2, 1),
             )
 
         if in_kernel:
-            grad_res, d_gains, d_mlp, d_attn = backward(
-                grad_res, fetched, records, gains, chips, q_width, kv_width, ff_width
+            grads = backward(
+                grad_res, last, fetched, records, gains, chips, q_width, kv_width, ff_width
             )
         else:
-            grad_res, d_gains, d_mlp, d_attn = backward_by_ops(grad_res)
-        d_hidden = restore(grad_res)
-        d_gains = restore(d_gains)
+            grads = backward_by_ops(grad_res)
+        grad_res, d_gains, x_out, *weight_grads = grads
+        count = 2 * layers
+        rows_low = jnp.concatenate(thirds(d_gains), axis=0)
+        d_gains = restore(rows_low).reshape(3, count, width).sum(axis=0)
         d_gains = d_gains + swap_head(d_gains)
         bit = 1
         while bit < n_ctx:
             d_gains = d_gains + lax.ppermute(d_gains, "ctx", [(i, i ^ bit) for i in range(n_ctx)])
             bit *= 2
         d_gains = lax.dynamic_slice(d_gains, (0, ctx * db), (2 * layers, db))
-        k_at, v_at = q_width, q_width + kv_width
+        restored = restore(jnp.concatenate([x_out, *thirds(grad_res)], axis=0))
+        out_hidden = restored[:own_rows].astype(BF16)
+        d_hidden = restored[own_rows:].reshape(3, own_rows, width).sum(axis=0)
         return (
             out_hidden,
             d_hidden,
             d_gains[:layers],
-            d_attn[:, :, :k_at],
-            d_attn[:, :, k_at:v_at],
-            d_attn[:, :, v_at:qkv_width],
-            d_attn[:, :, qkv_width:].transpose(0, 2, 1),
+            *weight_grads[:4],
             d_gains[layers:],
-            d_mlp[:, 1],
-            d_mlp[:, 2],
-            d_mlp[:, 0].transpose(0, 2, 1),
+            *weight_grads[4:],
         )
 
     return local

time: 874 us -> 768 us (0.88)
  Pallas kernels: 801 us -> 705 us
  matrix products: 19.8 us -> 7.72 us
    pallas_call x1, Pallas kernels: 414 us -> 333 us  [forward(): pl.pallas_call(functools.partial(forward_kernel, dims), out_shape=[jax.Sh...]
    pallas_call x1, Pallas kernels: 387 us -> 372 us  [backward(): pl.pallas_call(functools.partial(backward_kernel, dims), out_shape=[jax.S...]
    dot_general x3 -> x2, matrix products: 14.1 us -> 4.32 us  [dot_nt(): lax.dot_general(left, right, (((1,), (1,)), ((), ())), preferred_element_...]
  transfers between devices with their start and end apart: 5 -> 5, of which waited for: 2 -> 4; matrix products, arithmetic and copies ran while one was open for 2% -> 1% of each run, Pallas kernels for 0% -> 0%
where the time goes in v4:
time: 768 us; the launch traced here: 759 us
  Pallas kernels  705 us (92%)
  local copies, waits for them, and re-layouts  20.7 us (3%)
  other arithmetic  10.1 us (1%)
  waiting for transfers between devices  9.73 us (1%)
  matrix products  7.72 us (1%)
    pallas_call x1, Pallas kernels, backward(): pl.pallas_call(functools.partial(backward_kernel, dims), out_shape=[jax.S...  372 us
    pallas_call x1, Pallas kernels, forward(): pl.pallas_call(functools.partial(forward_kernel, dims), out_shape=[jax.Sh...  333 us
  transfers between devices with their start and end apart: 5, of which 4 were waited for; matrix products, arithmetic and copies ran while one was open for 1% of the time, Pallas kernels for 0%

profile of v4, /device:TPU:0, one launch (start us, length us, event | category | flops | bytes accessed | tf_op | source)
XLA Modules:
  0.0 759.2 jit_solution(18226174889639491112)
XLA Ops:
  0.7 0.9 slice_bitcast_fusion.7
  1.6 0.9 bitcast_dynamic-update-slice_fusion.1
  2.5 1.2 dynamic_slice.9
  4.6 3.0 fusion.2
  8.5 1.4 slice_bitcast_fusion.10
  12.0 0.8 copy.52.refs_12_.refs_24_
  13.0 1.2 slice_bitcast_fusion.1
  14.3 1.0 slice_bitcast_fusion
  15.8 0.9 multiply_sine_fusion
  17.5 0.8 pad_maximum_fusion.3.refs_5_
  18.4 1.2 pad_maximum_fusion.1
  19.6 333.0 %shard_map.221 = (bf16[16,96,2432]{2,1,0:T(8,128)(2,1)}, bf16[16,96,4096]{2,1,0:T(8,128)(2,1)}, bf16[16,96,2048]{2,1,0:T(8,128)(2,1)}, bf16[16,96,2304]{2,1,0:T(...) custom-call(f32[128,1536]{1,0:T(8,128)} %get-tuple-element.122.refs_, ...), custom_call_target="tpu_custom_call" | custom-call | tf_op jit(solution)/shard_map/pallas_call | solution.py:665
  352.6 2.4 pad_maximum_fusion.refs_18_
  355.0 372.1 %shard_map.222 = (f32[128,1536]{1,0:T(8,128)}, f32[4,1536]{1,0:T(4,128)}, bf16[128,1536]{1,0:T(8,128)(2,1)}, f32[2,96,768]{2,1,0:T(8,128)}, f32[2,96,384]{2,1,0:...) custom-call(f32[128,1536]{1,0:T(8,128)} %get-tuple-element.123.refs_, ...), custom_call_target="tpu_custom_call" | custom-call | tf_op jit(solution)/shard_map/pallas_call | solution.py:1276
  727.1 0.8 reduce-precision_convert_fusion.3
  728.0 1.7 fusion
  729.7 1.2 collective-permute-start
  730.9 2.7 collective-permute-done
  733.7 1.2 collective-permute-done.1
  734.9 0.9 collective-permute-start.2
  735.8 3.0 collective-permute-done.2
  738.8 0.9 collective-permute-start.3
  739.9 2.8 collective-permute-done.3
  742.7 1.5 collective-permute-start.4
  744.2 2.7 fusion.1
  747.8 1.0 copy-done.5
  748.8 1.1 copy.54
  749.9 1.1 reduce_sum.28
  751.0 2.9 copy.55
  754.5 0.8 copy.66
  756.7 1.1 copy.69
  757.9 1.1 copy.70
  (89 shorter events, 8.6 us)
Async XLA Ops:
  8.4 1.5 copy-start.14
  8.4 2.5 copy-start.13
  8.4 2.9 copy-start.15
  8.4 2.9 copy-start.16
  8.4 4.4 copy-start.8
  8.4 4.4 copy-start.11
  8.5 4.4 copy-start.12
  8.5 4.5 copy-start.3
  12.8 1.4 copy-start.4
  17.5 2.1 copy-start.2
  727.1 12.6 %copy-start.6 = (f32[128,1536]{1,0:T(8,128)S(1)}, f32[128,1536]{1,0:T(8,128)}, u32[]{:S(2)}) copy-start(f32[128,1536]{1,0:T(8,128)} %get-tuple-element.60) | copy-start | bytes 2359300
  728.0 16.2 %copy-start.17 = (bf16[128,1536]{1,0:T(8,128)(2,1)S(1)}, bf16[128,1536]{1,0:T(8,128)(2,1)}, u32[]{:S(2)}) copy-start(bf16[128,1536]{1,0:T(8,128)(2,1)} %get-tuple-element.59) | copy-start | bytes 1179652
  729.7 3.9 collective-permute-start
  733.6 1.3 collective-permute-start.1
  734.9 3.9 collective-permute-start.2
  738.8 3.9 collective-permute-start.3
  742.7 11.1 %collective-permute-start.4 = (f32[4,1536]{1,0:T(4,128)S(1)}, f32[4,1536]{1,0:T(4,128)S(1)}, u32[]{:S(2)}, u32[]{:S(2)}) collective-permute-start(f32[4,1536]{1,0:T(4,128)S(1)} %add.206), channel_id=1, source_target_pairs={{0,16},{2,18},{4,20},{6,22},{8,24},{10,26},{12,28},{14,30},{16,0},... | collective-permute-start | bytes 73736 | tf_op jit(solution)/shard_map/ppermute | solution.py:1711
  747.7 1.1 copy-start.5
  751.0 3.5 copy-start.7
  751.0 4.3 copy-start.10
  751.0 5.1 copy-start.9
  753.8 2.9 copy-start.1
  755.3 2.6 copy-start

commit v5 on v4

--- a/solution.py
+++ b/solution.py
@@ -737,7 +737,7 @@
             window = self.windows[d](slots[d])
             total = window[...].astype(F32) + self.here[d][...].astype(F32)
             if self.step < self.last:
-                window[...] = total.astype(BF16)
+                window[...] = total.astype(window.dtype)
             else:
                 self.finish(d, total)
         if self.step < self.last:
@@ -792,10 +792,10 @@
     weights = [next(it) for _ in range(parts * layers)]
     (
         kv_ref, normed_a_ref, qt_ref, lse_ref, att_ref, middle_ref, normed_m_ref,
-        gate_ref, up_ref, act_ref, x_in_ref, gain_ref,
+        gate_ref, up_ref, act_ref, x_first_ref, x_next_ref, gain_ref,
         cos_ref, sin_ref, kpos_ref, qpos_ref, qstart_ref,
-    ) = (next(it) for _ in range(17))
-    d_hidden_ref, d_gain_ref, x_out_ref = next(it), next(it), next(it)
+    ) = (next(it) for _ in range(18))
+    d_hidden_ref, d_gain_out_ref, x_out_ref = next(it), next(it), next(it)
     d_query_ref, d_key_ref, d_value_ref, d_out_ref, d_w_gate_ref, d_w_up_ref, d_down_ref = (
         next(it) for _ in range(7)
     )
@@ -803,8 +803,8 @@
     (
         wt, kv_buf, dkv_sib, dw_mlp, dw_attn, a_sib, at_buf, g_act, g_gu, g_att, acc,
         g_low, g2_low, b_send, b_recv, qt_l, lse_l, da_t, dq_t, dkv_sum, gu_buf, rows_f32, n_own,
-        stage, out_stage, turn_stage, land_kv, land_dkv, send_sems, recv_sems, load_sems, stage_sems,
-    ) = (next(it) for _ in range(32))
+        stage, out_stage, turn_stage, land_kv, land_dkv, d_gain_ref, d_gain_in, gain_slots, land_gain, send_sems, recv_sems, load_sems, stage_sems,
+    ) = (next(it) for _ in range(36))
 
     rows = g_ref.shape[0]
     tokens = 2 * rows
@@ -982,7 +982,7 @@
                 acc[...] += dot_nt(d_gate, flat(wt.at[at]))
             acc[...] += dot_nt(d_up, flat(wt.at[at + 1]))
             pending = following
-            rounds.pump(3 if len(rounds.active) > 2 else 1)
+            rounds.pump(2 if len(rounds.active) > 2 else 1)
         b_send[0] = acc[rows:tokens, :].astype(BF16)
         swap = links.to_head(b_send.at[0], b_recv.at[0])
         out_loads = [
@@ -1147,7 +1147,8 @@
                         total_up(i - 1)
                     else:
                         sums.pump(2)
-                    rounds.pump()
+                    if u % 2:
+                        rounds.pump()
             offer(i)
 
         if layer == layers - 1:
@@ -1155,7 +1156,8 @@
             links.sent(out_swap)
             b_send[2] = (rows_f32[...] + b_recv[2].astype(F32)).astype(BF16)
             local(b_send.at[2], x_out_ref, 11).wait()
-        here.append(local(x_in_ref.at[layer], rows_f32, 15))
+        x_in = x_next_ref.at[layer - 1] if layer else x_first_ref
+        here.append(local(x_in, rows_f32, 15))
         from_sib_g.wait_recv()
         turn_columns(g2_low[:, 0:side], a_sib[2])
         weight_grad(dw_attn, qkv_width, g_att, q_width)
@@ -1188,7 +1190,7 @@
         while sums.active:
             sums.pump()
             step += 1
-            if step % 3 == 0:
+            if step % 4 == 0:
                 rounds.pump()
             if step == 4:
                 from_sib_q.wait_recv()
@@ -1248,6 +1250,33 @@
         rounds.pump()
         swap.wait_recv()
         norm_back(acc[0:rows, :] + b_recv[1].astype(F32), rows_f32[...], gain_a, layer)
+    swap = links.to_head(d_gain_ref, d_gain_in.at[0])
+    rounds.pump(2)
+    swap.wait_recv()
+    gain_sum = d_gain_ref[...] + d_gain_in[0]
+    d_gain_in[1] = gain_sum
+    swap = links.to_sibling(d_gain_in.at[1, :, pl.ds(side, side)], d_gain_in.at[2, :, pl.ds(0, side)])
+    rounds.pump(2)
+    swap.wait_recv()
+    gain_sum = gain_sum[:, 0:side] + d_gain_in[2, :, 0:side]
+    gain_slots[...] = jnp.zeros_like(gain_slots)
+    for slot in range(chips):
+        for d in range(2):
+            gain_slots[slot, d, 0:layers, 0:db] = gain_sum[
+                d * layers : (d + 1) * layers, slot * db : (slot + 1) * db
+            ]
+
+    def gain_finish(d, total):
+        d_gain_out_ref[d] = total
+
+    rounds.start(
+        RingScatter(
+            links,
+            (lambda slot: gain_slots.at[slot, 0], lambda slot: gain_slots.at[slot, 1]),
+            (lambda step: land_gain.at[0, step], lambda step: land_gain.at[1, step]),
+            gain_finish,
+        )
+    )
     rounds.drain()
     links.finish()
 
@@ -1266,7 +1295,7 @@
     qkv_width = q_width + 2 * kv_width
     dims = (layers, chips, width, q_width, kv_width, ff)
     rings = 4 + 4 + pairs
-    copies = 1 + layers * (rings * 2 * steps + 4 + 4 + 1 + 2 * (ff // TILE) + 1 + 2 * pairs + 2)
+    copies = 3 + 2 * steps + layers * (rings * 2 * steps + 4 + 4 + 1 + 2 * (ff // TILE) + 1 + 2 * pairs + 2)
     any_spec = pl.BlockSpec(memory_space=pltpu.HBM)
     vmem = pl.BlockSpec(memory_space=pltpu.VMEM)
 
@@ -1277,7 +1306,7 @@
         functools.partial(backward_kernel, dims),
         out_shape=[
             jax.ShapeDtypeStruct((rows, width), F32),
-            jax.ShapeDtypeStruct((2 * layers, width), F32),
+            jax.ShapeDtypeStruct((2, 8, 128), F32),
             jax.ShapeDtypeStruct((rows, width), BF16),
             jax.ShapeDtypeStruct((layers, db, q_width), F32),
             jax.ShapeDtypeStruct((layers, db, kv_width), F32),
@@ -1291,7 +1320,7 @@
             landing(layers, 2, steps, db, q_width // 2),
             landing(layers, 2, steps, db, q_width // 2),
         ],
-        in_specs=[any_spec] * (len(weights) + 13) + [vmem] * 6,
+        in_specs=[any_spec] * (len(weights) + 14) + [vmem] * 6,
         out_specs=[vmem] * 2 + [any_spec] * 12,
         scratch_shapes=[
             pltpu.VMEM((6, slots, db, TILE), BF16),
@@ -1322,6 +1351,10 @@
             pltpu.VMEM((2, ff // 4, db), F32),
             pltpu.VMEM((2, 2, steps, db, -(-kv_width // 256) * 128), BF16),
             pltpu.VMEM((pairs, 2, steps, HEAD_SIZE, 2 * SEQS * ROWS), BF16),
+            pltpu.VMEM((2 * layers, width), F32),
+            pltpu.VMEM((3, 2 * layers, width), F32),
+            pltpu.VMEM((chips, 2, 8, 128), F32),
+            pltpu.VMEM((2, steps, 8, 128), F32),
             pltpu.SemaphoreType.DMA((copies,)),
             pltpu.SemaphoreType.DMA((copies,)),
             pltpu.SemaphoreType.DMA((18,)),
@@ -1600,9 +1633,8 @@
                 kv_width,
                 ff_width,
             )
-            residual_ins = jnp.concatenate([residual[None], saved[10]], axis=0)
             tables = (cosine.T, sine_table.T, kpos, qpos, qstart)
-            records = [*saved[:10], residual_ins, saved[11]]
+            records = [*saved[:10], residual, saved[10], saved[11]]
             return weights, tables, records, saved[12]
 
         in_kernel = n_ctx * ROWS <= 2048 and db == HEAD_SIZE
@@ -1699,18 +1731,19 @@
             grads = backward(
                 grad_res, last, fetched, records, gains, chips, q_width, kv_width, ff_width
             )
+            grad_res, d_gains, x_out, *weight_grads = grads
+            d_gains = d_gains[:, :layers, :db].reshape(2 * layers, db)
         else:
-            grads = backward_by_ops(grad_res)
-        grad_res, d_gains, x_out, *weight_grads = grads
-        count = 2 * layers
-        rows_low = jnp.concatenate(thirds(d_gains), axis=0)
-        d_gains = restore(rows_low).reshape(3, count, width).sum(axis=0)
-        d_gains = d_gains + swap_head(d_gains)
-        bit = 1
-        while bit < n_ctx:
-            d_gains = d_gains + lax.ppermute(d_gains, "ctx", [(i, i ^ bit) for i in range(n_ctx)])
-            bit *= 2
-        d_gains = lax.dynamic_slice(d_gains, (0, ctx * db), (2 * layers, db))
+            grad_res, d_gains, x_out, *weight_grads = backward_by_ops(grad_res)
+            parts = restore(jnp.concatenate(thirds(d_gains), axis=0))
+            d_gains = parts.reshape(3, 2 * layers, width).sum(axis=0)
+            d_gains = d_gains + swap_head(d_gains)
+            bit = 1
+            while bit < n_ctx:
+                pairs = [(i, i ^ bit) for i in range(n_ctx)]
+                d_gains = d_gains + lax.ppermute(d_gains, "ctx", pairs)
+                bit *= 2
+            d_gains = lax.dynamic_slice(d_gains, (0, ctx * db), (2 * layers, db))
         restored = restore(jnp.concatenate([x_out, *thirds(grad_res)], axis=0))
         out_hidden = restored[:own_rows].astype(BF16)
         d_hidden = restored[own_rows:].reshape(3, own_rows, width).sum(axis=0)

time: 768 us -> 755 us (0.983)
  waiting for transfers between devices: 9.73 us -> 0 us
    ppermute x5 -> x0, waiting for transfers between devices: 9.73 us -> none  [the longest x4 7 us: local(): lax.ppermute(d_gains, 'ctx', [(i, i ^ bit) for i in range(n_ctx)])]
  transfers between devices with their start and end apart: 5 -> 0, of which waited for: 4 -> 0; matrix products, arithmetic and copies ran while one was open for 1% -> 0% of each run, Pallas kernels for 0% -> 0%
where the time goes in v5:
time: 755 us; the launch traced here: 745 us
  Pallas kernels  706 us (94%)
  local copies, waits for them, and re-layouts  23.2 us (3%)
  other arithmetic  10 us (1%)
    pallas_call x1, Pallas kernels, backward(): pl.pallas_call(functools.partial(backward_kernel, dims), out_shape=[jax.S...  373 us
    pallas_call x1, Pallas kernels, forward(): pl.pallas_call(functools.partial(forward_kernel, dims), out_shape=[jax.Sh...  333 us

profile of v5, /device:TPU:0, one launch (start us, length us, event | category | flops | bytes accessed | tf_op | source)
XLA Modules:
  0.0 745.4 jit_solution(144176582680663494)
XLA Ops:
  0.7 1.4 dynamic_slice.6
  2.8 0.7 pad_maximum_fusion.3
  3.5 0.8 fusion.40
  4.3 0.7 fusion.36
  6.8 0.8 fusion.39
  7.6 0.8 fusion.35
  9.2 0.9 multiply_sine_fusion
  10.2 0.7 broadcast_add_fusion.refs_11_.refs_24_
  11.0 0.8 copy.52.refs_12_.refs_25_
  11.8 1.0 slice_bitcast_fusion.7
  12.8 0.9 slice_bitcast_fusion.6
  13.7 0.9 slice_bitcast_fusion.8
  14.6 0.8 pad_maximum_fusion.2.refs_5_
  15.8 1.2 pad_maximum_fusion
  17.2 1.0 slice_bitcast_fusion
  18.1 1.9 fusion.1
  20.1 0.8 slice.131.refs_1_
  20.8 1.2 fusion.38
  22.1 332.7 %shard_map.221 = (bf16[16,96,2432]{2,1,0:T(8,128)(2,1)}, bf16[16,96,4096]{2,1,0:T(8,128)(2,1)}, bf16[16,96,2048]{2,1,0:T(8,128)(2,1)}, bf16[16,96,2304]{2,1,0:T(...) custom-call(f32[128,1536]{1,0:T(8,128)} %get-tuple-element.121.refs_, ...), custom_call_target="tpu_custom_call" | custom-call | tf_op jit(solution)/shard_map/pallas_call | solution.py:665
  354.8 373.4 %shard_map.222 = (f32[128,1536]{1,0:T(8,128)}, f32[2,8,128]{2,1,0:T(8,128)}, bf16[128,1536]{1,0:T(8,128)(2,1)}, f32[2,96,768]{2,1,0:T(8,128)}, f32[2,96,384]{2,1...) custom-call(f32[128,1536]{1,0:T(8,128)} %get-tuple-element.122.refs_, ...), custom_call_target="tpu_custom_call" | custom-call | tf_op jit(solution)/shard_map/pallas_call | solution.py:1305
  728.3 1.3 slice_bitcast_fusion.10
  729.6 2.2 copy.54
  731.8 1.3 reduce-precision_convert_fusion.1
  733.1 2.7 fusion
  735.7 0.8 slice.130
  736.7 1.1 reduce_sum.19
  737.8 2.9 copy.55
  740.7 0.8 copy.66
  741.5 0.7 copy.67
  742.2 0.7 copy.68
  743.0 1.1 copy.69
  744.1 1.1 copy.70
  (65 shorter events, 4.0 us)
Async XLA Ops:
  0.6 14.9 %copy-start.8 = (bf16[2,768,96]{1,2,0:T(8,128)(2,1)S(1)}, bf16[2,768,96]{1,2,0:T(8,128)(2,1)}, u32[]{:S(2)}) copy-start(bf16[2,768,96]{1,2,0:T(8,128)(2,1)} %param.21) | copy-start | bytes 884740
  0.7 14.8 %copy-start.12 = (bf16[2,96,384]{2,1,0:T(8,128)(2,1)S(1)}, bf16[2,96,384]{2,1,0:T(8,128)(2,1)}, u32[]{:S(2)}) copy-start(bf16[2,96,384]{2,1,0:T(8,128)(2,1)} %param.20) | copy-start | bytes 442372
  0.7 14.8 %copy-start.11 = (bf16[2,96,384]{2,1,0:T(8,128)(2,1)S(1)}, bf16[2,96,384]{2,1,0:T(8,128)(2,1)}, u32[]{:S(2)}) copy-start(bf16[2,96,384]{2,1,0:T(8,128)(2,1)} %param.19) | copy-start | bytes 442372
  0.7 14.8 %copy-start.7 = (bf16[2,96,768]{2,1,0:T(8,128)(2,1)S(1)}, bf16[2,96,768]{2,1,0:T(8,128)(2,1)}, u32[]{:S(2)}) copy-start(bf16[2,96,768]{2,1,0:T(8,128)(2,1)} %param.18) | copy-start | bytes 884740
  0.7 14.9 %copy-start.3 = (bf16[2,96,2048]{2,1,0:T(8,128)(2,1)S(1)}, bf16[2,96,2048]{2,1,0:T(8,128)(2,1)}, u32[]{:S(2)}) copy-start(bf16[2,96,2048]{2,1,0:T(8,128)(2,1)} %param.23) | copy-start | bytes 2359300
  11.8 3.9 copy-start.4
  15.6 1.4 copy-start.2
  15.7 1.5 copy-start.5
  15.7 2.4 copy-start.13
  15.8 2.4 copy-start.14
  728.3 4.8 copy-start.15
  737.8 2.9 copy-start.6
  737.8 3.7 copy-start.10
  737.8 4.5 copy-start.9
  737.8 5.2 copy-start.1
  741.5 2.6 copy-start
